TPU v7x, 32 devices: a whole 2x2x4 slice. The times are simulated.
32 devices in a mesh: rows: 16 (over z, y, core), seq: 2 (over x).
Axes of the slice: x: 2, y: 2, z: 4, core: 2. Of those that a mesh axis runs over, the one named last changes fastest.
Arguments:
- patches: bfloat16 [64, 128, 48], P('rows', 'seq'), may hold values from -6 to 6
- seg_lengths: int32 [64, 4], P('rows'), may hold values from 1 to 96, 128 in all within a row
- class_labels: int32 [64, 4], P('rows'), may hold values from 0 to 999
- cotangent: float32 [64, 128, 48], P('rows', 'seq'), may hold values from -6 to 6
- w_in: float32 [2, 48, 768], P(None, None, 'rows'), may hold values from -0.875 to 0.875
- m_in: float32 [2, 48, 768], P(None, None, 'rows'), may hold values from -16 to 16
- v_in: float32 [2, 48, 768], P(None, None, 'rows'), may hold values from 39.3216 to 155.648
- w_table: float32 [2, 1000, 768], P(None, None, 'rows'), may hold values from -6 to 6
- m_table: float32 [2, 1000, 768], P(None, None, 'rows'), may hold values from -4 to 4
- v_table: float32 [2, 1000, 768], P(None, None, 'rows'), may hold values from 0.393216 to 1.55648
- w_qkv: float32 [4, 768, 2304], P(None, 'rows'), may hold values from -0.21875 to 0.21875
- m_qkv: float32 [4, 768, 2304], P(None, 'rows'), may hold values from -4 to 4
- v_qkv: float32 [4, 768, 2304], P(None, 'rows'), may hold values from 4.34176 to 17.2032
- w_o: float32 [4, 768, 768], P(None, 'rows'), may hold values from -0.625 to 0.625
- m_o: float32 [4, 768, 768], P(None, 'rows'), may hold values from -12 to 12
- v_o: float32 [4, 768, 768], P(None, 'rows'), may hold values from 17.2032 to 68.8128
- w_up: float32 [4, 768, 3072], P(None, 'rows'), may hold values from -0.21875 to 0.21875
- m_up: float32 [4, 768, 3072], P(None, 'rows'), may hold values from -12 to 12
- v_up: float32 [4, 768, 3072], P(None, 'rows'), may hold values from 17.2032 to 68.8128
- w_down: float32 [4, 3072, 768], P(None, 'rows'), may hold values from -0.109375 to 0.109375
- m_down: float32 [4, 3072, 768], P(None, 'rows'), may hold values from -4 to 4
- v_down: float32 [4, 3072, 768], P(None, 'rows'), may hold values from 4.34176 to 17.2032
- w_out: float32 [2, 768, 96], P(None, 'rows'), may hold values from -0.0625 to 0.0625
- m_out: float32 [2, 768, 96], P(None, 'rows'), may hold values from -64 to 64
- v_out: float32 [2, 768, 96], P(None, 'rows'), may hold values from 434.176 to 1720.32
- gains: float32 [2, 5, 768], P(None, None, 'rows'), may hold values from 0.5 to 1.5
- m_gains: float32 [2, 5, 768], P(None, None, 'rows'), may hold values from -16 to 16
- v_gains: float32 [2, 5, 768], P(None, None, 'rows'), may hold values from 39.3216 to 155.648
Outputs:
- latents: float32 [64, 128, 48], P('rows', 'seq')
- logdet: float32 [64, 128], P('rows', 'seq')
- patch_grad: float32 [64, 128, 48], P('rows', 'seq')
- new_m_in: float32 [2, 48, 768], P(None, None, 'rows')
- new_v_in: float32 [2, 48, 768], P(None, None, 'rows')
- new_w_in: float32 [2, 48, 768], P(None, None, 'rows')
- new_m_table: float32 [2, 1000, 768], P(None, None, 'rows')
- new_v_table: float32 [2, 1000, 768], P(None, None, 'rows')
- new_w_table: float32 [2, 1000, 768], P(None, None, 'rows')
- new_m_qkv: float32 [4, 768, 2304], P(None, 'rows')
- new_v_qkv: float32 [4, 768, 2304], P(None, 'rows')
- new_w_qkv: float32 [4, 768, 2304], P(None, 'rows')
- new_m_o: float32 [4, 768, 768], P(None, 'rows')
- new_v_o: float32 [4, 768, 768], P(None, 'rows')
- new_w_o: float32 [4, 768, 768], P(None, 'rows')
- new_m_up: float32 [4, 768, 3072], P(None, 'rows')
- new_v_up: float32 [4, 768, 3072], P(None, 'rows')
- new_w_up: float32 [4, 768, 3072], P(None, 'rows')
- new_m_down: float32 [4, 3072, 768], P(None, 'rows')
- new_v_down: float32 [4, 3072, 768], P(None, 'rows')
- new_w_down: float32 [4, 3072, 768], P(None, 'rows')
- new_m_out: float32 [2, 768, 96], P(None, 'rows')
- new_v_out: float32 [2, 768, 96], P(None, 'rows')
- new_w_out: float32 [2, 768, 96], P(None, 'rows')
- new_m_gains: float32 [2, 5, 768], P(None, None, 'rows')
- new_v_gains: float32 [2, 5, 768], P(None, None, 'rows')
- new_w_gains: float32 [2, 5, 768], P(None, None, 'rows')
Inputs may be any that keep to these rules, and one draw needn't show every extreme that they name: `seg_lengths`: each row's lengths sum to 128, and one of them is exactly 96.
All inputs are finite; a program needn't handle non-finite values.
Results may differ from a plain program's by a relative error of at most 0.012.
Values may be sent and summed in bfloat16 or wider, within the bound.
A program may use at most 576 MiB of HBM per device.

v0:
```python
from functools import partial

import jax
import jax.numpy as jnp
from jax import lax
from jax.sharding import PartitionSpec as P

HEADS = 12
HEAD_DIM = 64
LAYERS = 2
SEGS = 4
STEP = 10


EPS_NORM = 1e-05
MASKED = -1000000000.0
BETA_ONE = 0.9
BETA_TWO = 0.95
EPS_ADAM = 1e-08
DECAY = 0.1
RATES = (0.05, 0.3, 0.02, 0.05, 0.02, 0.01, 0.01, 0.3)


def passed_along(shard, axis, by):
    devices = lax.axis_size(axis)
    pairs = [(i, i + by) for i in range(devices) if 0 <= i + by < devices]
    return lax.ppermute(shard, axis, pairs)


def from_partner(shard, axis, apart):
    return lax.ppermute(shard, axis, [(i, i ^ 1 << apart) for i in range(lax.axis_size(axis))])


def normalize(hidden):
    center = hidden - jnp.mean(hidden, -1, keepdims=True)
    inverse = lax.rsqrt(jnp.mean(center * center, -1, keepdims=True) + EPS_NORM)
    return (center * inverse, inverse)


def normalize_back(normed, inverse, grad_normed):
    mean_grad = jnp.mean(grad_normed, -1, keepdims=True)
    mean_proj = jnp.mean(grad_normed * normed, -1, keepdims=True)
    return inverse * (grad_normed - mean_grad - normed * mean_proj)


def segment_of(places, seg_ends):
    return jnp.sum((places[:, None] >= seg_ends[None, :]).astype(jnp.int32), -1)


def class_rows(seg_ids, labels_row, classes):
    picked = jnp.sum(
        jnp.where(seg_ids[:, None] == jnp.arange(SEGS)[None, :], labels_row[None, :], 0), 1
    )
    return (picked[:, None] == jnp.arange(classes)[None, :]).astype(jnp.bfloat16)


def block_weights(gathered, block_index):
    layer_list = []
    for layer_index in range(LAYERS):
        where_at = block_index * LAYERS + layer_index
        layer_list.append(
            (
                gathered[2][where_at],
                gathered[3][where_at],
                gathered[4][where_at],
                gathered[5][where_at],
            )
        )
    return (
        gathered[0][block_index],
        gathered[1][block_index],
        layer_list,
        gathered[6][block_index],
        gathered[7][block_index],
    )


def attention_scores(query, key_rows, attend):
    scores = jnp.einsum(
        "chd,khd->hck", query, key_rows, preferred_element_type=jnp.float32
    ) * HEAD_DIM ** (-0.5)
    return jnp.where(attend[None], scores, MASKED)


def forward_block(inputs, onehot, seg_query, seg_keys, places, same_seg, weights):
    w_in, w_table, layer_list, w_out, gains = weights
    group = inputs.shape[0]
    channels = inputs.shape[1]
    width = w_in.shape[1]
    gain_rows = gains.astype(jnp.float32)
    key_places = jnp.arange(seg_keys.shape[0], dtype=jnp.int32)
    attend = (seg_query[:, None] == seg_keys[None, :]) & (places[:, None] >= key_places[None, :])
    hidden = jnp.dot(inputs.astype(jnp.bfloat16), w_in, preferred_element_type=jnp.float32)
    hidden = hidden + jnp.dot(onehot, w_table, preferred_element_type=jnp.float32)
    layer_saved = []
    for layer_index, (w_qkv, w_o, w_up, w_down) in enumerate(layer_list):
        normed_a, inverse_a = normalize(hidden)
        act_a = (normed_a * gain_rows[2 * layer_index]).astype(jnp.bfloat16)
        qkv = jnp.dot(act_a, w_qkv, preferred_element_type=jnp.float32).astype(jnp.bfloat16)
        kv_rows = lax.all_gather(qkv[:, width:], "seq", axis=0, tiled=True)
        query = qkv[:, :width].reshape(group, HEADS, HEAD_DIM)
        key_rows = kv_rows[:, :width].reshape(-1, HEADS, HEAD_DIM)
        value_rows = kv_rows[:, width:].reshape(-1, HEADS, HEAD_DIM)
        scores = attention_scores(query, key_rows, attend)
        row_top = jnp.max(scores, -1, keepdims=True)
        expo_rows = jnp.exp(scores - row_top)
        row_total = jnp.sum(expo_rows, -1, keepdims=True)
        soft_low = (expo_rows / row_total).astype(jnp.bfloat16)
        log_total = row_top + jnp.log(row_total)
        context = jnp.einsum(
            "hck,khd->chd", soft_low, value_rows, preferred_element_type=jnp.float32
        )
        context = context.reshape(group, width).astype(jnp.bfloat16)
        middle = hidden + jnp.dot(context, w_o, preferred_element_type=jnp.float32)
        normed_m, inverse_m = normalize(middle)
        act_m = (normed_m * gain_rows[2 * layer_index + 1]).astype(jnp.bfloat16)
        upper_rows = jnp.dot(act_m, w_up, preferred_element_type=jnp.float32)
        gelu_low = jax.nn.gelu(upper_rows, approximate=True).astype(jnp.bfloat16)
        hidden = middle + jnp.dot(gelu_low, w_down, preferred_element_type=jnp.float32)
        layer_saved.append(
            (
                normed_a,
                inverse_a,
                act_a,
                qkv,
                kv_rows,
                log_total,
                context,
                normed_m,
                inverse_m,
                act_m,
                upper_rows,
                gelu_low,
            )
        )
    normed_f, inverse_f = normalize(hidden)
    act_f = (normed_f * gain_rows[2 * LAYERS]).astype(jnp.bfloat16)
    prediction = jnp.dot(act_f, w_out, preferred_element_type=jnp.float32)
    carried = passed_along(prediction[-1:], "seq", 1)
    previous = jnp.concatenate([carried, prediction[:-1]], 0)
    shift_mu = jnp.where(same_seg[:, None], previous[:, :channels], 0.0)
    shift_alpha = jnp.where(same_seg[:, None], previous[:, channels:], 0.0)
    latent = (inputs - shift_mu) * jnp.exp(-shift_alpha)
    saved = (
        attend,
        seg_query,
        seg_keys,
        places,
        layer_saved,
        normed_f,
        inverse_f,
        act_f,
        shift_alpha,
        latent,
    )
    return (latent, -jnp.sum(shift_alpha, -1), saved)


def backward_block(inputs, onehot, same_seg, weights, saved, grad_latent):
    w_in, w_table, layer_list, w_out, gains = weights
    (
        attend,
        seg_query,
        seg_keys,
        places,
        layer_saved,
        normed_f,
        inverse_f,
        act_f,
        shift_alpha,
        latent,
    ) = saved
    group = inputs.shape[0]
    width = w_in.shape[1]
    factor = HEAD_DIM ** (-0.5)
    gain_rows = gains.astype(jnp.float32)
    scale_back = jnp.exp(-shift_alpha)
    grad_mu = -grad_latent * scale_back
    grad_alpha = 1.0 - grad_latent * latent
    grad_prev = jnp.where(same_seg[:, None], jnp.concatenate([grad_mu, grad_alpha], 1), 0.0)
    grad_inputs = grad_latent * scale_back
    returned = passed_along(grad_prev[:1], "seq", -1)
    grad_pred = jnp.concatenate([grad_prev[1:], returned], 0).astype(jnp.bfloat16)
    grad_w_out = jnp.dot(act_f.T, grad_pred, preferred_element_type=jnp.float32)
    grad_act = jnp.dot(grad_pred, w_out.T, preferred_element_type=jnp.float32)
    gain_grads = [None] * (2 * LAYERS + 1)
    gain_grads[2 * LAYERS] = jnp.sum(grad_act * normed_f, 0)
    grad_hidden = normalize_back(normed_f, inverse_f, grad_act * gain_rows[2 * LAYERS])
    layer_grads = [None] * LAYERS
    for layer_index in reversed(range(LAYERS)):
        w_qkv, w_o, w_up, w_down = layer_list[layer_index]
        (
            normed_a,
            inverse_a,
            act_a,
            qkv,
            kv_rows,
            log_total,
            context,
            normed_m,
            inverse_m,
            act_m,
            upper_rows,
            gelu_low,
        ) = layer_saved[layer_index]
        grad_branch = grad_hidden.astype(jnp.bfloat16)
        grad_w_down = jnp.dot(gelu_low.T, grad_branch, preferred_element_type=jnp.float32)
        grad_gelu = jnp.dot(grad_branch, w_down.T, preferred_element_type=jnp.float32)
        gelu_pull = jax.vjp(partial(jax.nn.gelu, approximate=True), upper_rows)[1]
        grad_upper = gelu_pull(grad_gelu)[0].astype(jnp.bfloat16)
        grad_w_up = jnp.dot(act_m.T, grad_upper, preferred_element_type=jnp.float32)
        grad_act_m = jnp.dot(grad_upper, w_up.T, preferred_element_type=jnp.float32)
        gain_grads[2 * layer_index + 1] = jnp.sum(grad_act_m * normed_m, 0)
        grad_middle = grad_hidden + normalize_back(
            normed_m, inverse_m, grad_act_m * gain_rows[2 * layer_index + 1]
        )
        grad_mid_low = grad_middle.astype(jnp.bfloat16)
        grad_w_o = jnp.dot(context.T, grad_mid_low, preferred_element_type=jnp.float32)
        grad_ctx_flat = jnp.dot(grad_mid_low, w_o.T, preferred_element_type=jnp.float32).astype(
            jnp.bfloat16
        )
        grad_context = grad_ctx_flat.reshape(group, HEADS, HEAD_DIM)
        query = qkv[:, :width].reshape(group, HEADS, HEAD_DIM)
        key_rows = kv_rows[:, :width].reshape(-1, HEADS, HEAD_DIM)
        value_rows = kv_rows[:, width:].reshape(-1, HEADS, HEAD_DIM)
        soft_rows = jnp.exp(attention_scores(query, key_rows, attend) - log_total)
        soft_low = soft_rows.astype(jnp.bfloat16)
        grad_soft = jnp.einsum(
            "chd,khd->hck", grad_context, value_rows, preferred_element_type=jnp.float32
        )
        row_delta = jnp.sum(soft_rows * grad_soft, -1, keepdims=True)
        grad_scores = (soft_rows * (grad_soft - row_delta)).astype(jnp.bfloat16)
        grad_query = (
            jnp.einsum("hck,khd->chd", grad_scores, key_rows, preferred_element_type=jnp.float32)
            * factor
        )
        grad_keys = (
            jnp.einsum("hck,chd->khd", grad_scores, query, preferred_element_type=jnp.float32)
            * factor
        )
        grad_values = jnp.einsum(
            "hck,chd->khd", soft_low, grad_context, preferred_element_type=jnp.float32
        )
        grad_kv = lax.psum_scatter(
            jnp.concatenate(
                [
                    grad_keys.reshape(group * lax.axis_size("seq"), width),
                    grad_values.reshape(group * lax.axis_size("seq"), width),
                ],
                1,
            ),
            "seq",
            scatter_dimension=0,
            tiled=True,
        )
        grad_qkv = jnp.concatenate([grad_query.reshape(group, width), grad_kv], 1).astype(
            jnp.bfloat16
        )
        grad_w_qkv = jnp.dot(act_a.T, grad_qkv, preferred_element_type=jnp.float32)
        grad_act_a = jnp.dot(grad_qkv, w_qkv.T, preferred_element_type=jnp.float32)
        gain_grads[2 * layer_index] = jnp.sum(grad_act_a * normed_a, 0)
        grad_hidden = grad_middle + normalize_back(
            normed_a, inverse_a, grad_act_a * gain_rows[2 * layer_index]
        )
        layer_grads[layer_index] = (grad_w_qkv, grad_w_o, grad_w_up, grad_w_down)
    grad_start = grad_hidden.astype(jnp.bfloat16)
    grad_w_in = jnp.dot(
        inputs.astype(jnp.bfloat16).T, grad_start, preferred_element_type=jnp.float32
    )
    grad_table = jnp.dot(onehot.T, grad_start, preferred_element_type=jnp.float32)
    grad_inputs = grad_inputs + jnp.dot(grad_start, w_in.T, preferred_element_type=jnp.float32)
    return (grad_inputs, (grad_w_in, grad_table, layer_grads, grad_w_out, jnp.stack(gain_grads, 0)))


def combine_grads(grads_one, grads_two):
    both = (grads_one, grads_two)
    layered = [layer_item for block_grads in both for layer_item in block_grads[2]]
    return (
        jnp.stack([grads_one[0], grads_two[0]], 0),
        jnp.stack([grads_one[1], grads_two[1]], 0),
        jnp.stack([layer_item[0] for layer_item in layered], 0),
        jnp.stack([layer_item[1] for layer_item in layered], 0),
        jnp.stack([layer_item[2] for layer_item in layered], 0),
        jnp.stack([layer_item[3] for layer_item in layered], 0),
        jnp.stack([grads_one[3], grads_two[3]], 0),
        jnp.stack([grads_one[4], grads_two[4]], 0),
    )


def add_up(totals, extra):
    if totals is None:
        return extra
    return tuple((left + right for left, right in zip(totals, extra)))


def adam_step(weight, first, second, grad, rate):
    first_new = BETA_ONE * first + (1.0 - BETA_ONE) * grad
    second_new = BETA_TWO * second + (1.0 - BETA_TWO) * grad * grad
    first_hat = first_new / (1.0 - BETA_ONE**STEP)
    second_hat = second_new / (1.0 - BETA_TWO**STEP)
    weight_new = weight - rate * (first_hat / (jnp.sqrt(second_hat) + EPS_ADAM) + DECAY * weight)
    return (first_new, second_new, weight_new)


def body(
    patches,
    seg_lengths,
    class_labels,
    cotangent,
    w_in,
    m_in,
    v_in,
    w_table,
    m_table,
    v_table,
    w_qkv,
    m_qkv,
    v_qkv,
    w_o,
    m_o,
    v_o,
    w_up,
    m_up,
    v_up,
    w_down,
    m_down,
    v_down,
    w_out,
    m_out,
    v_out,
    gains,
    m_gains,
    v_gains,
):
    masters = (w_in, w_table, w_qkv, w_o, w_up, w_down, w_out, gains)
    low_in, low_table, low_qkv, low_o, low_up, low_down, low_out, low_gains = tuple(
        (weight.astype(jnp.bfloat16) for weight in masters)
    )
    group = patches.shape[1]
    seq_count = lax.axis_size("seq")
    row_len = group * seq_count
    bit_count = seq_count.bit_length() - 1
    places = lax.axis_index("seq") * group + jnp.arange(group, dtype=jnp.int32)
    all_places = jnp.arange(row_len, dtype=jnp.int32)
    mirrored_places = row_len - 1 - places
    latent_list = []
    logdet_list = []
    grad_list = []
    grad_totals = None
    for batch_index in range(patches.shape[0]):
        gathered = (
            lax.all_gather(low_in, "rows", axis=2, tiled=True),
            lax.all_gather(low_table, "rows", axis=2, tiled=True),
            lax.all_gather(low_qkv, "rows", axis=1, tiled=True),
            lax.all_gather(low_o, "rows", axis=1, tiled=True),
            lax.all_gather(low_up, "rows", axis=1, tiled=True),
            lax.all_gather(low_down, "rows", axis=1, tiled=True),
            lax.all_gather(low_out, "rows", axis=1, tiled=True),
            lax.all_gather(low_gains, "rows", axis=2, tiled=True),
        )
        first_weights = block_weights(gathered, 0)
        second_weights = block_weights(gathered, 1)
        classes = gathered[1].shape[1]
        seg_ends = jnp.cumsum(seg_lengths[batch_index])
        labels_row = class_labels[batch_index]
        seg_fwd = segment_of(places, seg_ends)
        seg_fwd_keys = segment_of(all_places, seg_ends)
        same_fwd = (places >= 1) & (seg_fwd == segment_of(places - 1, seg_ends))
        seg_rev = segment_of(mirrored_places, seg_ends)
        seg_rev_keys = segment_of(row_len - 1 - all_places, seg_ends)
        same_rev = (places >= 1) & (seg_rev == segment_of(mirrored_places + 1, seg_ends))
        onehot_fwd = class_rows(seg_fwd, labels_row, classes)
        onehot_rev = class_rows(seg_rev, labels_row, classes)
        inputs_one = patches[batch_index].astype(jnp.float32)
        latent_one, det_one, saved_one = forward_block(
            inputs_one, onehot_fwd, seg_fwd, seg_fwd_keys, places, same_fwd, first_weights
        )
        payload = (latent_one, det_one)
        for bit_index in range(bit_count):
            payload = from_partner((payload[0], payload[1]), "seq", bit_index)
        inputs_two = payload[0][::-1]
        latent_two, det_two, saved_two = forward_block(
            inputs_two, onehot_rev, seg_rev, seg_rev_keys, places, same_rev, second_weights
        )
        latent_list.append(latent_two)
        logdet_list.append(det_two + payload[1][::-1])
        grad_two_in, grads_two = backward_block(
            inputs_two, onehot_rev, same_rev, second_weights, saved_two, cotangent[batch_index]
        )
        returned = grad_two_in[::-1]
        for bit_index in range(bit_count):
            returned = from_partner(returned, "seq", bit_index)
        grad_one_in, grads_one = backward_block(
            inputs_one, onehot_fwd, same_fwd, first_weights, saved_one, returned
        )
        grad_list.append(grad_one_in)
        grads_now = combine_grads(grads_one, grads_two)
        grad_totals = add_up(grad_totals, grads_now)
    grad_totals = (
        lax.psum_scatter(grad_totals[0], "rows", scatter_dimension=2, tiled=True),
        lax.psum_scatter(grad_totals[1], "rows", scatter_dimension=2, tiled=True),
        lax.psum_scatter(grad_totals[2], "rows", scatter_dimension=1, tiled=True),
        lax.psum_scatter(grad_totals[3], "rows", scatter_dimension=1, tiled=True),
        lax.psum_scatter(grad_totals[4], "rows", scatter_dimension=1, tiled=True),
        lax.psum_scatter(grad_totals[5], "rows", scatter_dimension=1, tiled=True),
        lax.psum_scatter(grad_totals[6], "rows", scatter_dimension=1, tiled=True),
        lax.psum_scatter(grad_totals[7], "rows", scatter_dimension=2, tiled=True),
    )
    summed = lax.psum(
        (
            grad_totals[0],
            grad_totals[1],
            grad_totals[2],
            grad_totals[3],
            grad_totals[4],
            grad_totals[5],
            grad_totals[6],
            grad_totals[7],
        ),
        "seq",
    )
    firsts = (m_in, m_table, m_qkv, m_o, m_up, m_down, m_out, m_gains)
    seconds = (v_in, v_table, v_qkv, v_o, v_up, v_down, v_out, v_gains)
    updates = [
        adam_step(
            masters[where_at],
            firsts[where_at],
            seconds[where_at],
            summed[where_at],
            RATES[where_at],
        )
        for where_at in range(8)
    ]
    return (
        jnp.stack(latent_list, 0),
        jnp.stack(logdet_list, 0),
        jnp.stack(grad_list, 0),
        updates[0][0],
        updates[0][1],
        updates[0][2],
        updates[1][0],
        updates[1][1],
        updates[1][2],
        updates[2][0],
        updates[2][1],
        updates[2][2],
        updates[3][0],
        updates[3][1],
        updates[3][2],
        updates[4][0],
        updates[4][1],
        updates[4][2],
        updates[5][0],
        updates[5][1],
        updates[5][2],
        updates[6][0],
        updates[6][1],
        updates[6][2],
        updates[7][0],
        updates[7][1],
        updates[7][2],
    )


def solution(mesh):
    return jax.shard_map(
        body,
        mesh=mesh,
        in_specs=(
            P("rows", "seq", None),
            P("rows", None),
            P("rows", None),
            P("rows", "seq", None),
            P(None, None, "rows"),
            P(None, None, "rows"),
            P(None, None, "rows"),
            P(None, None, "rows"),
            P(None, None, "rows"),
            P(None, None, "rows"),
            P(None, "rows", None),
            P(None, "rows", None),
            P(None, "rows", None),
            P(None, "rows", None),
            P(None, "rows", None),
            P(None, "rows", None),
            P(None, "rows", None),
            P(None, "rows", None),
            P(None, "rows", None),
            P(None, "rows", None),
            P(None, "rows", None),
            P(None, "rows", None),
            P(None, "rows", None),
            P(None, "rows", None),
            P(None, "rows", None),
            P(None, None, "rows"),
            P(None, None, "rows"),
            P(None, None, "rows"),
        ),
        out_specs=(
            P("rows", "seq", None),
            P("rows", "seq"),
            P("rows", "seq", None),
            P(None, None, "rows"),
            P(None, None, "rows"),
            P(None, None, "rows"),
            P(None, None, "rows"),
            P(None, None, "rows"),
            P(None, None, "rows"),
            P(None, "rows", None),
            P(None, "rows", None),
            P(None, "rows", None),
            P(None, "rows", None),
            P(None, "rows", None),
            P(None, "rows", None),
            P(None, "rows", None),
            P(None, "rows", None),
            P(None, "rows", None),
            P(None, "rows", None),
            P(None, "rows", None),
            P(None, "rows", None),
            P(None, "rows", None),
            P(None, "rows", None),
            P(None, "rows", None),
            P(None, None, "rows"),
            P(None, None, "rows"),
            P(None, None, "rows"),
        ),
        check_vma=False,
    )
```

profile of v0, /device:TPU:8, one launch (start us, length us, event | category | flops | bytes accessed | tf_op | source)
XLA Modules:
  0.0 2961.3 jit_solution(11886175757790176667)
XLA Ops:
  22.8 20.3 all_gather.96
  44.2 19.2 all_gather.98
  64.0 21.5 all_gather.105
  91.9 12.4 slice_reduce_fusion
  104.3 12.1 slice_reduce_fusion.5
  130.0 41.9 %all-gather.8.cloned.1.call-done = bf16[4,768,2304]{2,1,0:T(8,128)(2,1)} async-done(((bf16[4,48,2304]{2,1,0:T(8,128)(2,1)}), bf16[4,768,2304]{2,1,0:T(8,128)(2,1)}) %all-gather.8.cloned.1.call-update) | async-done | bytes 14155792 | tf_op jit(solution)/shard_map/all_gather | solution.py:354
  184.5 7.8 all_gather.108
  193.5 7.0 all_gather.112
  201.7 6.3 all_gather.116
  209.3 7.0 all_gather.100
  239.7 87.8 %all-gather.12.cloned.1.call-done = bf16[4,768,3072]{2,1,0:T(8,128)(2,1)} async-done(((bf16[4,48,3072]{2,1,0:T(8,128)(2,1)}), bf16[4,768,3072]{2,1,0:T(8,128)(2,1)}) %all-gather.12.cloned.1.call-update) | async-done | bytes 18874384 | tf_op jit(solution)/shard_map/all_gather | solution.py:356
  330.9 97.6 %all-gather.14.cloned.1.call-done = bf16[4,3072,768]{2,1,0:T(8,128)(2,1)} async-done(((bf16[4,192,768]{2,1,0:T(8,128)(2,1)}), bf16[4,3072,768]{2,1,0:T(8,128)(2,1)}) %all-gather.14.cloned.1.call-update) | async-done | bytes 18874384 | tf_op jit(solution)/shard_map/all_gather | solution.py:357
  465.5 7.7 all_gather.104
  474.5 7.1 all_gather.117
  483.6 6.6 all_gather.113
  493.9 6.6 all_gather.109
  574.6 6.3 all_gather.106
  593.9 6.8 all_gather.118
  614.6 6.5 all_gather.114
  653.0 6.5 all_gather.110
  677.0 6.6 all_gather.107
  705.5 6.3 all_gather.119
  733.3 6.8 all_gather.115
  762.9 6.5 all_gather.111
  922.5 6.2 reduce-scatter.91.cloned.1.call-done
  1000.0 13.2 reduce-scatter.69.cloned.1.call-done
  1014.5 18.9 reduce-scatter.85.cloned.1.call-done
  1046.6 6.6 reduce-scatter.93.cloned.1.call-done
  1168.3 18.9 reduce-scatter.87.cloned.1.call-done
  1200.3 6.5 reduce-scatter.95.cloned.1.call-done
  1275.3 9.1 reduce-scatter.81.cloned.1.call-done
  1285.6 18.9 reduce-scatter.89.cloned.1.call-done
  1317.6 6.7 reduce-scatter.97.cloned.1.call-done
  1338.2 10.4 copy.887
  1359.7 8.7 fusion.7
  1433.5 43.0 %fusion.5 = f32[4,768,2304]{2,1,0:T(8,128)} fusion(f32[1,768,2304]{2,1,0:T(8,128)} %convolution_bitcast_fusion.44, f32[1,768,2304]{2,1,0:T(8,128)} %convolution_bitcast_fusion.45, f32[1,768,2304]{2,1,0:T(8,128)} %convolution_bitcast_fusion.46, f32[1,768,2304]{2,1,0:T(8,128)} %convolution_bitcast_fusion.47, f32[1,768,2304]{2,1,0:T(8,128)} %convolution_bitcast_fusion.40, ...), kind=kLoop, calls=%fused_computation.8 | loop fusion | flops 106168320 | bytes 141557760 | tf_op jit(solution)/shard_map/add | solution.py:293
  1495.9 5.1 convolution_bitcast_fusion.5
  1501.0 5.1 convolution_bitcast_fusion.9
  1506.1 5.3 convolution_bitcast_fusion.13
  1511.5 6.1 convolution_bitcast_fusion.2
  1517.6 5.7 convolution_bitcast_fusion.6
  1533.4 5.4 convolution_bitcast_fusion.3
  1553.9 55.5 %fusion.3 = f32[4,3072,768]{2,1,0:T(8,128)} fusion(f32[1,3072,768]{2,1,0:T(8,128)} %convolution_bitcast_fusion.12, f32[1,3072,768]{2,1,0:T(8,128)} %convolution_bitcast_fusion.13, f32[1,3072,768]{2,1,0:T(8,128)} %convolution_bitcast_fusion.14, f32[1,3072,768]{2,1,0:T(8,128)} %convolution_bitcast_fusion.15, f32[1,3072,768]{2,1,0:T(8,128)} %convolution_bitcast_fusion.8, ...), kind=kLoop, calls=%fused_computation.5 | loop fusion | flops 141557760 | bytes 188743680 | tf_op jit(solution)/shard_map/add | solution.py:293
  1612.8 5.9 convolution_bitcast_fusion.20
  1618.7 5.8 convolution_bitcast_fusion.24
  1624.6 8.1 convolution_bitcast_fusion.28
  1632.7 8.0 convolution_bitcast_fusion.17
  1640.8 8.0 convolution_bitcast_fusion.21
  1648.9 7.1 convolution_bitcast_fusion.25
  1656.1 5.8 convolution_bitcast_fusion.29
  1661.9 5.5 convolution_bitcast_fusion.18
  1667.4 5.3 convolution_bitcast_fusion.22
  1672.8 5.8 convolution_bitcast_fusion.26
  1678.6 5.1 convolution_bitcast_fusion.30
  1683.8 5.1 convolution_bitcast_fusion.19
  1694.0 5.1 convolution_bitcast_fusion.27
  1704.3 58.5 %fusion.1 = f32[4,768,3072]{2,1,0:T(8,128)} fusion(f32[1,768,3072]{2,1,0:T(8,128)} %convolution_bitcast_fusion.28, f32[1,768,3072]{2,1,0:T(8,128)} %convolution_bitcast_fusion.29, f32[1,768,3072]{2,1,0:T(8,128)} %convolution_bitcast_fusion.30, f32[1,768,3072]{2,1,0:T(8,128)} %convolution_bitcast_fusion.31, f32[1,768,3072]{2,1,0:T(8,128)} %convolution_bitcast_fusion.24, ...), kind=kLoop, calls=%fused_computation.2 | loop fusion | flops 141557760 | bytes 188743680 | tf_op jit(solution)/shard_map/add | solution.py:293
  1782.2 104.5 %reduce-scatter.59.cloned.1.call-done = f32[4,48,2304]{2,1,0:T(8,128)} async-done(((f32[4,768,2304]{2,1,0:T(8,128)}), f32[4,48,2304]{2,1,0:T(8,128)}) %reduce-scatter.59.cloned.1.call-update) | async-done | bytes 1769488 | tf_op jit(solution)/shard_map/reduce_scatter | solution.py:402
  1886.7 372.4 %reduce-scatter.65.cloned.1.call-done = f32[4,192,768]{2,1,0:T(8,128)} async-done(((f32[4,3072,768]{2,1,0:T(8,128)}), f32[4,192,768]{2,1,0:T(8,128)}) %reduce-scatter.65.cloned.1.call-update) | async-done | bytes 2359312 | tf_op jit(solution)/shard_map/reduce_scatter | solution.py:405
  2259.1 371.6 %reduce-scatter.63.cloned.1.call-done = f32[4,48,3072]{2,1,0:T(8,128)} async-done(((f32[4,768,3072]{2,1,0:T(8,128)}), f32[4,48,3072]{2,1,0:T(8,128)}) %reduce-scatter.63.cloned.1.call-update) | async-done | bytes 2359312 | tf_op jit(solution)/shard_map/reduce_scatter | solution.py:404
  2652.7 38.2 %reduce-scatter.101.cloned.1.call-done = f32[48,10]{1,0:T(8,128)} async-done(((f32[768,10]{1,0:T(8,128)}), f32[48,10]{1,0:T(8,128)}) %reduce-scatter.101.cloned.1.call-update) | async-done | bytes 1936
  2691.9 57.8 %reduce-scatter.99.cloned.1.call-done = f32[48,96]{1,0:T(8,128)} async-done(((f32[768,96]{1,0:T(8,128)}), f32[48,96]{1,0:T(8,128)}) %reduce-scatter.99.cloned.1.call-update) | async-done | bytes 18448
  2751.4 10.3 all-reduce.3
  2766.6 166.1 %all-reduce.10.cloned.1.call-done = (f32[2,1000,48]{1,2,0:T(8,128)}, f32[4,48,2304]{2,1,0:T(8,128)}, f32[4,48,768]{2,1,0:T(8,128)}, f32[4,48,3072]{2,1,0:T(8,128)}, f32[4,192,768]{2,1,0:T(8,128)}) async-done(((f32[2,1000,48]{1,2,0:T(8,128)}, f32[4,48,2304]{2,1,0:T(8,128)}, f32[4,48,768]{2,1,0:T(8,128)}, f32[4,48,3072]{2,1,0:T(8,128)}, f32[4,192,768]{2,1,0:T(8,128)}), (f32[2,1000,48]{1,2,0:T(8,128)}, ...) | async-done | bytes 7461904 | tf_op jit(solution)/shard_map/psum | solution.py:409
  (3028 shorter events, 993.4 us)
Async XLA Ops:
  7.2 109.3 %all-gather.6.cloned.1.call-start = ((), (), s32[]{:S(2)}) async-start(), calls=%async_computation.22 | async-start | bytes 3342336 | tf_op jit(solution)/shard_map/all_gather | solution.py:353
  9.1 162.8 %all-gather.8.cloned.1.call-start = ((), (), s32[]{:S(2)}) async-start(), calls=%async_computation.23 | async-start | bytes 15040512 | tf_op jit(solution)/shard_map/all_gather | solution.py:354
  11.7 216.3 %all-gather.10.cloned.1.call-start = ((), (), s32[]{:S(2)}) async-start(), calls=%async_computation.24 | async-start | bytes 5013504 | tf_op jit(solution)/shard_map/all_gather | solution.py:355
  12.6 315.0 %all-gather.12.cloned.1.call-start = ((), (), s32[]{:S(2)}) async-start(), calls=%async_computation.25 | async-start | bytes 20054016 | tf_op jit(solution)/shard_map/all_gather | solution.py:356
  13.9 414.6 %all-gather.14.cloned.1.call-start = ((), (), s32[]{:S(2)}) async-start(), calls=%async_computation.26 | async-start | bytes 20054016 | tf_op jit(solution)/shard_map/all_gather | solution.py:357
  16.7 885.5 %reduce-scatter.75.cloned.1.call-start = ((), (), s32[]{:S(2)}) async-start(), calls=%async_computation.35 | async-start | bytes 1179648
  525.3 26.6 collective-permute-start
  536.3 16.5 collective-permute-start.9
  543.4 12.3 collective-permute-start.6
  550.6 5.8 collective-permute-start.3
  552.7 6.6 collective-permute-start.1
  553.6 7.6 collective-permute-start.10
  556.3 12.6 collective-permute-start.7
  557.2 90.5 %collective-permute-start.4 = (f32[64,48]{1,0:T(8,128)S(1)}, f32[64,48]{1,0:T(8,128)}, u32[]{:S(2)}, u32[]{:S(2)}) collective-permute-start(f32[64,48]{1,0:T(8,128)S(1)} %fusion.484), channel_id=1, source_target_pairs={{0,1},{1,0},{2,3},{3,2},{4,5},{5,4},{6,7},{7,6},{8,9},{9,8},{10,11... | collective-permute-start | bytes 36872 | tf_op jit(solution)/shard_map/ppermute | solution.py:31
  702.2 87.2 %collective-permute-start.2 = (f32[1,96]{1,0:T(1,128)}, f32[1,96]{1,0:T(1,128)}, u32[]{:S(2)}, u32[]{:S(2)}) collective-permute-start(f32[1,96]{1,0:T(1,128)} %slice.910), channel_id=1, source_target_pairs={{0,1},{2,3},{4,5},{6,7},{8,9},{10,11},{12,13},{14,15},{16,17},{18,... | collective-permute-start | bytes 1160 | tf_op jit(solution)/shard_map/ppermute | solution.py:27
  729.2 61.8 %collective-permute-start.11 = (f32[1,96]{1,0:T(1,128)}, f32[1,96]{1,0:T(1,128)}, u32[]{:S(2)}, u32[]{:S(2)}) collective-permute-start(f32[1,96]{1,0:T(1,128)} %slice.982), channel_id=1, source_target_pairs={{0,1},{2,3},{4,5},{6,7},{8,9},{10,11},{12,13},{14,15},{16,17},{18,... | collective-permute-start | bytes 1160 | tf_op jit(solution)/shard_map/ppermute | solution.py:27
  758.7 33.9 %collective-permute-start.8 = (f32[1,96]{1,0:T(1,128)}, f32[1,96]{1,0:T(1,128)}, u32[]{:S(2)}, u32[]{:S(2)}) collective-permute-start(f32[1,96]{1,0:T(1,128)} %slice.958), channel_id=1, source_target_pairs={{0,1},{2,3},{4,5},{6,7},{8,9},{10,11},{12,13},{14,15},{16,17},{18,... | collective-permute-start | bytes 1160 | tf_op jit(solution)/shard_map/ppermute | solution.py:27
  787.4 6.9 collective-permute-start.5
  795.2 5.6 collective-permute-start.22
  796.5 8.2 collective-permute-start.16
  797.8 7.9 collective-permute-start.25
  799.1 5.4 collective-permute-start.19
  852.2 52.0 %reduce-scatter.67.cloned.1.call-start = ((), (), s32[]{:S(2)}) async-start(), calls=%async_computation.31 | async-start | bytes 1179648
  868.0 41.0 %reduce-scatter.83.cloned.1.call-start = ((), (), s32[]{:S(2)}) async-start(), calls=%async_computation.39 | async-start | bytes 1179648
  882.7 46.1 %reduce-scatter.91.cloned.1.call-start = ((), (), s32[]{:S(2)}) async-start(), calls=%async_computation.43 | async-start | bytes 1179648
  897.9 100.9 %reduce-scatter.77.cloned.1.call-start = ((), (), s32[]{:S(2)}) async-start(), calls=%async_computation.36 | async-start | bytes 1179648
  975.9 37.4 %reduce-scatter.69.cloned.1.call-start = ((), (), s32[]{:S(2)}) async-start(), calls=%async_computation.32 | async-start | bytes 1179648
  985.1 48.2 %reduce-scatter.85.cloned.1.call-start = ((), (), s32[]{:S(2)}) async-start(), calls=%async_computation.40 | async-start | bytes 1179648
  992.4 60.8 %reduce-scatter.93.cloned.1.call-start = ((), (), s32[]{:S(2)}) async-start(), calls=%async_computation.44 | async-start | bytes 1179648
  998.6 162.2 %reduce-scatter.79.cloned.1.call-start = ((), (), s32[]{:S(2)}) async-start(), calls=%async_computation.37 | async-start | bytes 1179648
  1062.2 13.3 collective-permute-start.26
  1071.9 5.1 collective-permute-start.23
  1073.4 5.0 collective-permute-start.20
  1074.0 6.2 collective-permute-start.17
  1081.8 5.7 collective-permute-start.21
  1083.2 9.7 collective-permute-start.27
  1084.5 5.4 collective-permute-start.24
  1085.8 5.4 collective-permute-start.18
  1129.8 37.2 %reduce-scatter.71.cloned.1.call-start = ((), (), s32[]{:S(2)}) async-start(), calls=%async_computation.33 | async-start | bytes 1179648
  1139.0 48.1 %reduce-scatter.87.cloned.1.call-start = ((), (), s32[]{:S(2)}) async-start(), calls=%async_computation.41 | async-start | bytes 1179648
  1150.8 56.0 %reduce-scatter.95.cloned.1.call-start = ((), (), s32[]{:S(2)}) async-start(), calls=%async_computation.45 | async-start | bytes 1179648
  1160.6 113.4 %reduce-scatter.73.cloned.1.call-start = ((), (), s32[]{:S(2)}) async-start(), calls=%async_computation.34 | async-start | bytes 1179648
  1246.4 38.0 %reduce-scatter.81.cloned.1.call-start = ((), (), s32[]{:S(2)}) async-start(), calls=%async_computation.38 | async-start | bytes 1179648
  1256.2 48.2 %reduce-scatter.89.cloned.1.call-start = ((), (), s32[]{:S(2)}) async-start(), calls=%async_computation.42 | async-start | bytes 1179648
  1265.2 59.1 %reduce-scatter.97.cloned.1.call-start = ((), (), s32[]{:S(2)}) async-start(), calls=%async_computation.46 | async-start | bytes 1179648
  1273.8 506.3 %all-reduce.8.cloned.1.call-start = ((), (), s32[]{:S(2)}) async-start(), calls=%async_computation.49 | async-start | bytes 14155776
  1348.7 433.5 %reduce-scatter.61.cloned.1.call-start = ((), (), s32[]{:S(2)}) async-start(), calls=%async_computation.28 | async-start | bytes 10027008 | tf_op jit(solution)/shard_map/reduce_scatter | solution.py:403
  1368.4 518.2 %reduce-scatter.59.cloned.1.call-start = ((), (), s32[]{:S(2)}) async-start(), calls=%async_computation.27 | async-start | bytes 30081024 | tf_op jit(solution)/shard_map/reduce_scatter | solution.py:402
  1476.6 782.4 %reduce-scatter.65.cloned.1.call-start = ((), (), s32[]{:S(2)}) async-start(), calls=%async_computation.30 | async-start | bytes 40108032 | tf_op jit(solution)/shard_map/reduce_scatter | solution.py:405
  1609.5 1021.2 %reduce-scatter.63.cloned.1.call-start = ((), (), s32[]{:S(2)}) async-start(), calls=%async_computation.29 | async-start | bytes 40108032 | tf_op jit(solution)/shard_map/reduce_scatter | solution.py:404
  1763.2 927.7 %reduce-scatter.101.cloned.1.call-start = ((), (), s32[]{:S(2)}) async-start(), calls=%async_computation.48 | async-start | bytes 417792
  1776.7 973.0 %reduce-scatter.99.cloned.1.call-start = ((), (), s32[]{:S(2)}) async-start(), calls=%async_computation.47 | async-start | bytes 417792
  1778.5 1154.2 %all-reduce.10.cloned.1.call-start = ((), (), s32[]{:S(2)}) async-start(), calls=%async_computation.50 | async-start | bytes 14942208 | tf_op jit(solution)/shard_map/psum | solution.py:409
  1780.1 855.5 %copy-start.487 = (f32[64,96]{1,0:T(8,128)S(1)}, f32[64,96]{1,0:T(8,128)}, u32[]{:S(2)}) copy-start(f32[64,96]{1,0:T(8,128)} %copy-done.485) | copy-start | bytes 73732
  1780.2 855.5 %copy-start.637 = (pred[64]{0:T(512)(128)(4,1)S(1)}, pred[64]{0:T(512)(128)(4,1)}, u32[]{:S(2)}) copy-start(pred[64]{0:T(512)(128)(4,1)} %compare_and_fusion.4) | copy-start | bytes 196
  1780.2 855.5 %copy-start.780 = (f32[1,96]{1,0:T(1,128)S(1)}, f32[1,96]{1,0:T(1,128)}, u32[]{:S(2)}) copy-start(f32[1,96]{1,0:T(1,128)} %copy-done.778) | copy-start | bytes 1156
  1780.2 856.2 %copy-start.32 = (bf16[1,48,768]{2,1,0:T(8,128)(2,1)S(1)}, bf16[1,48,768]{2,1,0:T(8,128)(2,1)}, u32[]{:S(2)}) copy-start(bf16[1,48,768]{2,1,0:T(8,128)(2,1)} %copy-done.31) | copy-start | bytes 221188
  1781.2 855.3 %copy-start.493 = (f32[64,96]{1,0:T(8,128)S(1)}, f32[64,96]{1,0:T(8,128)}, u32[]{:S(2)}) copy-start(f32[64,96]{1,0:T(8,128)} %copy-done.491) | copy-start | bytes 73732
  1781.3 859.4 %copy-start.490 = (f32[64,96]{1,0:T(8,128)S(1)}, f32[64,96]{1,0:T(8,128)}, u32[]{:S(2)}) copy-start(f32[64,96]{1,0:T(8,128)} %copy-done.488) | copy-start | bytes 73732
  1781.3 859.4 %copy-start.496 = (f32[64,96]{1,0:T(8,128)S(1)}, f32[64,96]{1,0:T(8,128)}, u32[]{:S(2)}) copy-start(f32[64,96]{1,0:T(8,128)} %copy-done.494) | copy-start | bytes 73732
  2638.5 7.9 collective-permute-start.14
  2640.0 7.2 collective-permute-start.15
  2644.4 3.6 collective-permute-start.12
  2645.9 3.5 collective-permute-start.13
  (973 other events, 28685.4 us)
Sparse Core Ops, SparseCore 0:
  10.9 49.1 all-gather.5
  62.9 108.9 all-gather.7
  174.8 53.1 all-gather.9
  230.0 97.5 all-gather.11
  329.5 98.9 all-gather.13
  852.3 16.5 reduce-scatter.74
  871.2 17.4 reduce-scatter.66
  891.4 17.4 reduce-scatter.82
  911.3 17.4 reduce-scatter.90
  976.0 17.3 reduce-scatter.76
  995.8 17.4 reduce-scatter.68
  1015.9 17.4 reduce-scatter.84
  1035.7 17.4 reduce-scatter.92
  1129.9 17.4 reduce-scatter.78
  1149.5 17.4 reduce-scatter.70
  1169.7 17.4 reduce-scatter.86
  1189.3 17.4 reduce-scatter.94
  1246.5 17.4 reduce-scatter.72
  1266.9 17.4 reduce-scatter.80
  1287.0 17.4 reduce-scatter.88
  1306.8 17.4 reduce-scatter.96
  1348.8 150.7 all-reduce.7
  1503.6 111.5 reduce-scatter.60
  1619.8 266.8 reduce-scatter.58
  1891.5 367.5 reduce-scatter.64
  2263.7 366.9 reduce-scatter.62
  2635.0 55.9 reduce-scatter.100
  2695.0 54.5 reduce-scatter.98
  2753.4 179.2 all-reduce.9
where the time goes:
time: 2970 us; the launch traced here: 2960 us
  waiting for transfers between devices  1470 us (49%)
  matrix products  761 us (26%)
  other arithmetic  281 us (9%)
  local copies, waits for them, and re-layouts  200 us (7%)
  blocking collectives  180 us (6%)
  starting transfers between devices  43.5 us (1%)
  between operations  31.2 us (1%)
    reduce_scatter x1, waiting for transfers between devices, body(): lax.psum_scatter(grad_totals[5], 'rows', scatter_dimension=1, tiled=True)  372 us
    reduce_scatter x1, waiting for transfers between devices, body(): lax.psum_scatter(grad_totals[4], 'rows', scatter_dimension=1, tiled=True)  372 us
    unnamed x48, waiting for transfers between devices  210 us
    add x8, other arithmetic, add_up(): return tuple((left + right for left, right in zip(totals, extra)))  171 us
    psum x1, waiting for transfers between devices, body(): lax.psum((grad_totals[0], grad_totals[1], grad_totals[2], grad_totals[3],...  166 us
    all_gather x16, blocking collectives, forward_block(): kv_rows = lax.all_gather(qkv[:, width:], 'seq', axis=0, tiled=True)  108 us
    reduce_scatter x1, waiting for transfers between devices, body(): lax.psum_scatter(grad_totals[2], 'rows', scatter_dimension=1, tiled=True)  104 us
    all_gather x1, waiting for transfers between devices, body(): lax.all_gather(low_down, 'rows', axis=1, tiled=True)  97.6 us
  transfers between devices with their start and end apart: 57, of which 25 were waited for; matrix products, arithmetic and copies ran while one was open for 30% of the time, Pallas kernels for 0%

commit v1 on v0

v1 whole, which is shorter than its diff:
```python
import functools
from functools import partial

import jax
import jax.numpy as jnp
from jax import lax
from jax.experimental import pallas as pl
from jax.experimental.pallas import tpu as pltpu
from jax.sharding import PartitionSpec as P

HEADS = 12
HEAD_DIM = 64
LAYERS = 2
SEGS = 4
STEP = 10

EPS_NORM = 1e-05
MASKED = -1000000000.0
BETA_ONE = 0.9
BETA_TWO = 0.95
EPS_ADAM = 1e-08
DECAY = 0.1
RATES = (0.05, 0.3, 0.02, 0.05, 0.02, 0.01, 0.01, 0.3)

MESH_ID = pl.DeviceIdType.MESH
LANES = 128

def place():
    r = lax.axis_index("rows")
    x = lax.axis_index("seq")
    c = lax.rem(r, 2)
    y = lax.rem(r // 2, 2)
    z = r // 4
    return r, x, y, z, c

def units_of(shards, d1_share):
    units = []
    order = sorted(range(len(shards)), key=lambda a: shards[a].shape[0])
    layers = max(s.shape[0] // 2 for s in shards)
    todo = [(a, 0) for a in order if shards[a].shape[0] == 2]
    for l in range(layers):
        todo += [(a, l) for a in order if shards[a].shape[0] > 2]
    for a, l in todo:
        n, rows, cols = shards[a].shape
        half = cols // 2
        if rows >= 64:
            first = max(16, round(rows * d1_share / 16) * 16)
            split = (0, first)
        else:
            first = max(LANES, round(half * d1_share / LANES) * LANES)
            split = (1, first)
        units.append((a, l, n // 2, rows, half, split))
    return units

def wait_all_of(cell, sem):
    pltpu.make_async_copy(cell, cell, sem).wait()

def gather_kernel(units, n_arrays, *refs):
    srcs, outs = refs[:n_arrays], refs[n_arrays : 2 * n_arrays]
    send, recv, local = refs[2 * n_arrays :]
    r, x, y, z, c = place()
    stage = z // 2
    other = 1 - stage
    zi = lax.rem(z, 2)
    dev_x = (r, 1 - x)
    dev_y = (r + 2 - 4 * y, x)
    dev_s = (r + 1 - 2 * c, x)
    z_near = z + 1 - 2 * zi
    z_src = (z_near, other * 2, other * 2 + 1)
    dev_z = tuple((zz * 4 + y * 2 + c, x) for zz in z_src)
    barrier = pltpu.get_barrier_semaphore()
    partners = (dev_x, dev_y, dev_s) + dev_z
    for dev in partners:
        pl.semaphore_signal(barrier, 1, device_id=dev, device_id_type=MESH_ID)
    pl.semaphore_wait(barrier, len(partners))

    started = []

    def cell(u, zz, yy, cc, h=None, part=None):
        a, l, _, rows, half, (dim, first) = units[u]
        row0, nrow = (zz * 4 + yy * 2 + cc) * rows, rows
        col0, ncol = (0, 2 * half) if h is None else (h * half, half)
        if part is not None:
            if dim == 0:
                row0, nrow = (row0, first) if part == 0 else (row0 + first, rows - first)
            else:
                col0, ncol = (col0, first) if part == 0 else (col0 + first, half - first)
        if h is not None:
            col0 = pl.multiple_of(col0, LANES)
        return outs[a].at[l, pl.ds(pl.multiple_of(row0, 16), nrow), pl.ds(col0, ncol)]

    def own(u, b, h=None):
        a, l, layers, rows, half, _ = units[u]
        if h is None:
            return srcs[a].at[layers * b + l]
        return srcs[a].at[layers * b + l, :, pl.ds(pl.multiple_of(h * half, LANES), half)]

    def push(u, src, dst, idx, dev, slot=None):
        cp = pltpu.make_async_remote_copy(
            src_ref=src,
            dst_ref=dst,
            send_sem=send.at[u, idx if slot is None else slot],
            recv_sem=recv.at[u, idx],
            device_id=dev,
            device_id_type=MESH_ID,
        )
        cp.start()
        started.append(cp)

    def arrived(u, dst, idx):
        wait_all_of(dst, recv.at[u, idx])

    def begin(u):
        mine = cell(u, z, y, c, x)
        for i in range(2):
            push(u, own(u, other, x), mine, 1 + zi, dev_z[1 + i], slot=1 + i)
        push(u, own(u, stage, x), mine, 0, dev_z[0])
        push(u, own(u, stage, x), mine, 10, dev_y)
        push(u, own(u, stage), cell(u, z, y, c), 17, dev_s)
        pltpu.make_async_copy(own(u, stage), cell(u, z, y, c), local.at[u]).start()

    def spread(u):
        arrived(u, cell(u, z, 1 - y, c, x), 10)
        push(u, cell(u, z, 1 - y, c, x), cell(u, z, 1 - y, c, x), 6, dev_x)
        for j in range(3):
            piece = cell(u, z_src[j], y, c, x)
            arrived(u, piece, j)
            push(u, piece, piece, 3 + j, dev_x)
            push(u, piece, piece, 7 + j, dev_y)

    def corner(u):
        for j in range(3):
            arrived(u, cell(u, z_src[j], y, c, 1 - x), 3 + j)
            part = cell(u, z_src[j], y, c, 1 - x, 0)
            push(u, part, part, 11 + j, dev_y)
            arrived(u, cell(u, z_src[j], 1 - y, c, x), 7 + j)
            part = cell(u, z_src[j], 1 - y, c, x, 1)
            push(u, part, part, 14 + j, dev_x)
            slab = cell(u, z_src[j], y, c)
            push(u, slab, slab, 19 + j, dev_s)

    def finish(u):
        arrived(u, cell(u, z, 1 - y, c, 1 - x), 6)
        slab = cell(u, z, 1 - y, c)
        push(u, slab, slab, 18, dev_s)
        for j in range(3):
            arrived(u, cell(u, z_src[j], 1 - y, c, 1 - x, 0), 11 + j)
            arrived(u, cell(u, z_src[j], 1 - y, c, 1 - x, 1), 14 + j)
            slab = cell(u, z_src[j], 1 - y, c)
            push(u, slab, slab, 22 + j, dev_s)

    n = len(units)
    for u in range(n):
        begin(u)
    for t in range(n + 2):
        if t < n:
            spread(t)
        if 0 <= t - 1 < n:
            corner(t - 1)
        if 0 <= t - 2 < n:
            finish(t - 2)
    for u in range(n):
        arrived(u, cell(u, z, y, 1 - c), 17)
        arrived(u, cell(u, z, 1 - y, 1 - c), 18)
        for j in range(3):
            arrived(u, cell(u, z_src[j], y, 1 - c), 19 + j)
            arrived(u, cell(u, z_src[j], 1 - y, 1 - c), 22 + j)
        pltpu.make_async_copy(own(u, stage), cell(u, z, y, c), local.at[u]).wait()
    for cp in started:
        cp.wait_send()

def gather_blocks(shards, collective_id):
    units = units_of(shards, 0.5)
    out = [
        jax.ShapeDtypeStruct((s.shape[0] // 2, 16 * s.shape[1], s.shape[2]), s.dtype)
        for s in shards
    ]
    n = len(units)
    return pl.pallas_call(
        functools.partial(gather_kernel, units, len(shards)),
        out_shape=out,
        in_specs=[pl.BlockSpec(memory_space=pl.ANY)] * len(shards),
        out_specs=[pl.BlockSpec(memory_space=pl.ANY)] * len(shards),
        scratch_shapes=[
            pltpu.SemaphoreType.DMA((n, 25)),
            pltpu.SemaphoreType.DMA((n, 25)),
            pltpu.SemaphoreType.DMA((n,)),
        ],
        compiler_params=pltpu.CompilerParams(collective_id=collective_id, has_side_effects=True),
        name="gather_blocks",
    )(*shards)

def scatter_kernel(units, n_arrays, *refs):
    grads, outs = refs[:n_arrays], refs[n_arrays : 2 * n_arrays]
    n = len(units)
    rest = refs[2 * n_arrays :]
    acc, sib, in_x, in_y, in_d, in_z, fin = [rest[i * n : (i + 1) * n] for i in range(7)]
    send, recv, local, local_out = rest[7 * n :]
    r, x, y, z, c = place()
    stage = z // 2
    other = 1 - stage
    zi = lax.rem(z, 2)
    dev_x = (r, 1 - x)
    dev_y = (r + 2 - 4 * y, x)
    dev_s = (r + 1 - 2 * c, x)
    z_near = z + 1 - 2 * zi
    z_dst = (z_near, other * 2, other * 2 + 1)
    dev_z = tuple((zz * 4 + y * 2 + c, x) for zz in z_dst)
    barrier = pltpu.get_barrier_semaphore()
    partners = (dev_x, dev_y, dev_s) + dev_z
    for dev in partners:
        pl.semaphore_signal(barrier, 1, device_id=dev, device_id_type=MESH_ID)
    pl.semaphore_wait(barrier, len(partners))
    started = []

    def part_of(u, part):
        _, _, _, rows, half, (dim, first) = units[u]
        if dim == 0:
            return (pl.ds(0, first), pl.ds(0, half)) if part == 0 else (pl.ds(first, rows - first), pl.ds(0, half))
        return (pl.ds(0, rows), pl.ds(0, first)) if part == 0 else (pl.ds(0, rows), pl.ds(first, half - first))

    def push(u, src, dst, slot, dev, idx=None):
        cp = pltpu.make_async_remote_copy(
            src_ref=src,
            dst_ref=dst,
            send_sem=send.at[u, slot],
            recv_sem=recv.at[u, slot if idx is None else idx],
            device_id=dev,
            device_id_type=MESH_ID,
        )
        cp.start()
        started.append(cp)

    def arrived(u, dst, idx):
        wait_all_of(dst, recv.at[u, idx])

    def pieces(u, cc):
        a, l, _, rows, half, _ = units[u]
        for s in range(8):
            for h in range(2):
                row0 = pl.multiple_of((s * 2 + cc) * rows, 16)
                yield s, h, grads[a].at[l, pl.ds(row0, rows), pl.ds(h * half, half)]

    def begin(u):
        for s, h, src in pieces(u, 1 - c):
            push(u, src, sib[u].at[s, h], 18 + 2 * s + h, dev_s)
        for s, h, src in pieces(u, c):
            pltpu.make_async_copy(src, acc[u].at[s, h], local.at[u]).start()

    def chip_sum(u):
        wait_all_of(acc[u], local.at[u])
        for s in range(8):
            for h in range(2):
                arrived(u, sib[u].at[s, h], 18 + 2 * s + h)

        @pl.loop(0, 8)
        def _(s):
            for h in range(2):
                acc[u][s, h] = acc[u][s, h] + sib[u][s, h]

        for zz in range(4):
            slab = zz * 2 + 1 - y
            rs, cs = part_of(u, 0)
            push(u, acc[u].at[slab, 1 - x, rs, cs], in_d[u].at[zz, rs, cs], zz, dev_y)
            rs, cs = part_of(u, 1)
            push(u, acc[u].at[slab, 1 - x, rs, cs], in_d[u].at[zz, rs, cs], 4 + zz, dev_x)

    def side_sum(u):
        for zz in range(4):
            rs, cs = part_of(u, 0)
            arrived(u, in_d[u].at[zz, rs, cs], zz)
            acc[u][zz * 2 + y, 1 - x, rs, cs] = acc[u][zz * 2 + y, 1 - x, rs, cs] + in_d[u][zz, rs, cs]
            push(u, acc[u].at[zz * 2 + y, 1 - x], in_x[u].at[zz], 8 + zz, dev_x)
            rs, cs = part_of(u, 1)
            arrived(u, in_d[u].at[zz, rs, cs], 4 + zz)
            acc[u][zz * 2 + 1 - y, x, rs, cs] = acc[u][zz * 2 + 1 - y, x, rs, cs] + in_d[u][zz, rs, cs]
            push(u, acc[u].at[zz * 2 + 1 - y, x], in_y[u].at[zz], 12 + zz, dev_y)

    def plane_sum(u):
        for zz in range(4):
            arrived(u, in_x[u].at[zz], 8 + zz)
            arrived(u, in_y[u].at[zz], 12 + zz)
            acc[u][zz * 2 + y, x] = (
                acc[u][zz * 2 + y, x].astype(jnp.float32)
                + in_x[u][zz].astype(jnp.float32)
                + in_y[u][zz].astype(jnp.float32)
            ).astype(jnp.bfloat16)
        for i in range(2):
            push(u, acc[u].at[z_dst[1 + i] * 2 + y, x], in_z[u].at[1 + zi], 35 + i, dev_z[1 + i], idx=35 + zi)
        push(u, acc[u].at[z_near * 2 + y, x], in_z[u].at[0], 34, dev_z[0])

    def total(u):
        a, l, layers, rows, half, _ = units[u]
        for j in range(3):
            arrived(u, in_z[u].at[j], 34 + j)
        fin[u][0] = acc[u][z * 2 + y, x] + in_z[u][0]
        fin[u][1] = in_z[u][1] + in_z[u][2]
        for k, b in ((0, stage), (1, other)):
            dst = outs[a].at[layers * b + l, :, pl.ds(pl.multiple_of(x * half, LANES), half)]
            push(u, fin[u].at[k], dst, 16 + k, dev_x)
            pltpu.make_async_copy(fin[u].at[k], dst, local_out.at[u, k]).start()

    for u in range(n):
        begin(u)
    for t in range(n + 3):
        if t < n:
            chip_sum(t)
        if 0 <= t - 1 < n:
            side_sum(t - 1)
        if 0 <= t - 2 < n:
            plane_sum(t - 2)
        if 0 <= t - 3 < n:
            total(t - 3)
    for u in range(n):
        a, l, layers, rows, half, _ = units[u]
        for k, b in ((0, stage), (1, other)):
            there = outs[a].at[layers * b + l, :, pl.ds(pl.multiple_of((1 - x) * half, LANES), half)]
            arrived(u, there, 16 + k)
            dst = outs[a].at[layers * b + l, :, pl.ds(pl.multiple_of(x * half, LANES), half)]
            pltpu.make_async_copy(fin[u].at[k], dst, local_out.at[u, k]).wait()
    for cp in started:
        cp.wait_send()

def scatter_blocks(grads, collective_id):
    out = [
        jax.ShapeDtypeStruct((g.shape[0] * 2, g.shape[1] // 16, g.shape[2]), g.dtype) for g in grads
    ]
    units = units_of(out, 0.75)
    n = len(units)

    def bufs(lead):
        return [pltpu.VMEM(lead + (u[3], u[4]), jnp.bfloat16) for u in units]

    return pl.pallas_call(
        functools.partial(scatter_kernel, units, len(grads)),
        out_shape=out,
        in_specs=[pl.BlockSpec(memory_space=pl.ANY)] * len(grads),
        out_specs=[pl.BlockSpec(memory_space=pl.ANY)] * len(grads),
        scratch_shapes=bufs((8, 2))
        + bufs((8, 2))
        + bufs((4,))
        + bufs((4,))
        + bufs((4,))
        + bufs((3,))
        + bufs((2,))
        + [
            pltpu.SemaphoreType.DMA((n, 37)),
            pltpu.SemaphoreType.DMA((n, 37)),
            pltpu.SemaphoreType.DMA((n,)),
            pltpu.SemaphoreType.DMA((n, 2)),
        ],
        compiler_params=pltpu.CompilerParams(
            collective_id=collective_id, has_side_effects=True, vmem_limit_bytes=60 * 2**20
        ),
        name="scatter_blocks",
    )(*grads)


def dot(left, right, dims=((1,), (0,))):
    return lax.dot_general(left, right, (dims, ((), ())), preferred_element_type=jnp.float32)


def normalize(hidden):
    center = hidden - jnp.mean(hidden, -1, keepdims=True)
    inverse = lax.rsqrt(jnp.mean(center * center, -1, keepdims=True) + EPS_NORM)
    return (center * inverse, inverse)


def normalize_back(normed, inverse, grad_normed):
    mean_grad = jnp.mean(grad_normed, -1, keepdims=True)
    mean_proj = jnp.mean(grad_normed * normed, -1, keepdims=True)
    return inverse * (grad_normed - mean_grad - normed * mean_proj)


def padded(count, unit=256):
    return -(-count // unit) * unit


def side_columns(classes, channels, out, gains):
    table = padded(classes, 128)
    ends = [table, table + channels, table + channels + out, table + channels + out + gains]
    return ends, padded(ends[-1])


def pack_side(w_table, w_in, w_out, gains):
    blocks, classes, shard = w_table.shape
    ends, total = side_columns(classes, w_in.shape[1], w_out.shape[2], gains.shape[1])

    def gap(count):
        return jnp.zeros((blocks, shard, count), w_table.dtype)

    return jnp.concatenate(
        [
            jnp.swapaxes(w_table, 1, 2),
            gap(ends[0] - classes),
            jnp.swapaxes(w_in, 1, 2),
            w_out,
            jnp.swapaxes(gains, 1, 2),
            gap(total - ends[3]),
        ],
        2,
    )


def split_side(side, classes, channels, out, gains):
    ends, _ = side_columns(classes, channels, out, gains)
    return (
        jnp.swapaxes(side[..., :classes], -1, -2),
        jnp.swapaxes(side[..., ends[0] : ends[1]], -1, -2),
        side[..., ends[1] : ends[2]],
        jnp.swapaxes(side[..., ends[2] : ends[3]], -1, -2),
    )


def heads_of(flat, rows):
    return flat.reshape(rows, -1, HEADS, HEAD_DIM)


def attention_scores(query, key_rows, attend):
    scores = jnp.einsum(
        "rqhd,rkhd->rhqk", query, key_rows, preferred_element_type=jnp.float32
    ) * HEAD_DIM ** (-0.5)
    return jnp.where(attend[:, None], scores, MASKED)


def forward_block(inputs, seg_ids, labels, weights, sizes):
    w_qkv, w_o, w_up, w_down, side = weights
    classes, channels, out, gain_count = sizes
    ends, side_total = side_columns(*sizes)
    rows, length, _ = inputs.shape
    tokens = rows * length
    width = side.shape[0]
    places = jnp.arange(length, dtype=jnp.int32)
    attend = (seg_ids[:, :, None] == seg_ids[:, None, :]) & (
        places[None, :, None] >= places[None, None, :]
    )
    same_seg = jnp.concatenate(
        [jnp.zeros((rows, 1), bool), seg_ids[:, 1:] == seg_ids[:, :-1]], 1
    )[..., None]
    onehot = labels.reshape(tokens, 1) == jnp.arange(ends[0])[None, :]
    start = jnp.concatenate(
        [
            onehot.astype(jnp.bfloat16),
            inputs.reshape(tokens, channels).astype(jnp.bfloat16),
            jnp.zeros((tokens, side_total - ends[1]), jnp.bfloat16),
        ],
        1,
    )
    gain_rows = side[:, ends[2] : ends[3]].astype(jnp.float32).T
    hidden = dot(start, side, ((1,), (1,)))
    kept = []
    for layer in range(w_qkv.shape[0]):
        normed_a, inverse_a = normalize(hidden)
        act_a = (normed_a * gain_rows[2 * layer]).astype(jnp.bfloat16)
        qkv = dot(act_a, w_qkv[layer]).astype(jnp.bfloat16)
        query, key_rows, value_rows = [
            heads_of(qkv[:, i * width : (i + 1) * width], rows) for i in range(3)
        ]
        scores = attention_scores(query, key_rows, attend)
        row_top = jnp.max(scores, -1, keepdims=True)
        expo_rows = jnp.exp(scores - row_top)
        row_total = jnp.sum(expo_rows, -1, keepdims=True)
        soft_low = (expo_rows / row_total).astype(jnp.bfloat16)
        log_total = row_top + jnp.log(row_total)
        context = jnp.einsum(
            "rhqk,rkhd->rqhd", soft_low, value_rows, preferred_element_type=jnp.float32
        )
        context = context.reshape(tokens, width).astype(jnp.bfloat16)
        middle = hidden + dot(context, w_o[layer])
        normed_m, inverse_m = normalize(middle)
        act_m = (normed_m * gain_rows[2 * layer + 1]).astype(jnp.bfloat16)
        upper = dot(act_m, w_up[layer])
        gelu_low = jax.nn.gelu(upper, approximate=True).astype(jnp.bfloat16)
        hidden = middle + dot(gelu_low, w_down[layer])
        kept.append(
            (
                normed_a,
                inverse_a,
                act_a,
                qkv,
                log_total,
                context,
                normed_m,
                inverse_m,
                act_m,
                upper,
                gelu_low,
            )
        )
    normed_f, inverse_f = normalize(hidden)
    act_f = (normed_f * gain_rows[gain_count - 1]).astype(jnp.bfloat16)
    prediction = dot(act_f, side[:, ends[1] : ends[2]]).reshape(rows, length, out)
    previous = jnp.concatenate([jnp.zeros((rows, 1, out), jnp.float32), prediction[:, :-1]], 1)
    shift = jnp.where(same_seg, previous, 0.0)
    shift_alpha = shift[..., channels:]
    latent = (inputs - shift[..., :channels]) * jnp.exp(-shift_alpha)
    saved = (attend, same_seg, start, kept, normed_f, inverse_f, act_f, shift_alpha, latent)
    return (latent, -jnp.sum(shift_alpha, -1), saved)


def backward_block(grad_latent, saved, weights, sizes):
    w_qkv, w_o, w_up, w_down, side = weights
    classes, channels, out, gain_count = sizes
    ends, _ = side_columns(*sizes)
    attend, same_seg, start, kept, normed_f, inverse_f, act_f, shift_alpha, latent = saved
    rows, length, _ = latent.shape
    tokens = rows * length
    width = side.shape[0]
    factor = HEAD_DIM ** (-0.5)
    gain_rows = side[:, ends[2] : ends[3]].astype(jnp.float32).T
    scale_back = jnp.exp(-shift_alpha)
    grad_inputs = grad_latent * scale_back
    grad_prev = jnp.where(
        same_seg, jnp.concatenate([-grad_inputs, 1.0 - grad_latent * latent], 2), 0.0
    )
    grad_pred = jnp.concatenate([grad_prev[:, 1:], jnp.zeros((rows, 1, out), jnp.float32)], 1)
    grad_pred = grad_pred.reshape(tokens, out).astype(jnp.bfloat16)
    grad_act = dot(grad_pred, side[:, ends[1] : ends[2]], ((1,), (1,)))
    gain_grads = [None] * gain_count
    gain_grads[-1] = jnp.sum(grad_act * normed_f, 0)
    grad_hidden = normalize_back(normed_f, inverse_f, grad_act * gain_rows[gain_count - 1])
    pairs = [None] * w_qkv.shape[0]
    for layer in reversed(range(w_qkv.shape[0])):
        (
            normed_a,
            inverse_a,
            act_a,
            qkv,
            log_total,
            context,
            normed_m,
            inverse_m,
            act_m,
            upper,
            gelu_low,
        ) = kept[layer]
        grad_branch = grad_hidden.astype(jnp.bfloat16)
        grad_gelu = dot(grad_branch, w_down[layer], ((1,), (1,)))
        gelu_pull = jax.vjp(partial(jax.nn.gelu, approximate=True), upper)[1]
        grad_upper = gelu_pull(grad_gelu)[0].astype(jnp.bfloat16)
        grad_act_m = dot(grad_upper, w_up[layer], ((1,), (1,)))
        gain_grads[2 * layer + 1] = jnp.sum(grad_act_m * normed_m, 0)
        grad_middle = grad_hidden + normalize_back(
            normed_m, inverse_m, grad_act_m * gain_rows[2 * layer + 1]
        )
        grad_mid_low = grad_middle.astype(jnp.bfloat16)
        grad_context = heads_of(
            dot(grad_mid_low, w_o[layer], ((1,), (1,))).astype(jnp.bfloat16), rows
        )
        query, key_rows, value_rows = [
            heads_of(qkv[:, i * width : (i + 1) * width], rows) for i in range(3)
        ]
        soft_rows = jnp.exp(attention_scores(query, key_rows, attend) - log_total)
        soft_low = soft_rows.astype(jnp.bfloat16)
        grad_soft = jnp.einsum(
            "rqhd,rkhd->rhqk", grad_context, value_rows, preferred_element_type=jnp.float32
        )
        row_delta = jnp.sum(soft_rows * grad_soft, -1, keepdims=True)
        grad_scores = (soft_rows * (grad_soft - row_delta)).astype(jnp.bfloat16)
        grad_query = factor * jnp.einsum(
            "rhqk,rkhd->rqhd", grad_scores, key_rows, preferred_element_type=jnp.float32
        )
        grad_keys = factor * jnp.einsum(
            "rhqk,rqhd->rkhd", grad_scores, query, preferred_element_type=jnp.float32
        )
        grad_values = jnp.einsum(
            "rhqk,rqhd->rkhd", soft_low, grad_context, preferred_element_type=jnp.float32
        )
        grad_qkv = jnp.concatenate(
            [part.reshape(tokens, width) for part in (grad_query, grad_keys, grad_values)], 1
        ).astype(jnp.bfloat16)
        grad_act_a = dot(grad_qkv, w_qkv[layer], ((1,), (1,)))
        gain_grads[2 * layer] = jnp.sum(grad_act_a * normed_a, 0)
        grad_hidden = grad_middle + normalize_back(
            normed_a, inverse_a, grad_act_a * gain_rows[2 * layer]
        )
        pairs[layer] = (
            (act_a, grad_qkv),
            (context, grad_mid_low),
            (act_m, grad_upper),
            (gelu_low, grad_branch),
        )
    grad_start = grad_hidden.astype(jnp.bfloat16)
    grad_inputs = grad_inputs + dot(grad_start, side[:, ends[0] : ends[1]]).reshape(
        rows, length, channels
    )
    return grad_inputs, (
        pairs,
        (start[:, : ends[1]], grad_start),
        (act_f, grad_pred),
        jnp.stack(gain_grads, 1),
    )


def weight_grads(parts, side_total):
    pairs, (start, grad_start), (act_f, grad_pred), gain_grads = parts
    arrays = [
        jnp.stack([dot(*layer[i], ((0,), (0,))).astype(jnp.bfloat16) for layer in pairs], 0)
        for i in range(4)
    ]
    side = [
        dot(grad_start, start, ((0,), (0,))),
        dot(act_f, grad_pred, ((0,), (0,))),
        gain_grads,
    ]
    count = sum(part.shape[1] for part in side)
    side.append(jnp.zeros((gain_grads.shape[0], side_total - count), jnp.float32))
    side = jnp.concatenate(side, 1).astype(jnp.bfloat16)
    return arrays + [side[None]]


def adam_step(weight, first, second, grad, rate):
    first_new = BETA_ONE * first + (1.0 - BETA_ONE) * grad
    second_new = BETA_TWO * second + (1.0 - BETA_TWO) * grad * grad
    first_hat = first_new / (1.0 - BETA_ONE**STEP)
    second_hat = second_new / (1.0 - BETA_TWO**STEP)
    weight_new = weight - rate * (first_hat / (jnp.sqrt(second_hat) + EPS_ADAM) + DECAY * weight)
    return (first_new, second_new, weight_new)


def segment_of(places, seg_ends):
    return jnp.sum((places[None, :, None] >= seg_ends[:, None, :]).astype(jnp.int32), -1)


def row_facts(seg_lengths, class_labels, length):
    seg_ids = segment_of(jnp.arange(length, dtype=jnp.int32), jnp.cumsum(seg_lengths, 1))
    picked = seg_ids[:, :, None] == jnp.arange(SEGS)[None, None, :]
    return seg_ids, jnp.sum(jnp.where(picked, class_labels[:, None, :], 0), -1)


def staged(mine, low, sizes):
    half = lax.axis_size("rows") // 2
    second = lax.axis_index("rows") >= half
    swap = [(i, (i + half) % (2 * half)) for i in range(2 * half)]
    up = [(i, i + half) for i in range(half)]
    down = [(i + half, i) for i in range(half)]
    theirs = [lax.ppermute(part, "rows", swap) for part in mine]
    batch = [
        [jnp.where(second, b, a) for a, b in zip(mine, theirs)],
        [jnp.where(second, a, b) for a, b in zip(mine, theirs)],
    ]
    weights = list(gather_blocks(low, 1))
    weights[4] = weights[4][0]

    def facts(index):
        ahead, behind = batch[min(index, 1)], batch[max(index - 1, 0)]
        return [jnp.where(second, behind[i][:, ::-1], ahead[i]) for i in (2, 3)]

    steps = []
    arrived = None
    for index in range(3):
        inputs = batch[min(index, 1)][0]
        if arrived is None:
            inputs = jnp.where(second, 0.0, inputs)
        else:
            inputs = jnp.where(second, arrived[..., :-1], inputs)
        latent, logdet, saved = forward_block(inputs, *facts(index), weights, sizes)
        if arrived is not None:
            logdet = logdet + arrived[..., -1]
        steps.append((latent, logdet, saved))
        if index < 2:
            arrived = lax.ppermute(
                jnp.concatenate([latent, logdet[..., None]], 2)[:, ::-1], "rows", up
            )
    parts = []
    grad_inputs = []
    returned = jnp.zeros_like(batch[0][1])
    for index in range(3):
        grad_latent = jnp.where(second, batch[max(1 - index, 0)][1], returned)
        grad, part = backward_block(grad_latent, steps[2 - index][2], weights, sizes)
        parts.append(part)
        grad_inputs.append(grad)
        if index < 2:
            returned = lax.ppermute(grad[:, ::-1], "rows", down)
    chosen = jax.tree.map(lambda a, b: jnp.where(second, a, b), parts[0], parts[2])
    gain_grads = parts[1][3] + chosen[3]
    both = jax.tree.map(lambda a, b: jnp.concatenate([a, b], 0), parts[1], chosen)
    grads = weight_grads(both[:3] + (gain_grads,), low[4].shape[2])
    sums = scatter_blocks(grads, 2)

    def result(index):
        return jnp.concatenate([steps[index][0], steps[index][1][..., None]], 2)

    sent = jnp.where(second, result(1), jnp.pad(grad_inputs[1], ((0, 0), (0, 0), (0, 1))))
    received = lax.ppermute(sent, "rows", swap)
    outcome = jnp.where(second, result(2), received)
    patch_grad = jnp.where(second, received[..., :-1], grad_inputs[2])
    return outcome, patch_grad, sums


def unstaged(mine, low, sizes):
    inputs, cotangent, seg_ids, labels = mine
    whole = [lax.all_gather(part, "rows", axis=1, tiled=True) for part in low]

    def block(index):
        picked = [part[index * LAYERS : (index + 1) * LAYERS] for part in whole[:4]]
        return picked + [whole[4][index]]

    back = seg_ids[:, ::-1], labels[:, ::-1]
    latent_one, det_one, saved_one = forward_block(inputs, seg_ids, labels, block(0), sizes)
    latent_two, det_two, saved_two = forward_block(latent_one[:, ::-1], *back, block(1), sizes)
    outcome = jnp.concatenate([latent_two, (det_two + det_one[:, ::-1])[..., None]], 2)
    grad_mid, parts_two = backward_block(cotangent, saved_two, block(1), sizes)
    patch_grad, parts_one = backward_block(grad_mid[:, ::-1], saved_one, block(0), sizes)
    grads = [
        jnp.concatenate(pair, 0)
        for pair in zip(
            weight_grads(parts_one, low[4].shape[2]), weight_grads(parts_two, low[4].shape[2])
        )
    ]
    sums = [
        lax.psum(
            lax.psum_scatter(grad, "rows", scatter_dimension=1, tiled=True).astype(jnp.float32),
            "seq",
        )
        for grad in grads
    ]
    return outcome, patch_grad, sums


def body(
    patches,
    seg_lengths,
    class_labels,
    cotangent,
    w_in,
    m_in,
    v_in,
    w_table,
    m_table,
    v_table,
    w_qkv,
    m_qkv,
    v_qkv,
    w_o,
    m_o,
    v_o,
    w_up,
    m_up,
    v_up,
    w_down,
    m_down,
    v_down,
    w_out,
    m_out,
    v_out,
    gains,
    m_gains,
    v_gains,
):
    masters = (w_in, w_table, w_qkv, w_o, w_up, w_down, w_out, gains)
    low = [weight.astype(jnp.bfloat16) for weight in masters]
    sizes = (w_table.shape[1], w_in.shape[1], w_out.shape[2], gains.shape[1])
    shards = low[2:6] + [pack_side(low[1], low[0], low[6], low[7])]
    held, group, channels = patches.shape
    seq_count = lax.axis_size("seq")
    length = group * seq_count
    share = max(1, held // seq_count)
    copies = seq_count * share // held
    first_row = (lax.axis_index("seq") // copies) * share
    pieces = jnp.concatenate([patches.astype(jnp.float32), cotangent], 2)
    pieces = lax.all_gather(pieces, "seq", axis=1, tiled=True)
    pieces = lax.dynamic_slice_in_dim(pieces, first_row, share, 0)
    seg_ids, labels = row_facts(
        lax.dynamic_slice_in_dim(seg_lengths, first_row, share, 0),
        lax.dynamic_slice_in_dim(class_labels, first_row, share, 0),
        length,
    )
    mine = (pieces[..., :channels], pieces[..., channels:], seg_ids, labels)
    two_stages = seq_count == 2 and lax.axis_size("rows") == 16 and copies == 1
    outcome, patch_grad, sums = (staged if two_stages else unstaged)(mine, shards, sizes)
    results = lax.all_gather(jnp.concatenate([outcome, patch_grad], 2), "seq", axis=0)
    results = results[::copies].reshape((held,) + results.shape[2:])
    results = lax.dynamic_slice_in_dim(results, lax.axis_index("seq") * group, group, 1)
    sums = [total.astype(jnp.float32) / copies for total in sums]
    table, first, last, gain = split_side(sums[4], *sizes)
    grads = (first, table, sums[0], sums[1], sums[2], sums[3], last, gain)
    firsts = (m_in, m_table, m_qkv, m_o, m_up, m_down, m_out, m_gains)
    seconds = (v_in, v_table, v_qkv, v_o, v_up, v_down, v_out, v_gains)
    updates = [adam_step(*item) for item in zip(masters, firsts, seconds, grads, RATES)]
    return (
        results[..., :channels],
        results[..., channels],
        results[..., channels + 1 :],
    ) + tuple(part for update in updates for part in update)


def solution(mesh):
    tokens = P("rows", "seq", None)
    row = P("rows", None)
    last, middle = P(None, None, "rows"), P(None, "rows", None)
    weights = (last,) * 6 + (middle,) * 15 + (last,) * 3
    return jax.shard_map(
        body,
        mesh=mesh,
        in_specs=(tokens, row, row, tokens) + weights,
        out_specs=(tokens, P("rows", "seq"), tokens) + weights,
        check_vma=False,
    )
```

time: 2970 us -> 916 us (0.31)
  waiting for transfers between devices: 1470 us -> 1.5 us
  matrix products: 761 us -> 235 us
  Pallas kernels: 0 us -> 317 us
  blocking collectives: 180 us -> 11 us
  other arithmetic: 281 us -> 124 us
    reduce_scatter x4 -> x0, waiting for transfers between devices: 849 us -> none  [the longest x1 372 us: body(): lax.psum_scatter(grad_totals[5], 'rows', scatter_dimension=1, tiled=True)]
    dot_general x352 -> x106, matrix products: 761 us -> 235 us  [the longest x70 201 us: dot(): lax.dot_general(left, right, (dims, ((), ())), preferred_element_type=jnp...]
    pallas_call x0 -> x2, Pallas kernels: none -> 317 us  [the longest x1 177 us: scatter_blocks(): pl.pallas_call(functools.partial(scatter_kernel, units, len(grads)), out_...]
    all_gather x5 -> x0, waiting for transfers between devices: 232 us -> none  [the longest x1 97.6 us: body(): lax.all_gather(low_down, 'rows', axis=1, tiled=True)]
    unnamed x48 -> x0, waiting for transfers between devices: 210 us -> none
    psum x1 -> x0, waiting for transfers between devices: 166 us -> none  [body(): lax.psum((grad_totals[0], grad_totals[1], grad_totals[2], grad_totals[3],...]
    add x10 -> x5, other arithmetic: 171 us -> 4.92 us  [the longest x2 2.98 us: backward_block(): grad_inputs + dot(grad_start, side[:, ends[0]:ends[1]]).reshape(rows, len...]
    all_gather x19 -> x2, blocking collectives: 169 us -> 11 us  [the longest x1 5.64 us: body(): pieces = lax.all_gather(pieces, 'seq', axis=1, tiled=True)]
  transfers between devices with their start and end apart: 57 -> 9, of which waited for: 25 -> 1; matrix products, arithmetic and copies ran while one was open for 30% -> 43% of each run, Pallas kernels for 0% -> 35%
where the time goes in v1:
time: 916 us; the launch traced here: 905 us
  Pallas kernels  317 us (35%)
  matrix products  235 us (26%)
  local copies, waits for them, and re-layouts  188 us (21%)
  other arithmetic  124 us (14%)
  starting transfers between devices  20.2 us (2%)
  blocking collectives  11 us (1%)
    dot_general x70, matrix products, dot(): lax.dot_general(left, right, (dims, ((), ())), preferred_element_type=jnp...  201 us
    pallas_call x1, Pallas kernels, scatter_blocks(): pl.pallas_call(functools.partial(scatter_kernel, units, len(grads)), out_...  177 us
    pallas_call x1, Pallas kernels, gather_blocks(): pl.pallas_call(functools.partial(gather_kernel, units, len(shards)), out_...  140 us
    unnamed x743, local copies, waits for them, and re-layouts  50.6 us
    reshape x24, local copies, waits for them, and re-layouts, heads_of(): return flat.reshape(rows, -1, HEADS, HEAD_DIM)  34.9 us
    slice x24, local copies, waits for them, and re-layouts, forward_block(): qkv[:, i * width:(i + 1) * width]  32.3 us
    another operation x4, other arithmetic, weight_grads(): jnp.stack([dot(*layer[i], ((0,), (0,))).astype(jnp.bfloat16) for layer in...  21.7 us
    another operation x20, local copies, waits for them, and re-layouts, backward_block(): jnp.stack(gain_grads, 1)  18.8 us
  transfers between devices with their start and end apart: 9, of which 1 were waited for; matrix products, arithmetic and copies ran while one was open for 43% of the time, Pallas kernels for 35%

profile of v1, /device:TPU:8, one launch (start us, length us, event | category | flops | bytes accessed | tf_op | source)
XLA Modules:
  0.0 904.7 jit_solution(3307186186315428886)
XLA Ops:
  2.3 2.6 collective-permute-start.1
  8.4 5.6 all_gather.9
  15.1 2.7 collective-permute-start
  29.1 2.5 convert_element_type.417.refs_0_
  35.7 140.4 %gather_blocks.1 = (bf16[2,768,2304]{2,1,0:T(8,128)(2,1)}, bf16[2,768,768]{2,1,0:T(8,128)(2,1)}, bf16[2,768,3072]{2,1,0:T(8,128)(2,1)}, bf16[2,3072,768]{2,1,0:T(8,128)(2,1)}, bf16[1,768,1280]{2,1,0:T(8,128)(2,1)}) custom-call(bf16[4,48,2304]{2,1,0:T(8,128)(2,1)} %convert_element_type.417.refs_0_, bf16[4,48,768]{2,1,0:T(8,128)(2,1)} %convert_element_type.418.refs_1_, ...), custom_call_target="tpu_custom_call" | custom-call | tf_op jit(solution)/shard_map/gather_blocks/pallas_call | solution.py:179
  195.5 3.2 convolution_convert_fusion.11
  205.2 4.0 fusion.46
  209.2 2.1 fusion.495
  230.4 5.1 fusion.22
  235.6 2.1 fusion.498
  246.5 2.5 fusion.499
  250.2 3.2 convolution_convert_fusion.9
  271.7 6.9 multiply_convert_fusion.3
  300.2 6.1 multiply_convert_fusion.2
  310.0 2.1 fusion.428
  319.8 5.3 collective-permute-start.4
  337.2 2.6 fusion.506
  340.9 3.1 convolution_convert_fusion.7
  361.0 7.1 broadcast_select_fusion.1
  390.2 6.8 broadcast_select_fusion
  404.7 2.6 multiply_reduce_fusion.11
  407.6 5.4 fusion.113
  413.1 2.3 multiply_reduce_fusion.12
  419.2 2.2 fusion.239
  425.6 2.8 multiply_reduce_fusion.13
  430.3 5.7 fusion.106
  436.1 2.9 multiply_reduce_fusion.14
  443.5 2.2 fusion.240
  450.2 2.7 multiply_reduce_fusion.15
  479.4 2.6 multiply_reduce_fusion.16
  483.0 5.2 fusion.99
  488.2 5.1 multiply_reduce_fusion.17
  500.4 2.3 fusion.241
  506.7 4.6 multiply_reduce_fusion.18
  513.2 5.5 fusion.92
  518.8 2.9 multiply_reduce_fusion.19
  529.4 2.3 fusion.242
  535.7 4.4 multiply_reduce_fusion.20
  559.0 4.7 collective-permute-start.7
  569.5 2.6 multiply_reduce_fusion.6
  573.2 6.7 broadcast_select_fusion.2
  579.9 2.1 multiply_reduce_fusion.7
  589.3 2.3 fusion.243
  596.9 4.1 multiply_reduce_fusion.8
  601.6 2.2 broadcast_select_fusion.9
  603.8 6.7 broadcast_select_fusion.3
  610.6 3.0 multiply_reduce_fusion.9
  619.2 2.2 fusion.244
  625.6 2.2 multiply_reduce_fusion.10
  629.6 2.1 broadcast_select_fusion.7
  634.5 6.8 fusion.51
  646.4 4.3 fusion.50
  650.8 8.4 pad_maximum_fusion.1.refs_3_
  659.2 3.5 fusion.53
  666.7 3.5 pad_maximum_fusion.2.refs_0_
  670.2 6.3 fusion.48
  676.5 4.5 fusion.49
  681.1 8.2 pad_maximum_fusion.refs_2_
  689.9 3.1 concatenate.245.refs_4_
  693.0 176.9 %scatter_blocks.1 = (bf16[4,48,2304]{2,1,0:T(8,128)(2,1)}, bf16[4,48,768]{2,1,0:T(8,128)(2,1)}, bf16[4,48,3072]{2,1,0:T(8,128)(2,1)}, bf16[4,192,768]{2,1,0:T(8,128)(2,1)}, bf16[2,48,1280]{2,1,0:T(8,128)(2,1)}) custom-call(bf16[2,768,2304]{2,1,0:T(8,128)(2,1)} %pad_maximum_fusion.2.refs_0_, bf16[2,768,768]{2,1,0:T(8,128)(2,1)} %pad_maximum_fusion.3.refs_1_, ...), custom_call_target="tpu_custom_call" | custom-call | tf_op jit(solution)/shard_map/scatter_blocks/pallas_call | solution.py:334
  875.2 3.3 multiply_subtract_fusion.2
  880.5 4.4 multiply_subtract_fusion.1
  886.5 4.1 multiply_subtract_fusion
  897.5 5.4 all-gather
  (1171 shorter events, 334.7 us)
Async XLA Ops:
  0.7 27.0 %copy-start.113 = (f32[2,1000,48]{1,2,0:T(8,128)S(1)}, f32[2,1000,48]{1,2,0:T(8,128)}, u32[]{:S(2)}) copy-start(f32[2,1000,48]{1,2,0:T(8,128)} %param.35) | copy-start | bytes 1152004
  0.7 27.7 %copy-start.76 = (f32[4,48,768]{2,1,0:T(8,128)S(1)}, f32[4,48,768]{2,1,0:T(8,128)}, u32[]{:S(2)}) copy-start(f32[4,48,768]{2,1,0:T(8,128)} %param.41) | copy-start | bytes 1769476
  2.3 181.6 %collective-permute-start.1 = (s32[2,128]{1,0:T(2,128)}, s32[2,128]{1,0:T(2,128)}, u32[]{:S(2)}, u32[]{:S(2)}) collective-permute-start(s32[2,128]{1,0:T(2,128)} %convert_reduce_fusion), channel_id=1, source_target_pairs={{0,16},{2,18},{4,20},{6,22},{8,24},{10,26},{12,28},{14,30},{16,0},... | collective-permute-start | bytes 3080 | tf_op jit(solution)/shard_map/ppermute | solution.py:637
  6.3 176.1 %collective-permute-start.2 = (s32[2,128]{1,0:T(2,128)}, s32[2,128]{1,0:T(2,128)}, u32[]{:S(2)}, u32[]{:S(2)}) collective-permute-start(s32[2,128]{1,0:T(2,128)} %select_reduce_fusion), channel_id=1, source_target_pairs={{0,16},{2,18},{4,20},{6,22},{8,24},{10,26},{12,28},{14,30},{16,0},... | collective-permute-start | bytes 3080 | tf_op jit(solution)/shard_map/ppermute | solution.py:637
  15.0 229.0 %copy-start.129 = (f32[2,128,48]{1,0,2:T(2,128)}, f32[2,128,48]{1,0,2:T(2,128)S(1)}, u32[]{:S(2)}) copy-start(f32[2,128,48]{1,0,2:T(2,128)S(1)} %copy.1003) | copy-start | bytes 147460
  15.1 16.5 %copy-start.47 = (f32[4,48,3072]{2,1,0:T(8,128)S(1)}, f32[4,48,3072]{2,1,0:T(8,128)}, u32[]{:S(2)}) copy-start(f32[4,48,3072]{2,1,0:T(8,128)} %param.44) | copy-start | bytes 7077892
  15.1 176.4 %collective-permute-start = (f32[2,128,48]{1,0,2:T(2,128)S(1)}, f32[2,128,48]{1,0,2:T(2,128)S(1)}, u32[]{:S(2)}, u32[]{:S(2)}) collective-permute-start(f32[2,128,48]{1,0,2:T(2,128)S(1)} %copy.1003), channel_id=1, source_target_pairs={{0,16},{2,18},{4,20},{6,22},{8,24},{10,26},{12,28},{14,30},{16,0},... | collective-permute-start | bytes 147464 | tf_op jit(solution)/shard_map/ppermute | solution.py:637
  19.3 383.5 %collective-permute-start.5 = (f32[2,128,48]{1,0,2:T(2,128)}, f32[2,128,48]{1,0,2:T(2,128)}, u32[]{:S(2)}, u32[]{:S(2)}) collective-permute-start(f32[2,128,48]{1,0,2:T(2,128)} %copy.1004), channel_id=1, source_target_pairs={{0,16},{2,18},{4,20},{6,22},{8,24},{10,26},{12,28},{14,30},{16,0},... | collective-permute-start | bytes 147464 | tf_op jit(solution)/shard_map/ppermute | solution.py:637
  35.7 143.8 %copy-start.224 = (f32[2,5,48]{2,0,1:T(2,128)S(1)}, f32[2,5,48]{2,0,1:T(2,128)}, u32[]{:S(2)}) copy-start(f32[2,5,48]{2,0,1:T(2,128)} %broadcast_multiply_fusion) | copy-start | bytes 5764
  35.7 144.6 %copy-start.223 = (f32[2,5,48]{2,0,1:T(2,128)S(1)}, f32[2,5,48]{2,0,1:T(2,128)}, u32[]{:S(2)}) copy-start(f32[2,5,48]{2,0,1:T(2,128)} %broadcast_multiply_fusion.2) | copy-start | bytes 5764
  35.7 145.3 %copy-start.214 = (f32[2,48,48]{2,1,0:T(8,128)S(1)}, f32[2,48,48]{2,1,0:T(8,128)}, u32[]{:S(2)}) copy-start(f32[2,48,48]{2,1,0:T(8,128)} %param.33) | copy-start | bytes 55300
  176.1 10.7 %copy-start.211 = (pred[128,128]{0,1:T(8,128)(4,1)S(1)}, pred[128,128]{0,1:T(8,128)(4,1)}, u32[]{:S(2)}) copy-start(pred[128,128]{0,1:T(8,128)(4,1)} %iota_compare_fusion.3) | copy-start | bytes 49156
  178.8 14.5 %copy-start.1 = (bf16[1,768,1280]{2,1,0:T(8,128)(2,1)S(1)}, bf16[1,768,1280]{2,1,0:T(8,128)(2,1)}, u32[]{:S(2)}) copy-start(bf16[1,768,1280]{2,1,0:T(8,128)(2,1)} %get-tuple-element.37) | copy-start | bytes 5898244
  200.4 8.8 slice-start.15
  211.3 18.2 %copy-start.55 = (f32[256,768]{1,0:T(8,128)}, f32[256,768]{1,0:T(8,128)S(1)}, u32[]{:S(2)}) copy-start(f32[256,768]{1,0:T(8,128)S(1)} %get-tuple-element.365) | copy-start | bytes 2359300
  240.7 3.4 collective-permute-start.3
  249.0 20.3 %copy-start.17 = (f32[256,768]{1,0:T(8,128)}, f32[256,768]{1,0:T(8,128)S(1)}, u32[]{:S(2)}) copy-start(f32[256,768]{1,0:T(8,128)S(1)} %get-tuple-element.373) | copy-start | bytes 2359300
  270.1 8.5 copy-start.21
  270.1 8.5 copy-start.231
  270.1 8.5 slice-start.21
  270.1 11.2 %slice-start.35 = ((s8[7077888]{0:T(1024)(128)(4,1)}), s8[4194304]{0:T(1024)(128)(4,1)S(1)}, s32[]{:S(2)}) async-start(s8[7077888]{0:T(1024)(128)(4,1)} %bitcast.719), calls=%async_computation.35 | async-start | bytes 8388608
  270.4 8.2 copy-start.254
  271.7 9.6 %slice-start.36 = ((s8[7077888]{0:T(1024)(128)(4,1)}), s8[2883584]{0:T(1024)(128)(4,1)S(1)}, s32[]{:S(2)}) async-start(s8[7077888]{0:T(1024)(128)(4,1)} %bitcast.719), calls=%async_computation.36 | async-start | bytes 5767168
  280.1 17.8 %copy-start.23 = (f32[256,768]{1,0:T(8,128)}, f32[256,768]{1,0:T(8,128)S(1)}, u32[]{:S(2)}) copy-start(f32[256,768]{1,0:T(8,128)S(1)} %get-tuple-element.381) | copy-start | bytes 2359300
  298.0 8.4 slice-start.24
  308.1 25.5 %copy-start.66 = (bf16[256,1024]{1,0:T(8,128)(2,1)S(1)}, bf16[256,1024]{1,0:T(8,128)(2,1)}, u32[]{:S(2)}) copy-start(bf16[256,1024]{1,0:T(8,128)(2,1)} %fusion.271) | copy-start | bytes 1572868
  308.1 25.5 %copy-start.68 = (bf16[256,1024]{1,0:T(8,128)(2,1)S(1)}, bf16[256,1024]{1,0:T(8,128)(2,1)}, u32[]{:S(2)}) copy-start(bf16[256,1024]{1,0:T(8,128)(2,1)} %copy-done.67) | copy-start | bytes 1572868
  319.8 10.2 %collective-permute-start.4 = (f32[2,128,49]{1,0,2:T(2,128)}, f32[2,128,49]{1,0,2:T(2,128)S(1)}, u32[]{:S(2)}, u32[]{:S(2)}) collective-permute-start(f32[2,128,49]{1,0,2:T(2,128)} %rev.29), channel_id=1, source_target_pairs={{0,16},{2,18},{4,20},{6,22},{8,24},{10,26},{12,28},{14,30},{1,17},... | collective-permute-start | bytes 150536 | tf_op jit(solution)/shard_map/ppermute | solution.py:662
  359.5 8.6 slice-start.27
  359.5 11.9 %slice-start.37 = ((s8[7077888]{0:T(1024)(128)(4,1)}), s8[4194304]{0:T(1024)(128)(4,1)S(1)}, s32[]{:S(2)}) async-start(s8[7077888]{0:T(1024)(128)(4,1)} %bitcast.721), calls=%async_computation.37 | async-start | bytes 8388608
  360.1 8.0 copy-start.31
  360.1 7.9 copy-start.238
  361.0 10.4 %slice-start.38 = ((s8[7077888]{0:T(1024)(128)(4,1)}), s8[2883584]{0:T(1024)(128)(4,1)S(1)}, s32[]{:S(2)}) async-start(s8[7077888]{0:T(1024)(128)(4,1)} %bitcast.721), calls=%async_computation.38 | async-start | bytes 5767168
  388.7 8.3 slice-start.30
  389.3 26.1 %copy-start.244 = (f32[256]{0:T(256)}, f32[256]{0:T(256)S(1)}, u32[]{:S(2)}) copy-start(f32[256]{0:T(256)S(1)} %broadcast_multiply_fusion.34) | copy-start | bytes 3076
  390.2 25.2 %copy-start.272 = (f32[256]{0:T(256)}, f32[256]{0:T(256)S(1)}, u32[]{:S(2)}) copy-start(f32[256]{0:T(256)S(1)} %add_rsqrt_fusion.1) | copy-start | bytes 3076
  404.5 8.5 slice-start
  425.6 10.5 %slice-start.3 = ((s8[9437184]{0:T(1024)(128)(4,1)}), s8[4194304]{0:T(1024)(128)(4,1)S(1)}, s32[]{:S(2)}) async-start(s8[9437184]{0:T(1024)(128)(4,1)} %bitcast.697), calls=%async_computation.3 | async-start | bytes 8388608
  430.3 8.7 copy-start.59
  460.2 16.4 %collective-permute-start.6 = (f32[2,128,48]{1,0,2:T(2,128)}, f32[2,128,48]{1,0,2:T(2,128)}, u32[]{:S(2)}, u32[]{:S(2)}) collective-permute-start(f32[2,128,48]{1,0,2:T(2,128)} %rev.32), channel_id=1, source_target_pairs={{16,0},{18,2},{20,4},{22,6},{24,8},{26,10},{28,12},{30,14},{17,1},... | collective-permute-start | bytes 147464 | tf_op jit(solution)/shard_map/ppermute | solution.py:674
  506.7 12.0 %slice-start.6 = ((s8[9437184]{0:T(1024)(128)(4,1)}), s8[4194304]{0:T(1024)(128)(4,1)S(1)}, s32[]{:S(2)}) async-start(s8[9437184]{0:T(1024)(128)(4,1)} %bitcast.699), calls=%async_computation.6 | async-start | bytes 8388608
  540.2 29.3 %copy-start.222 = (f32[256]{0:T(256)S(1)}, f32[256]{0:T(256)}, u32[]{:S(2)}) copy-start(f32[256]{0:T(256)} %copy-done.220) | copy-start | bytes 3076
  548.2 16.8 %collective-permute-start.8 = (f32[2,128,48]{1,0,2:T(2,128)}, f32[2,128,48]{1,0,2:T(2,128)}, u32[]{:S(2)}, u32[]{:S(2)}) collective-permute-start(f32[2,128,48]{1,0,2:T(2,128)} %rev.33), channel_id=1, source_target_pairs={{16,0},{18,2},{20,4},{22,6},{24,8},{26,10},{28,12},{30,14},{17,1},... | collective-permute-start | bytes 147464 | tf_op jit(solution)/shard_map/ppermute | solution.py:674
  559.0 336.7 %collective-permute-start.7 = (f32[2,128,49]{1,0,2:T(2,128)}, f32[2,128,49]{1,0,2:T(2,128)}, u32[]{:S(2)}, u32[]{:S(2)}) collective-permute-start(f32[2,128,49]{1,0,2:T(2,128)} %pad_select_fusion.3), channel_id=1, source_target_pairs={{0,16},{2,18},{4,20},{6,22},{8,24},{10,26},{12,28},{14,30},{16,0},... | collective-permute-start | bytes 150536 | tf_op jit(solution)/shard_map/ppermute | solution.py:685
  569.5 10.4 %slice-start.9 = ((s8[9437184]{0:T(1024)(128)(4,1)}), s8[4194304]{0:T(1024)(128)(4,1)S(1)}, s32[]{:S(2)}) async-start(s8[9437184]{0:T(1024)(128)(4,1)} %bitcast.701), calls=%async_computation.9 | async-start | bytes 8388608
  601.6 8.9 slice-start.12
  650.8 8.4 copy-start.130
  650.8 8.4 copy-start.171
  650.8 8.4 copy-start.182
  681.1 8.3 copy-start.112
  681.1 8.3 copy-start.176
  681.1 8.3 copy-start.216
  681.1 8.3 copy-start.217
  692.9 178.1 %copy-start.147 = (f32[2,48,48]{1,2,0:T(8,128)S(1)}, f32[2,48,48]{1,2,0:T(8,128)}, u32[]{:S(2)}) copy-start(f32[2,48,48]{1,2,0:T(8,128)} %copy-done.146) | copy-start | bytes 55300
  692.9 178.1 %copy-start.202 = (f32[2,48,48]{1,2,0:T(8,128)S(1)}, f32[2,48,48]{1,2,0:T(8,128)}, u32[]{:S(2)}) copy-start(f32[2,48,48]{1,2,0:T(8,128)} %copy.947) | copy-start | bytes 55300
  692.9 178.1 %copy-start.203 = (f32[2,48,48]{1,2,0:T(8,128)S(1)}, f32[2,48,48]{1,2,0:T(8,128)}, u32[]{:S(2)}) copy-start(f32[2,48,48]{1,2,0:T(8,128)} %copy.959) | copy-start | bytes 55300
  692.9 178.2 %copy-start.114 = (f32[2,1000,48]{1,2,0:T(8,128)S(1)}, f32[2,1000,48]{1,2,0:T(8,128)}, u32[]{:S(2)}) copy-start(f32[2,1000,48]{1,2,0:T(8,128)} %param.35) | copy-start | bytes 1152004
  692.9 178.2 %copy-start.174 = (f32[2,1000,48]{1,2,0:T(8,128)S(1)}, f32[2,1000,48]{1,2,0:T(8,128)}, u32[]{:S(2)}) copy-start(f32[2,1000,48]{1,2,0:T(8,128)} %param.37) | copy-start | bytes 1152004
  692.9 178.2 %copy-start.175 = (f32[2,1000,48]{1,2,0:T(8,128)S(1)}, f32[2,1000,48]{1,2,0:T(8,128)}, u32[]{:S(2)}) copy-start(f32[2,1000,48]{1,2,0:T(8,128)} %param.36) | copy-start | bytes 1152004
  692.9 179.4 %copy-start.144 = (f32[4,48,768]{2,1,0:T(8,128)S(1)}, f32[4,48,768]{2,1,0:T(8,128)}, u32[]{:S(2)}) copy-start(f32[4,48,768]{2,1,0:T(8,128)} %param.42) | copy-start | bytes 1769476
  886.5 9.2 %copy-start.137 = (f32[2,128,96]{1,0,2:T(2,128)S(1)}, f32[2,128,96]{1,0,2:T(2,128)}, u32[]{:S(2)}) copy-start(f32[2,128,96]{1,0,2:T(2,128)} %copy-done.136) | copy-start | bytes 294916
  886.5 9.2 %copy-start.151 = (f32[2,128,48]{1,0,2:T(2,128)S(1)}, f32[2,128,48]{1,0,2:T(2,128)}, u32[]{:S(2)}) copy-start(f32[2,128,48]{1,0,2:T(2,128)} %copy-done.150) | copy-start | bytes 147460
  886.5 10.1 %copy-start.200 = (f32[2,128,48]{1,0,2:T(2,128)S(1)}, f32[2,128,48]{1,0,2:T(2,128)}, u32[]{:S(2)}) copy-start(f32[2,128,48]{1,0,2:T(2,128)} %get-tuple-element.310) | copy-start | bytes 147460
  886.5 10.1 %copy-start.274 = (f32[2,128,1]{1,0,2:T(2,128)S(1)}, f32[2,128,1]{1,0,2:T(2,128)}, u32[]{:S(2)}) copy-start(f32[2,128,1]{1,0,2:T(2,128)} %slice_add_fusion) | copy-start | bytes 3076
  (302 other events, 1006.5 us)

commit v2 on v1

--- a/solution.py
+++ b/solution.py
@@ -25,6 +25,7 @@
 MESH_ID = pl.DeviceIdType.MESH
 LANES = 128
 
+
 def place():
     r = lax.axis_index("rows")
     x = lax.axis_index("seq")
@@ -32,6 +33,7 @@
     y = lax.rem(r // 2, 2)
     z = r // 4
     return r, x, y, z, c
+
 
 def units_of(shards, d1_share):
     units = []
@@ -52,8 +54,10 @@
         units.append((a, l, n // 2, rows, half, split))
     return units
 
+
 def wait_all_of(cell, sem):
     pltpu.make_async_copy(cell, cell, sem).wait()
+
 
 def gather_kernel(units, n_arrays, *refs):
     srcs, outs = refs[:n_arrays], refs[n_arrays : 2 * n_arrays]
@@ -74,6 +78,8 @@
         pl.semaphore_signal(barrier, 1, device_id=dev, device_id_type=MESH_ID)
     pl.semaphore_wait(barrier, len(partners))
 
+    inner = stage != zi
+    dev_inner = ((1 + other) * 4 + y * 2 + c, x)
     started = []
 
     def cell(u, zz, yy, cc, h=None, part=None):
@@ -110,10 +116,24 @@
     def arrived(u, dst, idx):
         wait_all_of(dst, recv.at[u, idx])
 
+    def relay_copy(u, piece, j):
+        return pltpu.make_async_remote_copy(
+            src_ref=piece,
+            dst_ref=piece,
+            send_sem=send.at[u, 24 + j],
+            recv_sem=recv.at[u, j],
+            device_id=dev_z[0],
+            device_id_type=MESH_ID,
+        )
+
+    def relay(u, piece, j):
+        @pl.when(inner)
+        def _():
+            relay_copy(u, piece, j).start()
+
     def begin(u):
         mine = cell(u, z, y, c, x)
-        for i in range(2):
-            push(u, own(u, other, x), mine, 1 + zi, dev_z[1 + i], slot=1 + i)
+        push(u, own(u, other, x), mine, 1 + zi, dev_inner, slot=1)
         push(u, own(u, stage, x), mine, 0, dev_z[0])
         push(u, own(u, stage, x), mine, 10, dev_y)
         push(u, own(u, stage), cell(u, z, y, c), 17, dev_s)
@@ -125,6 +145,8 @@
         for j in range(3):
             piece = cell(u, z_src[j], y, c, x)
             arrived(u, piece, j)
+            if j > 0:
+                relay(u, piece, j)
             push(u, piece, piece, 3 + j, dev_x)
             push(u, piece, piece, 7 + j, dev_y)
 
@@ -166,8 +188,15 @@
             arrived(u, cell(u, z_src[j], y, 1 - c), 19 + j)
             arrived(u, cell(u, z_src[j], 1 - y, 1 - c), 22 + j)
         pltpu.make_async_copy(own(u, stage), cell(u, z, y, c), local.at[u]).wait()
+        for j in (1, 2):
+
+            @pl.when(inner)
+            def _():
+                relay_copy(u, cell(u, z_src[j], y, c, x), j).wait_send()
+
     for cp in started:
         cp.wait_send()
+
 
 def gather_blocks(shards, collective_id):
     units = units_of(shards, 0.5)
@@ -182,7 +211,7 @@
         in_specs=[pl.BlockSpec(memory_space=pl.ANY)] * len(shards),
         out_specs=[pl.BlockSpec(memory_space=pl.ANY)] * len(shards),
         scratch_shapes=[
-            pltpu.SemaphoreType.DMA((n, 25)),
+            pltpu.SemaphoreType.DMA((n, 27)),
             pltpu.SemaphoreType.DMA((n, 25)),
             pltpu.SemaphoreType.DMA((n,)),
         ],
@@ -190,12 +219,579 @@
         name="gather_blocks",
     )(*shards)
 
-def scatter_kernel(units, n_arrays, *refs):
-    grads, outs = refs[:n_arrays], refs[n_arrays : 2 * n_arrays]
+
+TOKENS = 256
+HALF_LANES = 64
+FORWARD_VMEM = 58 * 2**20
+
+
+def lane_of(shape):
+    return lax.broadcasted_iota(jnp.int32, shape, len(shape) - 1)
+
+
+def norm_rows(hidden):
+    center = hidden - jnp.mean(hidden, -1, keepdims=True)
+    inverse = lax.rsqrt(jnp.mean(center * center, -1, keepdims=True) + EPS_NORM)
+    return center * inverse, inverse
+
+
+def gelu_and_slope(v):
+    root = 0.7978845608028654
+    square = v * v
+    wave = jnp.tanh(root * (v + 0.044715 * (square * v)))
+    near = 0.5 * (1.0 + wave)
+    slope = near + (0.5 * root) * v * (1.0 - wave * wave) * (1.0 + (3 * 0.044715) * square)
+    return v * near, slope
+
+
+def both_heads(pair, first):
+    zero = jnp.zeros_like(pair)
+    return jnp.concatenate([jnp.where(first, pair, zero), jnp.where(first, zero, pair)], 0)
+
+
+def step_forward_kernel(
+    sizes,
+    inputs,
+    labels,
+    seg_col,
+    seg_row,
+    same,
+    hbm_qkv,
+    hbm_o,
+    hbm_up,
+    hbm_down,
+    hbm_side,
+    gain_rows,
+    out_latent,
+    out_na,
+    out_aa,
+    out_qkv,
+    out_p,
+    out_ctx,
+    out_nm,
+    out_am,
+    out_slope,
+    out_gelu,
+    out_stat,
+    out_nf,
+    out_af,
+    out_tail,
+    out_start,
+    w_qkv,
+    w_o,
+    w_up,
+    w_down,
+    w_side,
+    na,
+    aa,
+    qkv,
+    prob,
+    ctx,
+    nm,
+    am,
+    slope,
+    gelu,
+    stat,
+    nf,
+    af,
+    tail,
+    start,
+    hidden,
+    w_sem,
+    out_sem,
+    last_sem,
+):
+    rows, length, classes, channels = sizes
+    layers, width = w_qkv.shape[0], w_qkv.shape[1]
+    loads = [(hbm_side, w_side, 0)]
+    for layer in range(layers):
+        for i, (src, dst) in enumerate(
+            ((hbm_qkv, w_qkv), (hbm_o, w_o), (hbm_up, w_up), (hbm_down, w_down))
+        ):
+            loads.append((src.at[layer], dst.at[layer], 1 + 4 * layer + i))
+    for src, dst, i in loads:
+        pltpu.make_async_copy(src, dst, w_sem.at[i]).start()
+
+    def ready(layer, i, dst):
+        pltpu.make_async_copy(dst.at[layer], dst.at[layer], w_sem.at[1 + 4 * layer + i]).wait()
+
+    def save(layer, i, src, dst):
+        pltpu.make_async_copy(src, dst.at[layer], out_sem.at[layer, i]).start()
+
+    table = classes
+    start[:, :table] = (labels[...] == lane_of((TOKENS, table))).astype(jnp.bfloat16)
+    start[:, table:] = inputs[...].astype(jnp.bfloat16)
+    pltpu.make_async_copy(w_side, w_side, w_sem.at[0]).wait()
+    hidden[...] = lax.dot_general(
+        start[...],
+        w_side[:, : table + LANES],
+        (((1,), (1,)), ((), ())),
+        preferred_element_type=jnp.float32,
+    )
+
+    def saves(layer):
+        return (
+            (na.at[layer], out_na),
+            (aa.at[layer], out_aa),
+            (qkv.at[layer], out_qkv),
+            (prob.at[layer], out_p),
+            (ctx.at[layer], out_ctx),
+            (nm.at[layer], out_nm),
+            (am.at[layer], out_am),
+            (slope, out_slope),
+            (gelu.at[layer], out_gelu),
+            (stat.at[layer], out_stat),
+        )
+
+    for layer in range(layers):
+        out = saves(layer)
+        normed, inverse_a = norm_rows(hidden[...])
+        na[layer] = normed
+        save(layer, 0, *out[0])
+        aa[layer] = (normed * gain_rows[2 * layer : 2 * layer + 1, :]).astype(jnp.bfloat16)
+        save(layer, 1, *out[1])
+        ready(layer, 0, w_qkv)
+
+        @pl.loop(0, 3)
+        def _(i):
+            cols = pl.ds(pl.multiple_of(i * width, LANES), width)
+            qkv[layer, :, cols] = jnp.dot(
+                aa[layer], w_qkv[layer, :, cols], preferred_element_type=jnp.float32
+            ).astype(jnp.bfloat16)
+
+        save(layer, 2, *out[2])
+        pairs = width // LANES
+        for row in range(rows):
+            toks = pl.ds(row * length, length)
+            causal = lax.broadcasted_iota(jnp.int32, (length, length), 0) >= lane_of(
+                (length, length)
+            )
+            attend = (seg_col[toks, :] == seg_row[row : row + 1, :]) & causal
+            attend = jnp.concatenate([attend.astype(jnp.float32)] * 2, 0) > 0.5
+            first = lane_of((length, LANES)) < HALF_LANES
+
+            def each_pair(pair):
+                def part(i):
+                    return qkv[
+                        layer, toks, pl.ds(i * width + pair * LANES, LANES)
+                    ]
+
+                query = both_heads(part(0), first)
+                scores = (
+                    lax.dot_general(
+                        query, part(1), (((1,), (1,)), ((), ())), preferred_element_type=jnp.float32
+                    )
+                    * HEAD_DIM ** (-0.5)
+                )
+                scores = jnp.where(attend, scores, MASKED)
+                expo = jnp.exp(scores - jnp.max(scores, -1, keepdims=True))
+                soft = expo / jnp.sum(expo, -1, keepdims=True)
+                prob[layer, row * pairs + pair] = soft
+                mixed = jnp.dot(
+                    soft.astype(jnp.bfloat16), part(2), preferred_element_type=jnp.float32
+                )
+                ctx[layer, toks, pl.ds(pair * LANES, LANES)] = jnp.where(
+                    first, mixed[:length], mixed[length:]
+                ).astype(jnp.bfloat16)
+
+            for pair in range(pairs):
+                each_pair(pair)
+
+        save(layer, 3, *out[3])
+        save(layer, 4, *out[4])
+        ready(layer, 1, w_o)
+        hidden[...] = hidden[...] + jnp.dot(
+            ctx[layer], w_o[layer], preferred_element_type=jnp.float32
+        )
+        normed, inverse_m = norm_rows(hidden[...])
+        nm[layer] = normed
+        save(layer, 5, *out[5])
+        am[layer] = (normed * gain_rows[2 * layer + 1 : 2 * layer + 2, :]).astype(jnp.bfloat16)
+        save(layer, 6, *out[6])
+        stat[layer] = jnp.where(lane_of((TOKENS, LANES)) == 0, inverse_a, inverse_m)
+        save(layer, 9, *out[9])
+        ready(layer, 2, w_up)
+        if layer > 0:
+            pltpu.make_async_copy(slope, slope, out_sem.at[layer - 1, 7]).wait()
+
+        @pl.loop(0, w_up.shape[2] // width)
+        def _(i):
+            cols = pl.ds(pl.multiple_of(i * width, LANES), width)
+            upper = jnp.dot(am[layer], w_up[layer, :, cols], preferred_element_type=jnp.float32)
+            value, rate = gelu_and_slope(upper)
+            gelu[layer, :, cols] = value.astype(jnp.bfloat16)
+            slope[:, cols] = rate
+
+        save(layer, 7, *out[7])
+        save(layer, 8, *out[8])
+        ready(layer, 3, w_down)
+        half = width // 2
+
+        @pl.loop(0, 2)
+        def _(i):
+            cols = pl.ds(pl.multiple_of(i * half, LANES), half)
+            hidden[:, cols] = hidden[:, cols] + jnp.dot(
+                gelu[layer], w_down[layer, :, cols], preferred_element_type=jnp.float32
+            )
+
+    normed, inverse_f = norm_rows(hidden[...])
+    nf[...] = normed
+    af[...] = (normed * gain_rows[2 * layers : 2 * layers + 1, :]).astype(jnp.bfloat16)
+    prediction = jnp.dot(
+        af[...], w_side[:, table + LANES :], preferred_element_type=jnp.float32
+    )
+    previous = pltpu.roll(prediction, 1, 0)
+    lane = lane_of((TOKENS, LANES))
+    shown = (same[...] > 0) & (lane < channels)
+    shift_alpha = jnp.where(shown, pltpu.roll(previous, LANES - channels, 1), 0.0)
+    shift_mu = jnp.where(shown, previous, 0.0)
+    latent = (inputs[...] - shift_mu) * jnp.exp(-shift_alpha)
+    logdet = -jnp.sum(shift_alpha, -1, keepdims=True)
+    out_latent[...] = jnp.where(lane == channels, logdet + inputs[...], latent)
+    tail[0] = latent
+    tail[1] = shift_alpha
+    tail[2] = jnp.broadcast_to(inverse_f, (TOKENS, LANES))
+    final = ((nf, out_nf), (af, out_af), (tail, out_tail), (start, out_start))
+    for i, (src, dst) in enumerate(final):
+        pltpu.make_async_copy(src, dst, last_sem.at[i]).start()
+    for layer in range(layers):
+        for i, (src, dst) in enumerate(saves(layer)):
+            if i != 7 or layer == layers - 1:
+                pltpu.make_async_copy(src, dst.at[layer], out_sem.at[layer, i]).wait()
+    for i, (src, dst) in enumerate(final):
+        pltpu.make_async_copy(src, dst, last_sem.at[i]).wait()
+
+
+def step_forward(inputs, labels, seg_ids, same, weights, gain_rows, table, channels):
+    w_qkv, w_o, w_up, w_down, side = weights
+    rows, length = seg_ids.shape
+    layers, width, hidden = w_up.shape
+    pairs = rows * width // LANES
+    low, full = jnp.bfloat16, jnp.float32
+    kept = [
+        ((layers, TOKENS, width), full),
+        ((layers, TOKENS, width), low),
+        ((layers, TOKENS, 3 * width), low),
+        ((layers, pairs, 2 * length, length), full),
+        ((layers, TOKENS, width), low),
+        ((layers, TOKENS, width), full),
+        ((layers, TOKENS, width), low),
+        ((layers, TOKENS, hidden), full),
+        ((layers, TOKENS, hidden), low),
+        ((layers, TOKENS, LANES), full),
+        ((TOKENS, width), full),
+        ((TOKENS, width), low),
+        ((3, TOKENS, LANES), full),
+        ((TOKENS, table + LANES), low),
+    ]
+    scratch = [pltpu.VMEM(w.shape, low) for w in weights]
+    for i, (shape, kind) in enumerate(kept):
+        scratch.append(pltpu.VMEM(shape[1:] if i == 7 else shape, kind))
+    scratch += [
+        pltpu.VMEM((TOKENS, width), full),
+        pltpu.SemaphoreType.DMA((1 + 4 * layers,)),
+        pltpu.SemaphoreType.DMA((layers, 10)),
+        pltpu.SemaphoreType.DMA((4,)),
+    ]
+    vmem, hbm = pl.BlockSpec(memory_space=pltpu.VMEM), pl.BlockSpec(memory_space=pl.ANY)
+    flops = 2 * TOKENS * (sum(w.size for w in weights))
+    return pl.pallas_call(
+        functools.partial(step_forward_kernel, (rows, length, table, channels)),
+        out_shape=[jax.ShapeDtypeStruct((TOKENS, LANES), full)]
+        + [jax.ShapeDtypeStruct(shape, kind) for shape, kind in kept],
+        in_specs=[vmem] * 5 + [hbm] * 5 + [vmem],
+        out_specs=[vmem] + [hbm] * len(kept),
+        scratch_shapes=scratch,
+        cost_estimate=pl.CostEstimate(flops=flops, bytes_accessed=50 * 2**20, transcendentals=0),
+        compiler_params=pltpu.CompilerParams(vmem_limit_bytes=FORWARD_VMEM),
+        name="step_forward",
+    )(
+        inputs,
+        labels,
+        seg_ids.reshape(TOKENS, 1),
+        seg_ids,
+        same,
+        w_qkv,
+        w_o,
+        w_up,
+        w_down,
+        side,
+        gain_rows,
+    )
+
+
+def norm_rows_back(normed, inverse, grad_normed):
+    mean_grad = jnp.mean(grad_normed, -1, keepdims=True)
+    mean_proj = jnp.mean(grad_normed * normed, -1, keepdims=True)
+    return inverse * (grad_normed - mean_grad - normed * mean_proj)
+
+
+def by_rows(left, right):
+    return lax.dot_general(
+        left, right, (((1,), (1,)), ((), ())), preferred_element_type=jnp.float32
+    )
+
+
+def down_columns(left, right):
+    return lax.dot_general(
+        left, right, (((0,), (0,)), ((), ())), preferred_element_type=jnp.float32
+    )
+
+
+def step_backward_kernel(
+    sizes,
+    grad_latent,
+    same,
+    hbm_qkv,
+    hbm_o,
+    hbm_up,
+    hbm_down,
+    hbm_side,
+    gain_rows,
+    in_na,
+    in_qkv,
+    in_p,
+    in_nm,
+    in_slope,
+    in_stat,
+    in_nf,
+    in_tail,
+    out_grad,
+    out_gains,
+    out_gqkv,
+    out_gmid,
+    out_gup,
+    out_gbr,
+    out_gstart,
+    out_gpred,
+    w_qkv,
+    w_o,
+    w_up,
+    w_down,
+    w_side,
+    na,
+    qkv,
+    prob,
+    nm,
+    slope,
+    stat,
+    nf,
+    tail,
+    gqkv,
+    gmid,
+    gup,
+    gbr,
+    gstart,
+    gpred,
+    ghid,
+    gact,
+    gctx,
+    w_sem,
+    in_sem,
+    out_sem,
+    last_sem,
+):
+    rows, length, table, channels = sizes
+    layers, width = w_qkv.shape[0], w_qkv.shape[1]
+    pairs = width // LANES
+    order = list(reversed(range(layers)))
+    weights = ((hbm_down, w_down), (hbm_up, w_up), (hbm_o, w_o), (hbm_qkv, w_qkv))
+    layered = ((in_slope, slope), (in_nm, nm), (in_p, prob), (in_qkv, qkv), (in_na, na))
+
+    def load(src, dst, sem):
+        return pltpu.make_async_copy(src, dst, sem)
+
+    def layer_load(layer, i):
+        src, dst = layered[i]
+        return load(src.at[layer], dst if i == 0 else dst.at[layer], in_sem.at[layer, i])
+
+    def weight_load(layer, i):
+        src, dst = weights[i]
+        return load(src.at[layer], dst.at[layer], w_sem.at[1 + 4 * layer + i])
+
+    single = ((in_tail, tail), (in_nf, nf), (in_stat, stat))
+    for i, (src, dst) in enumerate(single):
+        load(src, dst, last_sem.at[i]).start()
+    load(hbm_side, w_side, w_sem.at[0]).start()
+    for layer in order:
+        for i in range(4):
+            weight_load(layer, i).start()
+            if i > 0 or layer == order[0]:
+                layer_load(layer, i).start()
+        layer_load(layer, 4).start()
+
+    def save(layer, i, src, dst):
+        pltpu.make_async_copy(src, dst.at[layer], out_sem.at[layer, i]).start()
+
+    lane = lane_of((TOKENS, LANES))
+    load(in_tail, tail, last_sem.at[0]).wait()
+    out_gains[...] = jnp.zeros_like(out_gains)
+    scaled = grad_latent[...] * jnp.exp(-tail[1])
+    grad_alpha = 1.0 - grad_latent[...] * tail[0]
+    grad_prev = jnp.where(lane < channels, -scaled, pltpu.roll(grad_alpha, channels, 1))
+    grad_prev = jnp.where((same[...] > 0) & (lane < 2 * channels), grad_prev, 0.0)
+    gpred[...] = pltpu.roll(grad_prev, TOKENS - 1, 0).astype(jnp.bfloat16)
+    out_gpred[...] = gpred[...]
+    load(hbm_side, w_side, w_sem.at[0]).wait()
+    gact[...] = by_rows(gpred[...], w_side[:, table + LANES :])
+    load(in_nf, nf, last_sem.at[1]).wait()
+    load(in_stat, stat, last_sem.at[2]).wait()
+
+    def through_norm(normed, inverse, index):
+        grad = gact[...]
+        out_gains[index : index + 1, :] = jnp.sum(grad * normed, 0, keepdims=True)
+        return norm_rows_back(normed, inverse, grad * gain_rows[index : index + 1, :])
+
+    ghid[...] = through_norm(nf[...], tail[2][:, :1], 2 * layers)
+    for layer in order:
+        gbr[layer] = ghid[...].astype(jnp.bfloat16)
+        save(layer, 3, gbr.at[layer], out_gbr)
+        weight_load(layer, 0).wait()
+        layer_load(layer, 0).wait()
+        if layer != order[0]:
+            pltpu.make_async_copy(gup, out_gup.at[layer + 1], out_sem.at[layer + 1, 2]).wait()
+
+        @pl.loop(0, w_up.shape[2] // width)
+        def _(i):
+            cols = pl.ds(pl.multiple_of(i * width, LANES), width)
+            gup[:, cols] = (by_rows(gbr[layer], w_down[layer, cols, :]) * slope[:, cols]).astype(
+                jnp.bfloat16
+            )
+
+        save(layer, 2, gup, out_gup)
+        if layer > 0:
+            layer_load(layer - 1, 0).start()
+        weight_load(layer, 1).wait()
+
+        half = width // 2
+
+        @pl.loop(0, 2)
+        def _(i):
+            cols = pl.ds(pl.multiple_of(i * half, LANES), half)
+            gact[:, cols] = by_rows(gup[...], w_up[layer, cols, :])
+
+        layer_load(layer, 1).wait()
+        ghid[...] = ghid[...] + through_norm(nm[layer], stat[layer][:, 1:2], 2 * layer + 1)
+        gmid[layer] = ghid[...].astype(jnp.bfloat16)
+        save(layer, 1, gmid.at[layer], out_gmid)
+        weight_load(layer, 2).wait()
+        gctx[...] = by_rows(gmid[layer], w_o[layer]).astype(jnp.bfloat16)
+        layer_load(layer, 2).wait()
+        layer_load(layer, 3).wait()
+        for row in range(rows):
+            toks = pl.ds(row * length, length)
+            first = lane_of((length, LANES)) < HALF_LANES
+
+            def each_pair(pair):
+                def at(i):
+                    return pl.ds(i * width + pair * LANES, LANES)
+
+                query = both_heads(qkv[layer, toks, at(0)], first)
+                key = qkv[layer, toks, at(1)]
+                value = qkv[layer, toks, at(2)]
+                grad = both_heads(gctx[toks, at(0)], first)
+                soft = prob[layer, row * pairs + pair]
+                grad_soft = by_rows(grad, value)
+                delta = jnp.sum(soft * grad_soft, -1, keepdims=True)
+                grad_scores = (soft * (grad_soft - delta)).astype(jnp.bfloat16)
+                factor = HEAD_DIM ** (-0.5)
+                mixed = jnp.dot(grad_scores, key, preferred_element_type=jnp.float32) * factor
+                gqkv[layer, toks, at(0)] = jnp.where(
+                    first, mixed[:length], mixed[length:]
+                ).astype(jnp.bfloat16)
+                gqkv[layer, toks, at(1)] = (down_columns(grad_scores, query) * factor).astype(
+                    jnp.bfloat16
+                )
+                gqkv[layer, toks, at(2)] = down_columns(soft.astype(jnp.bfloat16), grad).astype(
+                    jnp.bfloat16
+                )
+
+            for pair in range(pairs):
+                each_pair(pair)
+
+        save(layer, 0, gqkv.at[layer], out_gqkv)
+        weight_load(layer, 3).wait()
+
+        @pl.loop(0, 2)
+        def _(i):
+            cols = pl.ds(pl.multiple_of(i * half, LANES), half)
+            gact[:, cols] = by_rows(gqkv[layer], w_qkv[layer, cols, :])
+
+        layer_load(layer, 4).wait()
+        ghid[...] = ghid[...] + through_norm(na[layer], stat[layer][:, :1], 2 * layer)
+    gstart[...] = ghid[...].astype(jnp.bfloat16)
+    pltpu.make_async_copy(gstart, out_gstart, last_sem.at[3]).start()
+    grad_inputs = scaled + jnp.dot(
+        gstart[...], w_side[:, table : table + LANES], preferred_element_type=jnp.float32
+    )
+    out_grad[...] = jnp.where(lane < channels, grad_inputs, 0.0)
+    pltpu.make_async_copy(gstart, out_gstart, last_sem.at[3]).wait()
+    for layer in range(layers):
+        done = ((gqkv.at[layer], out_gqkv), (gmid.at[layer], out_gmid), (gup, out_gup))
+        done = done + ((gbr.at[layer], out_gbr),)
+        for i, (src, dst) in enumerate(done):
+            if i != 2 or layer == 0:
+                pltpu.make_async_copy(src, dst.at[layer], out_sem.at[layer, i]).wait()
+
+
+def step_backward(grad_latent, same, weights, gain_rows, kept, rows, length, table, channels):
+    w_qkv, w_o, w_up, w_down, side = weights
+    layers, width, hidden = w_up.shape
+    na, aa, qkv, prob, ctx, nm, am, slope, gelu, stat, nf, af, tail, start = kept
+    used = [na, qkv, prob, nm, slope, stat, nf, tail]
+    low, full = jnp.bfloat16, jnp.float32
+    made = [
+        (layers, TOKENS, 3 * width),
+        (layers, TOKENS, width),
+        (layers, TOKENS, hidden),
+        (layers, TOKENS, width),
+        (TOKENS, width),
+        (TOKENS, LANES),
+    ]
+    scratch = [pltpu.VMEM(w.shape, low) for w in weights]
+    scratch += [
+        pltpu.VMEM(part.shape[1:] if i == 4 else part.shape, part.dtype)
+        for i, part in enumerate(used)
+    ]
+    scratch += [pltpu.VMEM(s[1:] if i == 2 else s, low) for i, s in enumerate(made)]
+    scratch += [
+        pltpu.VMEM((TOKENS, width), full),
+        pltpu.VMEM((TOKENS, width), full),
+        pltpu.VMEM((TOKENS, width), low),
+        pltpu.SemaphoreType.DMA((1 + 4 * layers,)),
+        pltpu.SemaphoreType.DMA((layers, 5)),
+        pltpu.SemaphoreType.DMA((layers, 4)),
+        pltpu.SemaphoreType.DMA((4,)),
+    ]
+    vmem, hbm = pl.BlockSpec(memory_space=pltpu.VMEM), pl.BlockSpec(memory_space=pl.ANY)
+    flops = 2 * TOKENS * (sum(w.size for w in weights))
+    return pl.pallas_call(
+        functools.partial(step_backward_kernel, (rows, length, table, channels)),
+        out_shape=[
+            jax.ShapeDtypeStruct((TOKENS, LANES), full),
+            jax.ShapeDtypeStruct((8, width), full),
+        ]
+        + [jax.ShapeDtypeStruct(shape, low) for shape in made],
+        in_specs=[vmem] * 2 + [hbm] * 5 + [vmem] + [hbm] * len(used),
+        out_specs=[vmem] * 2 + [hbm] * 5 + [vmem],
+        scratch_shapes=scratch,
+        cost_estimate=pl.CostEstimate(flops=flops, bytes_accessed=50 * 2**20, transcendentals=0),
+        compiler_params=pltpu.CompilerParams(vmem_limit_bytes=FORWARD_VMEM),
+        name="step_backward",
+    )(grad_latent, same, w_qkv, w_o, w_up, w_down, side, gain_rows, *used)
+
+
+def products_kernel(units, n_pairs, *refs):
+    per = 2 * n_pairs
+    first, middle, final = refs[:per], refs[per : 2 * per], refs[2 * per : 3 * per]
+    gain_cols = refs[3 * per]
+    outs = refs[3 * per + 1 : 3 * per + 6]
+    rest = refs[3 * per + 6 :]
+    bufs, made, turned = rest[:per], rest[per : per + 5], rest[per + 5]
+    rest = rest[per + 6 :]
     n = len(units)
-    rest = refs[2 * n_arrays :]
-    acc, sib, in_x, in_y, in_d, in_z, fin = [rest[i * n : (i + 1) * n] for i in range(7)]
-    send, recv, local, local_out = rest[7 * n :]
+    acc, in_x, in_y, in_d, in_z = [rest[i * n : (i + 1) * n] for i in range(5)]
+    in_sem, send, recv, local_out = rest[5 * n :]
     r, x, y, z, c = place()
     stage = z // 2
     other = 1 - stage
@@ -203,21 +799,43 @@
     dev_x = (r, 1 - x)
     dev_y = (r + 2 - 4 * y, x)
     dev_s = (r + 1 - 2 * c, x)
-    z_near = z + 1 - 2 * zi
-    z_dst = (z_near, other * 2, other * 2 + 1)
+    z_dst = (z + 1 - 2 * zi, other * 2, other * 2 + 1)
     dev_z = tuple((zz * 4 + y * 2 + c, x) for zz in z_dst)
     barrier = pltpu.get_barrier_semaphore()
     partners = (dev_x, dev_y, dev_s) + dev_z
     for dev in partners:
         pl.semaphore_signal(barrier, 1, device_id=dev, device_id_type=MESH_ID)
+
+    def loads(i, layer):
+        def view(ref):
+            return ref.at[layer] if len(ref.shape) == 3 else ref
+
+        lower, upper = bufs[i].at[pl.ds(0, TOKENS)], bufs[i].at[pl.ds(TOKENS, TOKENS)]
+        return view(first[i]), view(middle[i]), view(final[i]), lower, upper
+
+    def fetch(i, layer):
+        a, b, c, lower, upper = loads(i, layer)
+        pltpu.make_async_copy(b, lower, in_sem.at[layer, 2 * i]).start()
+
+        @pl.when(stage == 1)
+        def _():
+            pltpu.make_async_copy(c, upper, in_sem.at[layer, 2 * i + 1]).start()
+
+        @pl.when(stage == 0)
+        def _():
+            pltpu.make_async_copy(a, upper, in_sem.at[layer, 2 * i + 1]).start()
+
+    def fetched(i, layer):
+        a, b, c, lower, upper = loads(i, layer)
+        pltpu.make_async_copy(b, lower, in_sem.at[layer, 2 * i]).wait()
+        pltpu.make_async_copy(a, upper, in_sem.at[layer, 2 * i + 1]).wait()
+
+    for i in (8, 9, 10, 11):
+        fetch(i, 0)
+    for i in range(8):
+        fetch(i, 0)
     pl.semaphore_wait(barrier, len(partners))
-    started = []
-
-    def part_of(u, part):
-        _, _, _, rows, half, (dim, first) = units[u]
-        if dim == 0:
-            return (pl.ds(0, first), pl.ds(0, half)) if part == 0 else (pl.ds(first, rows - first), pl.ds(0, half))
-        return (pl.ds(0, rows), pl.ds(0, first)) if part == 0 else (pl.ds(0, rows), pl.ds(first, half - first))
+    started = {}
 
     def push(u, src, dst, slot, dev, idx=None):
         cp = pltpu.make_async_remote_copy(
@@ -229,131 +847,174 @@
             device_id_type=MESH_ID,
         )
         cp.start()
-        started.append(cp)
+        started[u, slot] = cp
 
     def arrived(u, dst, idx):
         wait_all_of(dst, recv.at[u, idx])
 
-    def pieces(u, cc):
-        a, l, _, rows, half, _ = units[u]
-        for s in range(8):
-            for h in range(2):
-                row0 = pl.multiple_of((s * 2 + cc) * rows, 16)
-                yield s, h, grads[a].at[l, pl.ds(row0, rows), pl.ds(h * half, half)]
-
-    def begin(u):
-        for s, h, src in pieces(u, 1 - c):
-            push(u, src, sib[u].at[s, h], 18 + 2 * s + h, dev_s)
-        for s, h, src in pieces(u, c):
-            pltpu.make_async_copy(src, acc[u].at[s, h], local.at[u]).start()
+    def part_of(u, part):
+        _, _, _, rows, half, (dim, cut) = units[u]
+        if dim == 0:
+            return (pl.ds(0, cut), pl.ds(0, half)) if part == 0 else (pl.ds(cut, rows - cut), pl.ds(0, half))
+        return (pl.ds(0, rows), pl.ds(0, cut)) if part == 0 else (pl.ds(0, rows), pl.ds(cut, half - cut))
+
+    block, strip = turned.shape[0], 3 * LANES
+
+    def multiply(out, rows, right, m, begin, count, wide, extra=None):
+        def one(cols, out_cols):
+            product = jnp.dot(turned[...], right[:, cols], preferred_element_type=jnp.float32)
+            if extra is not None:
+                product = product + extra[...]
+            product = product.astype(jnp.bfloat16)
+            for k in range(block // rows):
+                s = m * (block // rows) + k
+                out[s // 4, (s // 2) % 2, s % 2, :, out_cols] = product[k * rows : (k + 1) * rows]
+
+        if count == 1:
+            one(slice(0, wide), slice(begin, begin + wide))
+        else:
+
+            @pl.loop(0, count)
+            def _(i):
+                cols = pl.ds(pl.multiple_of(i * wide, LANES), wide)
+                one(cols, cols)
+
+    def product(u):
+        a, layer, _, rows, half, _ = units[u]
+        if a == 4:
+            for i in (8, 9, 10, 11):
+                fetched(i, 0)
+            turned[...] = bufs[9][...].T
+            multiply(made[4], rows, bufs[8], 0, 0, bufs[8].shape[1] // strip, strip)
+            turned[...] = bufs[10][...].T
+            multiply(made[4], rows, bufs[11], 0, bufs[8].shape[1], 1, LANES, gain_cols)
+        else:
+            fetched(2 * a, layer)
+            fetched(2 * a + 1, layer)
+            if layer > 0:
+                for h in range(2):
+                    started.pop((u - 4, h)).wait_send()
+            for m in range(bufs[2 * a].shape[1] // block):
+                turned[...] = bufs[2 * a][:, m * block : (m + 1) * block].T
+                multiply(made[a], rows, bufs[2 * a + 1], m, 0, 2 * half // strip, strip)
+            if layer + 1 < units[-1][1] + 1:
+                fetch(2 * a, layer + 1)
+                fetch(2 * a + 1, layer + 1)
+        for h in range(2):
+            cols = pl.ds(h * half, half)
+            push(u, made[a].at[:, :, 1 - c, :, cols], acc[u].at[:, :, h], h, dev_s)
 
     def chip_sum(u):
-        wait_all_of(acc[u], local.at[u])
-        for s in range(8):
-            for h in range(2):
-                arrived(u, sib[u].at[s, h], 18 + 2 * s + h)
-
-        @pl.loop(0, 8)
-        def _(s):
-            for h in range(2):
-                acc[u][s, h] = acc[u][s, h] + sib[u][s, h]
-
-        for zz in range(4):
-            slab = zz * 2 + 1 - y
-            rs, cs = part_of(u, 0)
-            push(u, acc[u].at[slab, 1 - x, rs, cs], in_d[u].at[zz, rs, cs], zz, dev_y)
-            rs, cs = part_of(u, 1)
-            push(u, acc[u].at[slab, 1 - x, rs, cs], in_d[u].at[zz, rs, cs], 4 + zz, dev_x)
+        a, layer, _, rows, half, _ = units[u]
+        for h in range(2):
+            arrived(u, acc[u].at[:, :, h], h)
+
+        @pl.loop(0, 4)
+        def _(zz):
+            for yy in range(2):
+                for h in range(2):
+                    mine = made[a][zz, yy, c, :, h * half : (h + 1) * half]
+                    acc[u][zz, yy, h] = acc[u][zz, yy, h] + mine
+
+        for part, dev in ((0, dev_y), (1, dev_x)):
+            rs, cs = part_of(u, part)
+            push(u, acc[u].at[:, 1 - y, 1 - x, rs, cs], in_d[u].at[:, rs, cs], 2 + part, dev)
 
     def side_sum(u):
-        for zz in range(4):
-            rs, cs = part_of(u, 0)
-            arrived(u, in_d[u].at[zz, rs, cs], zz)
-            acc[u][zz * 2 + y, 1 - x, rs, cs] = acc[u][zz * 2 + y, 1 - x, rs, cs] + in_d[u][zz, rs, cs]
-            push(u, acc[u].at[zz * 2 + y, 1 - x], in_x[u].at[zz], 8 + zz, dev_x)
-            rs, cs = part_of(u, 1)
-            arrived(u, in_d[u].at[zz, rs, cs], 4 + zz)
-            acc[u][zz * 2 + 1 - y, x, rs, cs] = acc[u][zz * 2 + 1 - y, x, rs, cs] + in_d[u][zz, rs, cs]
-            push(u, acc[u].at[zz * 2 + 1 - y, x], in_y[u].at[zz], 12 + zz, dev_y)
+        for part, yy, h, dev, into in ((0, y, 1 - x, dev_x, in_x), (1, 1 - y, x, dev_y, in_y)):
+            rs, cs = part_of(u, part)
+            arrived(u, in_d[u].at[:, rs, cs], 2 + part)
+
+            @pl.loop(0, 4)
+            def _(zz):
+                acc[u][zz, yy, h, rs, cs] = acc[u][zz, yy, h, rs, cs] + in_d[u][zz, rs, cs]
+
+            push(u, acc[u].at[:, yy, h], into[u], 4 + part, dev)
 
     def plane_sum(u):
-        for zz in range(4):
-            arrived(u, in_x[u].at[zz], 8 + zz)
-            arrived(u, in_y[u].at[zz], 12 + zz)
-            acc[u][zz * 2 + y, x] = (
-                acc[u][zz * 2 + y, x].astype(jnp.float32)
+        arrived(u, in_x[u], 4)
+        arrived(u, in_y[u], 5)
+
+        @pl.loop(0, 4)
+        def _(zz):
+            acc[u][zz, y, x] = (
+                acc[u][zz, y, x].astype(jnp.float32)
                 + in_x[u][zz].astype(jnp.float32)
                 + in_y[u][zz].astype(jnp.float32)
             ).astype(jnp.bfloat16)
+
         for i in range(2):
-            push(u, acc[u].at[z_dst[1 + i] * 2 + y, x], in_z[u].at[1 + zi], 35 + i, dev_z[1 + i], idx=35 + zi)
-        push(u, acc[u].at[z_near * 2 + y, x], in_z[u].at[0], 34, dev_z[0])
+            push(u, acc[u].at[z_dst[1 + i], y, x], in_z[u].at[1 + zi], 7 + i, dev_z[1 + i], idx=7 + zi)
+        push(u, acc[u].at[z_dst[0], y, x], in_z[u].at[0], 6, dev_z[0])
+
+    def owned(u, b, h):
+        a, layer, layers, _, half, _ = units[u]
+        return outs[a].at[layers * b + layer, :, pl.ds(pl.multiple_of(h * half, LANES), half)]
+
+    def totals(u):
+        return ((acc[u].at[z, y, x], stage), (in_z[u].at[1], other))
 
     def total(u):
-        a, l, layers, rows, half, _ = units[u]
         for j in range(3):
-            arrived(u, in_z[u].at[j], 34 + j)
-        fin[u][0] = acc[u][z * 2 + y, x] + in_z[u][0]
-        fin[u][1] = in_z[u][1] + in_z[u][2]
-        for k, b in ((0, stage), (1, other)):
-            dst = outs[a].at[layers * b + l, :, pl.ds(pl.multiple_of(x * half, LANES), half)]
-            push(u, fin[u].at[k], dst, 16 + k, dev_x)
-            pltpu.make_async_copy(fin[u].at[k], dst, local_out.at[u, k]).start()
-
+            arrived(u, in_z[u].at[j], 6 + j)
+        acc[u][z, y, x] = acc[u][z, y, x] + in_z[u][0]
+        in_z[u][1] = in_z[u][1] + in_z[u][2]
+        for k, (src, b) in enumerate(totals(u)):
+            push(u, src, owned(u, b, x), 9 + k, dev_x)
+            pltpu.make_async_copy(src, owned(u, b, x), local_out.at[u, k]).start()
+
+    lags = (0, 1, 3, 5, 7)
+    for t in range(n + lags[-1]):
+        for lag, part in zip(lags, (product, chip_sum, side_sum, plane_sum, total)):
+            if 0 <= t - lag < n:
+                part(t - lag)
     for u in range(n):
-        begin(u)
-    for t in range(n + 3):
-        if t < n:
-            chip_sum(t)
-        if 0 <= t - 1 < n:
-            side_sum(t - 1)
-        if 0 <= t - 2 < n:
-            plane_sum(t - 2)
-        if 0 <= t - 3 < n:
-            total(t - 3)
-    for u in range(n):
-        a, l, layers, rows, half, _ = units[u]
-        for k, b in ((0, stage), (1, other)):
-            there = outs[a].at[layers * b + l, :, pl.ds(pl.multiple_of((1 - x) * half, LANES), half)]
-            arrived(u, there, 16 + k)
-            dst = outs[a].at[layers * b + l, :, pl.ds(pl.multiple_of(x * half, LANES), half)]
-            pltpu.make_async_copy(fin[u].at[k], dst, local_out.at[u, k]).wait()
-    for cp in started:
+        for k, (src, b) in enumerate(totals(u)):
+            arrived(u, owned(u, b, 1 - x), 9 + k)
+            pltpu.make_async_copy(src, owned(u, b, x), local_out.at[u, k]).wait()
+    for cp in started.values():
         cp.wait_send()
 
-def scatter_blocks(grads, collective_id):
-    out = [
-        jax.ShapeDtypeStruct((g.shape[0] * 2, g.shape[1] // 16, g.shape[2]), g.dtype) for g in grads
-    ]
+
+def summed_products(operands, gain_cols, shards, collective_id):
+    low = jnp.bfloat16
+    out = [jax.ShapeDtypeStruct(s.shape, low) for s in shards]
     units = units_of(out, 0.75)
     n = len(units)
-
-    def bufs(lead):
-        return [pltpu.VMEM(lead + (u[3], u[4]), jnp.bfloat16) for u in units]
+    layers = max(u[1] for u in units) + 1
+    n_pairs = len(operands[0]) // 2
+    width = operands[0][0].shape[-1]
+    hbm, vmem = pl.BlockSpec(memory_space=pl.ANY), pl.BlockSpec(memory_space=pltpu.VMEM)
+
+    def slots(lead):
+        return [pltpu.VMEM(lead + (u[3], u[4]), low) for u in units]
 
     return pl.pallas_call(
-        functools.partial(scatter_kernel, units, len(grads)),
+        functools.partial(products_kernel, units, n_pairs),
         out_shape=out,
-        in_specs=[pl.BlockSpec(memory_space=pl.ANY)] * len(grads),
-        out_specs=[pl.BlockSpec(memory_space=pl.ANY)] * len(grads),
-        scratch_shapes=bufs((8, 2))
-        + bufs((8, 2))
-        + bufs((4,))
-        + bufs((4,))
-        + bufs((4,))
-        + bufs((3,))
-        + bufs((2,))
+        in_specs=[hbm] * (6 * n_pairs) + [vmem],
+        out_specs=[hbm] * 5,
+        scratch_shapes=[
+            pltpu.VMEM((2 * TOKENS, part.shape[-1]), low) for part in operands[0]
+        ]
+        + [pltpu.VMEM((4, 2, 2) + s.shape[1:], low) for s in shards]
+        + [pltpu.VMEM((width, 2 * TOKENS), low)]
+        + slots((4, 2, 2))
+        + slots((4,))
+        + slots((4,))
+        + slots((4,))
+        + slots((3,))
         + [
-            pltpu.SemaphoreType.DMA((n, 37)),
-            pltpu.SemaphoreType.DMA((n, 37)),
-            pltpu.SemaphoreType.DMA((n,)),
+            pltpu.SemaphoreType.DMA((layers, 4 * n_pairs)),
+            pltpu.SemaphoreType.DMA((n, 11)),
+            pltpu.SemaphoreType.DMA((n, 11)),
             pltpu.SemaphoreType.DMA((n, 2)),
         ],
         compiler_params=pltpu.CompilerParams(
-            collective_id=collective_id, has_side_effects=True, vmem_limit_bytes=60 * 2**20
+            collective_id=collective_id, has_side_effects=True, vmem_limit_bytes=62 * 2**20
         ),
-        name="scatter_blocks",
-    )(*grads)
+        name="summed_products",
+    )(*[part for step in operands for part in step], gain_cols)
 
 
 def dot(left, right, dims=((1,), (0,))):
@@ -372,19 +1033,20 @@
     return inverse * (grad_normed - mean_grad - normed * mean_proj)
 
 
-def padded(count, unit=256):
+def padded(count, unit):
     return -(-count // unit) * unit
 
 
 def side_columns(classes, channels, out, gains):
-    table = padded(classes, 128)
-    ends = [table, table + channels, table + channels + out, table + channels + out + gains]
-    return ends, padded(ends[-1])
+    table = padded(classes, LANES)
+    last = table + padded(channels, LANES)
+    return table, last, padded(last + out + gains, 2 * LANES)
 
 
 def pack_side(w_table, w_in, w_out, gains):
     blocks, classes, shard = w_table.shape
-    ends, total = side_columns(classes, w_in.shape[1], w_out.shape[2], gains.shape[1])
+    channels, out, gain_count = w_in.shape[1], w_out.shape[2], gains.shape[1]
+    table, last, total = side_columns(classes, channels, out, gain_count)
 
     def gap(count):
         return jnp.zeros((blocks, shard, count), w_table.dtype)
@@ -392,23 +1054,24 @@
     return jnp.concatenate(
         [
             jnp.swapaxes(w_table, 1, 2),
-            gap(ends[0] - classes),
+            gap(table - classes),
             jnp.swapaxes(w_in, 1, 2),
+            gap(last - table - channels),
             w_out,
             jnp.swapaxes(gains, 1, 2),
-            gap(total - ends[3]),
+            gap(total - last - out - gain_count),
         ],
         2,
     )
 
 
 def split_side(side, classes, channels, out, gains):
-    ends, _ = side_columns(classes, channels, out, gains)
+    table, last, _ = side_columns(classes, channels, out, gains)
     return (
         jnp.swapaxes(side[..., :classes], -1, -2),
-        jnp.swapaxes(side[..., ends[0] : ends[1]], -1, -2),
-        side[..., ends[1] : ends[2]],
-        jnp.swapaxes(side[..., ends[2] : ends[3]], -1, -2),
+        jnp.swapaxes(side[..., table : table + channels], -1, -2),
+        side[..., last : last + out],
+        jnp.swapaxes(side[..., last + out : last + out + gains], -1, -2),
     )
 
 
@@ -426,7 +1089,7 @@
 def forward_block(inputs, seg_ids, labels, weights, sizes):
     w_qkv, w_o, w_up, w_down, side = weights
     classes, channels, out, gain_count = sizes
-    ends, side_total = side_columns(*sizes)
+    table, last, _ = side_columns(*sizes)
     rows, length, _ = inputs.shape
     tokens = rows * length
     width = side.shape[0]
@@ -437,17 +1100,17 @@
     same_seg = jnp.concatenate(
         [jnp.zeros((rows, 1), bool), seg_ids[:, 1:] == seg_ids[:, :-1]], 1
     )[..., None]
-    onehot = labels.reshape(tokens, 1) == jnp.arange(ends[0])[None, :]
+    onehot = labels.reshape(tokens, 1) == jnp.arange(table)[None, :]
     start = jnp.concatenate(
         [
             onehot.astype(jnp.bfloat16),
             inputs.reshape(tokens, channels).astype(jnp.bfloat16),
-            jnp.zeros((tokens, side_total - ends[1]), jnp.bfloat16),
+            jnp.zeros((tokens, last - table - channels), jnp.bfloat16),
         ],
         1,
     )
-    gain_rows = side[:, ends[2] : ends[3]].astype(jnp.float32).T
-    hidden = dot(start, side, ((1,), (1,)))
+    gain_rows = side[:, last + out : last + out + gain_count].astype(jnp.float32).T
+    hidden = dot(start, side[:, :last], ((1,), (1,)))
     kept = []
     for layer in range(w_qkv.shape[0]):
         normed_a, inverse_a = normalize(hidden)
@@ -489,7 +1152,7 @@
         )
     normed_f, inverse_f = normalize(hidden)
     act_f = (normed_f * gain_rows[gain_count - 1]).astype(jnp.bfloat16)
-    prediction = dot(act_f, side[:, ends[1] : ends[2]]).reshape(rows, length, out)
+    prediction = dot(act_f, side[:, last : last + out]).reshape(rows, length, out)
     previous = jnp.concatenate([jnp.zeros((rows, 1, out), jnp.float32), prediction[:, :-1]], 1)
     shift = jnp.where(same_seg, previous, 0.0)
     shift_alpha = shift[..., channels:]
@@ -501,13 +1164,13 @@
 def backward_block(grad_latent, saved, weights, sizes):
     w_qkv, w_o, w_up, w_down, side = weights
     classes, channels, out, gain_count = sizes
-    ends, _ = side_columns(*sizes)
+    table, last, _ = side_columns(*sizes)
     attend, same_seg, start, kept, normed_f, inverse_f, act_f, shift_alpha, latent = saved
     rows, length, _ = latent.shape
     tokens = rows * length
     width = side.shape[0]
     factor = HEAD_DIM ** (-0.5)
-    gain_rows = side[:, ends[2] : ends[3]].astype(jnp.float32).T
+    gain_rows = side[:, last + out : last + out + gain_count].astype(jnp.float32).T
     scale_back = jnp.exp(-shift_alpha)
     grad_inputs = grad_latent * scale_back
     grad_prev = jnp.where(
@@ -515,7 +1178,7 @@
     )
     grad_pred = jnp.concatenate([grad_prev[:, 1:], jnp.zeros((rows, 1, out), jnp.float32)], 1)
     grad_pred = grad_pred.reshape(tokens, out).astype(jnp.bfloat16)
-    grad_act = dot(grad_pred, side[:, ends[1] : ends[2]], ((1,), (1,)))
+    grad_act = dot(grad_pred, side[:, last : last + out], ((1,), (1,)))
     gain_grads = [None] * gain_count
     gain_grads[-1] = jnp.sum(grad_act * normed_f, 0)
     grad_hidden = normalize_back(normed_f, inverse_f, grad_act * gain_rows[gain_count - 1])
@@ -581,12 +1244,12 @@
             (gelu_low, grad_branch),
         )
     grad_start = grad_hidden.astype(jnp.bfloat16)
-    grad_inputs = grad_inputs + dot(grad_start, side[:, ends[0] : ends[1]]).reshape(
+    grad_inputs = grad_inputs + dot(grad_start, side[:, table : table + channels]).reshape(
         rows, length, channels
     )
     return grad_inputs, (
         pairs,
-        (start[:, : ends[1]], grad_start),
+        (start, grad_start),
         (act_f, grad_pred),
         jnp.stack(gain_grads, 1),
     )
@@ -634,58 +1297,78 @@
     swap = [(i, (i + half) % (2 * half)) for i in range(2 * half)]
     up = [(i, i + half) for i in range(half)]
     down = [(i + half, i) for i in range(half)]
+    classes, channels, out, gain_count = sizes
+    table, last, _ = side_columns(*sizes)
+    rows, length, _ = mine[0].shape
+
+    def wide(part):
+        return jnp.pad(part, ((0, 0), (0, 0), (0, LANES - part.shape[2])))
+
+    def back(part):
+        return part.reshape(rows, length, LANES)[:, ::-1].reshape(TOKENS, LANES)
+
+    mine = (wide(mine[0]), wide(mine[1])) + mine[2:]
     theirs = [lax.ppermute(part, "rows", swap) for part in mine]
     batch = [
         [jnp.where(second, b, a) for a, b in zip(mine, theirs)],
         [jnp.where(second, a, b) for a, b in zip(mine, theirs)],
     ]
+    for part in batch:
+        part[0] = part[0].reshape(TOKENS, LANES)
+        part[1] = part[1].reshape(TOKENS, LANES)
+    facts = []
+    for index in range(3):
+        ahead, behind = batch[min(index, 1)], batch[max(index - 1, 0)]
+        seg_ids, labels = [jnp.where(second, behind[i][:, ::-1], ahead[i]) for i in (2, 3)]
+        same = seg_ids[:, 1:] == seg_ids[:, :-1]
+        same = jnp.pad(same.astype(jnp.int32), ((0, 0), (1, 0))).reshape(TOKENS, 1)
+        facts.append((labels.reshape(TOKENS, 1), seg_ids, same))
     weights = list(gather_blocks(low, 1))
     weights[4] = weights[4][0]
-
-    def facts(index):
-        ahead, behind = batch[min(index, 1)], batch[max(index - 1, 0)]
-        return [jnp.where(second, behind[i][:, ::-1], ahead[i]) for i in (2, 3)]
-
+    gain_rows = weights[4][:, last + out : last + out + gain_count].astype(jnp.float32).T
+    gain_rows = jnp.pad(gain_rows, ((0, 8 - gain_count), (0, 0)))
     steps = []
-    arrived = None
+    arrived = jnp.zeros((TOKENS, LANES), jnp.float32)
     for index in range(3):
-        inputs = batch[min(index, 1)][0]
-        if arrived is None:
-            inputs = jnp.where(second, 0.0, inputs)
-        else:
-            inputs = jnp.where(second, arrived[..., :-1], inputs)
-        latent, logdet, saved = forward_block(inputs, *facts(index), weights, sizes)
-        if arrived is not None:
-            logdet = logdet + arrived[..., -1]
-        steps.append((latent, logdet, saved))
+        inputs = jnp.where(second, arrived, batch[min(index, 1)][0])
+        steps.append(step_forward(inputs, *facts[index], weights, gain_rows, table, channels))
         if index < 2:
-            arrived = lax.ppermute(
-                jnp.concatenate([latent, logdet[..., None]], 2)[:, ::-1], "rows", up
-            )
-    parts = []
-    grad_inputs = []
-    returned = jnp.zeros_like(batch[0][1])
+            arrived = back(lax.ppermute(steps[-1][0], "rows", up))
+    made = []
+    returned = jnp.zeros((TOKENS, LANES), jnp.float32)
     for index in range(3):
         grad_latent = jnp.where(second, batch[max(1 - index, 0)][1], returned)
-        grad, part = backward_block(grad_latent, steps[2 - index][2], weights, sizes)
-        parts.append(part)
-        grad_inputs.append(grad)
+        made.append(
+            step_backward(
+                grad_latent,
+                facts[2 - index][2],
+                weights,
+                gain_rows,
+                steps[2 - index][1:],
+                rows,
+                length,
+                table,
+                channels,
+            )
+        )
         if index < 2:
-            returned = lax.ppermute(grad[:, ::-1], "rows", down)
-    chosen = jax.tree.map(lambda a, b: jnp.where(second, a, b), parts[0], parts[2])
-    gain_grads = parts[1][3] + chosen[3]
-    both = jax.tree.map(lambda a, b: jnp.concatenate([a, b], 0), parts[1], chosen)
-    grads = weight_grads(both[:3] + (gain_grads,), low[4].shape[2])
-    sums = scatter_blocks(grads, 2)
-
-    def result(index):
-        return jnp.concatenate([steps[index][0], steps[index][1][..., None]], 2)
-
-    sent = jnp.where(second, result(1), jnp.pad(grad_inputs[1], ((0, 0), (0, 0), (0, 1))))
+            returned = back(lax.ppermute(made[-1][0], "rows", down))
+    gain_grads = made[1][1] + jnp.where(second, made[0][1], made[2][1])
+    gain_cols = jnp.pad(gain_grads[:gain_count].T, ((0, 0), (out, LANES - out - gain_count)))
+
+    def operands(step, grads):
+        _, na, aa, qkv, prob, ctx, nm, am, slope, gelu, stat, nf, af, tail, start = step
+        _, _, gqkv, gmid, gup, gbr, gstart, gpred = grads
+        return (aa, gqkv, ctx, gmid, am, gup, gelu, gbr, start, gstart, af, gpred)
+
+    sums = summed_products(
+        [operands(steps[i], made[2 - i]) for i in range(3)], gain_cols, low, 2
+    )
+    sent = jnp.where(second, steps[1][0], made[1][0])
     received = lax.ppermute(sent, "rows", swap)
-    outcome = jnp.where(second, result(2), received)
-    patch_grad = jnp.where(second, received[..., :-1], grad_inputs[2])
-    return outcome, patch_grad, sums
+    outcome = jnp.where(second, steps[2][0], received).reshape(rows, length, LANES)
+    patch_grad = jnp.where(second, received, made[2][0]).reshape(rows, length, LANES)
+    return outcome[..., : channels + 1], patch_grad[..., :channels], sums
 
 
 def unstaged(mine, low, sizes):

time: 916 us -> 624 us (0.68)
  matrix products: 235 us -> 0 us
  Pallas kernels: 317 us -> 498 us
  local copies, waits for them, and re-layouts: 188 us -> 30.4 us
  other arithmetic: 124 us -> 37.9 us
  waiting for transfers between devices: 1.5 us -> 11.1 us
    dot_general x106 -> x0, matrix products: 235 us -> none  [the longest x70 201 us: dot(): lax.dot_general(left, right, (dims, ((), ())), preferred_element_type=jnp...]
    pallas_call x1 -> x7, Pallas kernels: 177 us -> 367 us  [the longest x1 180 us: summed_products(): pl.pallas_call(functools.partial(products_kernel, units, n_pairs), out_sh...]
    unnamed x743 -> x91, local copies, waits for them, and re-layouts: 50.6 us -> 6.51 us
    slice x28 -> x1, local copies, waits for them, and re-layouts: 35.6 us -> 0.19 us  [staged(): gain_grads[:gain_count]]
    reshape x30 -> x13, local copies, waits for them, and re-layouts: 39.5 us -> 7.63 us  [the longest x3 2.41 us: staged(): facts.append((labels.reshape(TOKENS, 1), seg_ids, same))]
    another operation x7 -> x0, other arithmetic: 23.4 us -> none  [the longest x4 21.7 us: weight_grads(): jnp.stack([dot(*layer[i], ((0,), (0,))).astype(jnp.bfloat16) for layer in...]
    select_n x21 -> x13, other arithmetic: 22.4 us -> 2.96 us  [the longest x4 1.31 us: staged(): jnp.where(second, behind[i][:, ::-1], ahead[i])]
    another operation x21 -> x0, local copies, waits for them, and re-layouts: 18.8 us -> none  [the longest x20 18.8 us: backward_block(): jnp.stack(gain_grads, 1)]
  transfers between devices with their start and end apart: 9 -> 9, of which waited for: 1 -> 3; matrix products, arithmetic and copies ran while one was open for 43% -> 7% of each run, Pallas kernels for 35% -> 64%
where the time goes in v2:
time: 624 us; the launch traced here: 619 us
  Pallas kernels  498 us (80%)
  other arithmetic  37.9 us (6%)
  local copies, waits for them, and re-layouts  30.4 us (5%)
  starting transfers between devices  28.8 us (5%)
  blocking collectives  11.3 us (2%)
  waiting for transfers between devices  11.1 us (2%)
    pallas_call x1, Pallas kernels, summed_products(): pl.pallas_call(functools.partial(products_kernel, units, n_pairs), out_sh...  180 us
    pallas_call x1, Pallas kernels, gather_blocks(): pl.pallas_call(functools.partial(gather_kernel, units, len(shards)), out_...  132 us
    pallas_call x3, Pallas kernels, step_backward(): pl.pallas_call(functools.partial(step_backward_kernel, (rows, length, tab...  113 us
    pallas_call x3, Pallas kernels, step_forward(): pl.pallas_call(functools.partial(step_forward_kernel, (rows, length, tabl...  73.5 us
    sub x8, other arithmetic, adam_step(): weight - rate * (first_hat / (jnp.sqrt(second_hat) + EPS_ADAM) + DECAY *...  19.9 us
    ppermute x2, starting transfers between devices, staged(): arrived = back(lax.ppermute(steps[-1][0], 'rows', up))  17.7 us
  transfers between devices with their start and end apart: 9, of which 3 were waited for; matrix products, arithmetic and copies ran while one was open for 7% of the time, Pallas kernels for 64%

profile of v2, /device:TPU:8, one launch (start us, length us, event | category | flops | bytes accessed | tf_op | source)
XLA Modules:
  0.0 619.3 jit_solution(25702542527609300)
XLA Ops:
  0.7 0.8 constant_dynamic-slice_fusion.4
  2.3 2.6 collective-permute-start.2
  4.9 1.4 select_reduce_fusion
  6.6 0.8 convert_element_type.56
  7.4 0.9 pad_maximum_fusion
  8.4 5.6 all_gather.9
  14.3 0.7 pad.30
  15.0 2.6 collective-permute-start
  17.6 0.7 pad.36
  19.3 0.7 copy.272
  20.0 0.7 convert_bitcast_fusion
  21.4 2.8 convert_element_type.60.refs_2_
  24.2 1.1 convert_element_type.61.refs_3_
  25.3 0.8 copy-done.3
  26.1 1.0 convert_element_type.58.refs_0_
  27.1 0.7 convert_element_type.59.refs_1_
  27.9 0.8 concatenate.10.refs_4_
  28.7 131.8 %gather_blocks.1 = (bf16[2,768,2304]{2,1,0:T(8,128)(2,1)}, bf16[2,768,768]{2,1,0:T(8,128)(2,1)}, bf16[2,768,3072]{2,1,0:T(8,128)(2,1)}, bf16[2,3072,768]{2,1,0:T(8,128)(2,1)}, bf16[1,768,1280]{2,1,0:T(8,128)(2,1)}) custom-call(bf16[4,48,2304]{2,1,0:T(8,128)(2,1)} %convert_element_type.58.refs_0_, bf16[4,48,768]{2,1,0:T(8,128)(2,1)} %convert_element_type.59.refs_1_, ...), custom_call_target="tpu_custom_call" | custom-call | tf_op jit(solution)/shard_map/gather_blocks/pallas_call | solution.py:208
  160.5 3.2 copy.273
  164.7 0.7 broadcast_select_fusion.15
  166.1 0.8 copy.274.labels
  166.9 0.7 broadcast_select_fusion.13
  167.7 0.7 broadcast_select_fusion.8
  168.5 0.8 copy.276.same
  169.3 0.8 copy.275.seg_col
  171.3 24.4 %step_forward.3 = (f32[256,128]{1,0:T(8,128)}, f32[2,256,768]{2,1,0:T(8,128)}, bf16[2,256,768]{2,1,0:T(8,128)(2,1)}, bf16[2,256,2304]{2,1,0:T(8,128)(2,1)}, f32[...) custom-call(f32[256,128]{1,0:T(8,128)} %bitcast.70, ...), custom_call_target="tpu_custom_call" | custom-call | flops 7751073792 | bytes 52428800 | tf_op jit(solution)/shard_map/step_forward/pallas_call | solution.py:498
  195.7 13.2 %collective-permute-start.3 = (f32[256,128]{1,0:T(8,128)}, f32[256,128]{1,0:T(8,128)S(1)}, u32[]{:S(2)}, u32[]{:S(2)}) collective-permute-start(f32[256,128]{1,0:T(8,128)} %get-tuple-element.111), channel_id=1, source_target_pairs={{0,16},{2,18},{4,20},{6,22},{8,24},{10,26},{12,28},{14,30},{1,17},... | collective-permute-start | bytes 393224 | tf_op jit(solution)/shard_map/ppermute | solution.py:1336
  208.9 0.8 copy.280.labels
  209.7 0.8 copy.282.same
  210.5 0.8 copy.281.seg_col
  211.3 0.8 copy.286.labels
  212.2 0.8 copy.288.same
  213.0 0.8 copy.287.seg_col
  214.7 24.5 %step_forward.4 = (f32[256,128]{1,0:T(8,128)}, f32[2,256,768]{2,1,0:T(8,128)}, bf16[2,256,768]{2,1,0:T(8,128)(2,1)}, bf16[2,256,2304]{2,1,0:T(8,128)(2,1)}, f32[...) custom-call(f32[256,128]{1,0:T(8,128)} %bitcast.71, ...), custom_call_target="tpu_custom_call" | custom-call | flops 7751073792 | bytes 52428800 | tf_op jit(solution)/shard_map/step_forward/pallas_call | solution.py:498
  239.2 4.5 collective-permute-start.4
  244.5 2.5 collective-permute-done.4
  247.9 24.6 %step_forward.5 = (f32[256,128]{1,0:T(8,128)}, f32[2,256,768]{2,1,0:T(8,128)}, bf16[2,256,768]{2,1,0:T(8,128)(2,1)}, bf16[2,256,2304]{2,1,0:T(8,128)(2,1)}, f32[...) custom-call(f32[256,128]{1,0:T(8,128)} %bitcast.72, ...), custom_call_target="tpu_custom_call" | custom-call | flops 7751073792 | bytes 52428800 | tf_op jit(solution)/shard_map/step_forward/pallas_call | solution.py:498
  272.6 37.6 %step_backward.3 = (f32[256,128]{1,0:T(8,128)}, f32[8,768]{1,0:T(8,128)}, bf16[2,256,2304]{2,1,0:T(8,128)(2,1)}, bf16[2,256,768]{2,1,0:T(8,128)(2,1)}, bf16[2,25...) custom-call(f32[256,128]{1,0:T(8,128)} %bitcast.68, ...), custom_call_target="tpu_custom_call" | custom-call | flops 7751073792 | bytes 52428800 | tf_op jit(solution)/shard_map/step_backward/pallas_call | solution.py:768
  310.2 1.3 collective-permute-start.6
  311.8 0.9 copy.304
  312.7 5.5 collective-permute-done.6
  319.0 37.4 %step_backward.4 = (f32[256,128]{1,0:T(8,128)}, f32[8,768]{1,0:T(8,128)}, bf16[2,256,2304]{2,1,0:T(8,128)(2,1)}, bf16[2,256,768]{2,1,0:T(8,128)(2,1)}, bf16[2,25...) custom-call(f32[256,128]{1,0:T(8,128)} %bitcast.73, ...), custom_call_target="tpu_custom_call" | custom-call | flops 7751073792 | bytes 52428800 | tf_op jit(solution)/shard_map/step_backward/pallas_call | solution.py:768
  356.4 1.3 collective-permute-start.8
  357.8 0.9 broadcast_select_fusion.5
  358.7 2.7 collective-permute-start.7
  361.4 3.1 collective-permute-done.8
  365.4 37.6 %step_backward.5 = (f32[256,128]{1,0:T(8,128)}, f32[8,768]{1,0:T(8,128)}, bf16[2,256,2304]{2,1,0:T(8,128)(2,1)}, bf16[2,256,768]{2,1,0:T(8,128)(2,1)}, bf16[2,25...) custom-call(f32[256,128]{1,0:T(8,128)} %bitcast.69, ...), custom_call_target="tpu_custom_call" | custom-call | flops 7751073792 | bytes 52428800 | tf_op jit(solution)/shard_map/step_backward/pallas_call | solution.py:768
  403.0 0.9 copy.305
  404.3 0.9 pad.37.refs_36_
  405.2 180.4 %summed_products.1 = (bf16[4,48,2304]{2,1,0:T(8,128)(2,1)}, bf16[4,48,768]{2,1,0:T(8,128)(2,1)}, bf16[4,48,3072]{2,1,0:T(8,128)(2,1)}, bf16[4,192,768]{2,1,0:T(8,128)(2,1)}, bf16[2,48,1280]{2,1,0:T(8,128)(2,1)}) custom-call(bf16[2,256,768]{2,1,0:T(8,128)(2,1)} %get-tuple-element.141.refs_0_, bf16[2,256,2304]{2,1,0:T(8,128)(2,1)} %get-tuple-element.142.refs_1_, ...), custom_call_target="tpu_custom_call" | custom-call | tf_op jit(solution)/shard_map/summed_products/pallas_call | solution.py:992
  585.6 1.0 convert_element_type.66
  586.8 0.7 copy.319
  588.8 0.7 copy.316
  589.5 0.7 copy.317
  590.2 0.7 copy.318
  591.2 5.7 all-gather
  597.6 0.8 constant_dynamic-slice_fusion.2
  598.4 2.5 multiply_subtract_fusion.4
  600.9 1.5 multiply_subtract_fusion.6
  602.4 6.7 %multiply_subtract_fusion = (f32[4,192,768]{2,1,0:T(8,128)}, f32[4,192,768]{2,1,0:T(8,128)}, f32[4,192,768]{2,1,0:T(8,128)}) fusion(f32[4,192,768]{2,1,0:T(8,128)S(1)} %copy-done.1, bf16[4,192,768]{2,1,0:T(8,128)(2,1)S(1)} %copy-done.13, f32[4,192,768]{2,1,0:T(8,128)} %param.49, f32[4,192,768]{2,1,0:T(8,128)} %param.48), kind=kLoop, calls=%fused_computation.9 | loop fusion | flops 9437184 | bytes 15335424 | tf_op jit(solution)/shard_map/sub | solution.py:1280
  609.2 4.4 multiply_subtract_fusion.1
  613.5 0.8 copy-done.14
  614.4 3.2 multiply_subtract_fusion.2
  617.6 1.5 multiply_subtract_fusion.3
  (147 shorter events, 13.7 us)
Async XLA Ops:
  0.7 18.0 %copy-start.26 = (f32[2,48,48]{2,1,0:T(8,128)S(1)}, f32[2,48,48]{2,1,0:T(8,128)}, u32[]{:S(2)}) copy-start(f32[2,48,48]{2,1,0:T(8,128)} %param.32) | copy-start | bytes 55300
  0.7 18.0 %copy-start.35 = (f32[2,5,48]{2,0,1:T(2,128)S(1)}, f32[2,5,48]{2,0,1:T(2,128)}, u32[]{:S(2)}) copy-start(f32[2,5,48]{2,0,1:T(2,128)} %param.53) | copy-start | bytes 5764
  0.7 19.3 %copy-start.11 = (f32[2,1000,48]{1,2,0:T(8,128)S(1)}, f32[2,1000,48]{1,2,0:T(8,128)}, u32[]{:S(2)}) copy-start(f32[2,1000,48]{1,2,0:T(8,128)} %param.35) | copy-start | bytes 1152004
  0.7 20.0 %copy-start.19 = (f32[2,48,96]{2,1,0:T(8,128)S(1)}, f32[2,48,96]{2,1,0:T(8,128)}, u32[]{:S(2)}) copy-start(f32[2,48,96]{2,1,0:T(8,128)} %param.50) | copy-start | bytes 110596
  2.3 164.6 %collective-permute-start.2 = (s32[2,128]{1,0:T(2,128)}, s32[2,128]{1,0:T(2,128)}, u32[]{:S(2)}, u32[]{:S(2)}) collective-permute-start(s32[2,128]{1,0:T(2,128)} %convert_reduce_fusion), channel_id=1, source_target_pairs={{0,16},{2,18},{4,20},{6,22},{8,24},{10,26},{12,28},{14,30},{16,0},... | collective-permute-start | bytes 3080 | tf_op jit(solution)/shard_map/ppermute | solution.py:1311
  6.3 158.4 %collective-permute-start.1 = (s32[2,128]{1,0:T(2,128)}, s32[2,128]{1,0:T(2,128)}, u32[]{:S(2)}, u32[]{:S(2)}) collective-permute-start(s32[2,128]{1,0:T(2,128)} %select_reduce_fusion), channel_id=1, source_target_pairs={{0,16},{2,18},{4,20},{6,22},{8,24},{10,26},{12,28},{14,30},{16,0},... | collective-permute-start | bytes 3080 | tf_op jit(solution)/shard_map/ppermute | solution.py:1311
  15.0 9.2 %copy-start = (f32[4,192,768]{2,1,0:T(8,128)S(1)}, f32[4,192,768]{2,1,0:T(8,128)}, u32[]{:S(2)}) copy-start(f32[4,192,768]{2,1,0:T(8,128)} %param.47) | copy-start | bytes 7077892
  15.0 155.5 %collective-permute-start = (f32[2,128,128]{2,0,1:T(2,128)}, f32[2,128,128]{2,0,1:T(2,128)S(1)}, u32[]{:S(2)}, u32[]{:S(2)}) collective-permute-start(f32[2,128,128]{2,0,1:T(2,128)} %pad.30), channel_id=1, source_target_pairs={{0,16},{2,18},{4,20},{6,22},{8,24},{10,26},{12,28},{14,30},{16,0},... | collective-permute-start | bytes 393224 | tf_op jit(solution)/shard_map/ppermute | solution.py:1311
  18.3 225.5 %collective-permute-start.5 = (f32[2,128,128]{2,0,1:T(2,128)}, f32[2,128,128]{2,0,1:T(2,128)S(1)}, u32[]{:S(2)}, u32[]{:S(2)}) collective-permute-start(f32[2,128,128]{2,0,1:T(2,128)} %pad.36), channel_id=1, source_target_pairs={{0,16},{2,18},{4,20},{6,22},{8,24},{10,26},{12,28},{14,30},{16,0},... | collective-permute-start | bytes 393224 | tf_op jit(solution)/shard_map/ppermute | solution.py:1311
  24.2 1.9 copy-start.3
  24.2 2.9 copy-start.5
  26.1 1.8 copy-start.15
  26.1 1.8 copy-start.24
  26.1 1.8 copy-start.25
  160.5 3.2 copy-start.37
  160.5 4.0 copy-start.36
  168.4 2.9 copy-start.33
  168.4 42.1 %copy-start.32 = (s32[2,128]{1,0:T(2,128)}, s32[2,128]{1,0:T(2,128)S(1)}, u32[]{:S(2)}) copy-start(s32[2,128]{1,0:T(2,128)S(1)} %get-tuple-element.344.seg_row) | copy-start | bytes 3076
  170.4 42.6 %copy-start.31 = (s32[2,128]{1,0:T(2,128)}, s32[2,128]{1,0:T(2,128)S(1)}, u32[]{:S(2)}) copy-start(s32[2,128]{1,0:T(2,128)S(1)} %broadcast_select_fusion.6.seg_row) | copy-start | bytes 3076
  195.7 18.2 %collective-permute-start.3 = (f32[256,128]{1,0:T(8,128)}, f32[256,128]{1,0:T(8,128)S(1)}, u32[]{:S(2)}, u32[]{:S(2)}) collective-permute-start(f32[256,128]{1,0:T(8,128)} %get-tuple-element.111), channel_id=1, source_target_pairs={{0,16},{2,18},{4,20},{6,22},{8,24},{10,26},{12,28},{14,30},{1,17},... | collective-permute-start | bytes 393224 | tf_op jit(solution)/shard_map/ppermute | solution.py:1336
  239.2 7.8 %collective-permute-start.4 = (f32[256,128]{1,0:T(8,128)}, f32[256,128]{1,0:T(8,128)S(1)}, u32[]{:S(2)}, u32[]{:S(2)}) collective-permute-start(f32[256,128]{1,0:T(8,128)} %get-tuple-element.112), channel_id=1, source_target_pairs={{0,16},{2,18},{4,20},{6,22},{8,24},{10,26},{12,28},{14,30},{1,17},... | collective-permute-start | bytes 393224 | tf_op jit(solution)/shard_map/ppermute | solution.py:1336
  272.5 39.0 %copy-start.38 = (f32[2,5,48]{2,0,1:T(2,128)S(1)}, f32[2,5,48]{2,0,1:T(2,128)}, u32[]{:S(2)}) copy-start(f32[2,5,48]{2,0,1:T(2,128)} %param.55) | copy-start | bytes 5764
  272.6 39.1 %copy-start.27 = (f32[2,48,48]{2,1,0:T(8,128)S(1)}, f32[2,48,48]{2,1,0:T(8,128)}, u32[]{:S(2)}) copy-start(f32[2,48,48]{2,1,0:T(8,128)} %param.33) | copy-start | bytes 55300
  272.6 39.1 %copy-start.28 = (f32[2,48,48]{2,1,0:T(8,128)S(1)}, f32[2,48,48]{2,1,0:T(8,128)}, u32[]{:S(2)}) copy-start(f32[2,48,48]{2,1,0:T(8,128)} %param.34) | copy-start | bytes 55300
  310.2 8.0 %collective-permute-start.6 = (f32[256,128]{1,0:T(8,128)}, f32[256,128]{1,0:T(8,128)S(1)}, u32[]{:S(2)}, u32[]{:S(2)}) collective-permute-start(f32[256,128]{1,0:T(8,128)} %get-tuple-element.122), channel_id=1, source_target_pairs={{16,0},{18,2},{20,4},{22,6},{24,8},{26,10},{28,12},{30,14},{17,1},... | collective-permute-start | bytes 393224 | tf_op jit(solution)/shard_map/ppermute | solution.py:1355
  319.0 38.7 %copy-start.21 = (f32[256,128]{1,0:T(8,128)S(1)}, f32[256,128]{1,0:T(8,128)}, u32[]{:S(2)}) copy-start(f32[256,128]{1,0:T(8,128)} %get-tuple-element.112) | copy-start | bytes 393220
  356.4 8.0 %collective-permute-start.8 = (f32[256,128]{1,0:T(8,128)}, f32[256,128]{1,0:T(8,128)S(1)}, u32[]{:S(2)}, u32[]{:S(2)}) collective-permute-start(f32[256,128]{1,0:T(8,128)} %get-tuple-element.131), channel_id=1, source_target_pairs={{16,0},{18,2},{20,4},{22,6},{24,8},{26,10},{28,12},{30,14},{17,1},... | collective-permute-start | bytes 393224 | tf_op jit(solution)/shard_map/ppermute | solution.py:1355
  358.7 232.2 %collective-permute-start.7 = (f32[256,128]{1,0:T(8,128)S(1)}, f32[256,128]{1,0:T(8,128)S(1)}, u32[]{:S(2)}, u32[]{:S(2)}) collective-permute-start(f32[256,128]{1,0:T(8,128)S(1)} %broadcast_select_fusion.5), channel_id=1, source_target_pairs={{0,16},{2,18},{4,20},{6,22},{8,24},{10,26},{12,28},{14,30},{16,0},... | collective-permute-start | bytes 393224 | tf_op jit(solution)/shard_map/ppermute | solution.py:1368
  365.4 38.7 %copy-start.34 = (f32[8,768]{1,0:T(8,128)S(1)}, f32[8,768]{1,0:T(8,128)}, u32[]{:S(2)}) copy-start(f32[8,768]{1,0:T(8,128)} %get-tuple-element.177) | copy-start | bytes 73732
  405.2 185.7 %copy-start.22 = (f32[256,128]{1,0:T(8,128)S(1)}, f32[256,128]{1,0:T(8,128)}, u32[]{:S(2)}) copy-start(f32[256,128]{1,0:T(8,128)} %get-tuple-element.113) | copy-start | bytes 393220
  405.2 185.7 %copy-start.23 = (f32[256,128]{1,0:T(8,128)S(1)}, f32[256,128]{1,0:T(8,128)}, u32[]{:S(2)}) copy-start(f32[256,128]{1,0:T(8,128)} %get-tuple-element.140) | copy-start | bytes 393220
  586.6 4.3 copy-start.8
  590.9 10.0 %copy-start.20 = (f32[2,48,96]{2,1,0:T(8,128)S(1)}, f32[2,48,96]{2,1,0:T(8,128)}, u32[]{:S(2)}) copy-start(f32[2,48,96]{2,1,0:T(8,128)} %param.50) | copy-start | bytes 110596
  591.0 10.0 %copy-start.29 = (f32[2,48,96]{2,1,0:T(8,128)S(1)}, f32[2,48,96]{2,1,0:T(8,128)}, u32[]{:S(2)}) copy-start(f32[2,48,96]{2,1,0:T(8,128)} %param.52) | copy-start | bytes 110596
  591.0 10.0 %copy-start.30 = (f32[2,48,96]{2,1,0:T(8,128)S(1)}, f32[2,48,96]{2,1,0:T(8,128)}, u32[]{:S(2)}) copy-start(f32[2,48,96]{2,1,0:T(8,128)} %param.51) | copy-start | bytes 110596
  591.0 11.4 %copy-start.1 = (f32[4,192,768]{2,1,0:T(8,128)S(1)}, f32[4,192,768]{2,1,0:T(8,128)}, u32[]{:S(2)}) copy-start(f32[4,192,768]{2,1,0:T(8,128)} %param.47) | copy-start | bytes 7077892
  591.2 11.2 %copy-start.13 = (bf16[4,192,768]{2,1,0:T(8,128)(2,1)S(1)}, bf16[4,192,768]{2,1,0:T(8,128)(2,1)}, u32[]{:S(2)}) copy-start(bf16[4,192,768]{2,1,0:T(8,128)(2,1)} %get-tuple-element.184) | copy-start | bytes 3538948
  602.4 6.7 %copy-start.2 = (f32[4,48,3072]{2,1,0:T(8,128)S(1)}, f32[4,48,3072]{2,1,0:T(8,128)}, u32[]{:S(2)}) copy-start(f32[4,48,3072]{2,1,0:T(8,128)} %param.44) | copy-start | bytes 7077892
  602.4 6.7 %copy-start.6 = (f32[4,48,3072]{2,1,0:T(8,128)S(1)}, f32[4,48,3072]{2,1,0:T(8,128)}, u32[]{:S(2)}) copy-start(f32[4,48,3072]{2,1,0:T(8,128)} %param.46) | copy-start | bytes 7077892
  602.4 6.7 %copy-start.7 = (f32[4,48,3072]{2,1,0:T(8,128)S(1)}, f32[4,48,3072]{2,1,0:T(8,128)}, u32[]{:S(2)}) copy-start(f32[4,48,3072]{2,1,0:T(8,128)} %param.45) | copy-start | bytes 7077892
  602.4 6.7 %copy-start.12 = (bf16[4,48,3072]{2,1,0:T(8,128)(2,1)S(1)}, bf16[4,48,3072]{2,1,0:T(8,128)(2,1)}, u32[]{:S(2)}) copy-start(bf16[4,48,3072]{2,1,0:T(8,128)(2,1)} %get-tuple-element.183) | copy-start | bytes 3538948
  609.1 4.4 copy-start.4
  609.2 4.4 copy-start.9
  609.2 4.4 copy-start.10
  609.2 5.2 copy-start.14
  614.4 3.2 copy-start.16
  614.4 3.2 copy-start.17
  614.4 3.2 copy-start.18

commit v3 on v1

v3 whole, which is shorter than its diff:
```python
import functools
from functools import partial

import jax
import jax.numpy as jnp
from jax import lax
from jax.experimental import pallas as pl
from jax.experimental.pallas import tpu as pltpu
from jax.sharding import PartitionSpec as P

HEADS = 12
HEAD_DIM = 64
LAYERS = 2
SEGS = 4
STEP = 10

EPS_NORM = 1e-05
MASKED = -1000000000.0
BETA_ONE = 0.9
BETA_TWO = 0.95
EPS_ADAM = 1e-08
DECAY = 0.1
RATES = (0.05, 0.3, 0.02, 0.05, 0.02, 0.01, 0.01, 0.3)

MESH_ID = pl.DeviceIdType.MESH
LANES = 128
LATE = (0, 1, 2)
GATHER_LAGS = (1.5, 3.5, 5.5, 8.5, 0.0, 1.0, 1.7, 3.0)


def place():
    r = lax.axis_index("rows")
    x = lax.axis_index("seq")
    c = lax.rem(r, 2)
    y = lax.rem(r // 2, 2)
    z = r // 4
    return r, x, y, z, c


def units_of(shards, d1_share):
    units = []
    order = sorted(range(len(shards)), key=lambda a: shards[a].shape[0])
    layers = max(s.shape[0] // 2 for s in shards)
    todo = [(a, 0) for a in order if shards[a].shape[0] == 2]
    for l in range(layers):
        todo += [(a, l) for a in order if shards[a].shape[0] > 2]
    for a, l in todo:
        n, rows, cols = shards[a].shape
        half = cols // 2
        if rows >= 64:
            first = max(16, round(rows * d1_share / 16) * 16)
            split = (0, first)
        else:
            first = max(LANES, round(half * d1_share / LANES) * LANES)
            split = (1, first)
        units.append((a, l, n // 2, rows, half, split))
    return units


def wait_all_of(cell, sem):
    pltpu.make_async_copy(cell, cell, sem).wait()


def gather_kernel(units, late, lags, n_arrays, *refs):
    srcs, outs = refs[:n_arrays], refs[n_arrays : 2 * n_arrays]
    send, recv, local = refs[2 * n_arrays :]
    r, x, y, z, c = place()
    stage = z // 2
    other = 1 - stage
    zi = lax.rem(z, 2)
    dev_x = (r, 1 - x)
    dev_y = (r + 2 - 4 * y, x)
    dev_s = (r + 1 - 2 * c, x)
    z_near = z + 1 - 2 * zi
    z_src = (z_near, other * 2, other * 2 + 1)
    dev_z = tuple((zz * 4 + y * 2 + c, x) for zz in z_src)
    barrier = pltpu.get_barrier_semaphore()
    partners = (dev_x, dev_y, dev_s) + dev_z
    for dev in partners:
        pl.semaphore_signal(barrier, 1, device_id=dev, device_id_type=MESH_ID)
    pl.semaphore_wait(barrier, len(partners))

    inner = stage != zi
    dev_inner = ((1 + other) * 4 + y * 2 + c, x)
    side_of = jnp.where(inner, other, stage)
    z_mine, z_theirs = 2 * side_of, 2 - 2 * side_of
    started = []

    def cell(u, zz, yy, cc, h=None, part=None):
        a, l, _, rows, half, (dim, first) = units[u]
        row0, nrow = (zz * 4 + yy * 2 + cc) * rows, rows
        col0, ncol = (0, 2 * half) if h is None else (h * half, half)
        if part is not None:
            if dim == 0:
                row0, nrow = (row0, first) if part == 0 else (row0 + first, rows - first)
            else:
                col0, ncol = (col0, first) if part == 0 else (col0 + first, half - first)
        if h is not None:
            col0 = pl.multiple_of(col0, LANES)
        return outs[a].at[l, pl.ds(pl.multiple_of(row0, 16), nrow), pl.ds(col0, ncol)]

    def own(u, b, h=None):
        a, l, layers, rows, half, _ = units[u]
        if h is None:
            return srcs[a].at[layers * b + l]
        return srcs[a].at[layers * b + l, :, pl.ds(pl.multiple_of(h * half, LANES), half)]

    def push(u, src, dst, idx, dev, slot=None):
        cp = pltpu.make_async_remote_copy(
            src_ref=src,
            dst_ref=dst,
            send_sem=send.at[u, idx if slot is None else slot],
            recv_sem=recv.at[u, idx],
            device_id=dev,
            device_id_type=MESH_ID,
        )
        cp.start()
        started.append(cp)

    def arrived(u, dst, idx):
        wait_all_of(dst, recv.at[u, idx])

    def relay_copy(u, piece, j):
        return pltpu.make_async_remote_copy(
            src_ref=piece,
            dst_ref=piece,
            send_sem=send.at[u, 24 + j],
            recv_sem=recv.at[u, j],
            device_id=dev_z[0],
            device_id_type=MESH_ID,
        )

    def relay(u, piece, j):
        @pl.when(inner)
        def _():
            relay_copy(u, piece, j).start()

    def begin(u):
        mine = cell(u, z, y, c, x)
        push(u, own(u, other, x), mine, 1 + zi, dev_inner, slot=1)
        if u in late:

            @pl.when(inner)
            def _():
                near_copy(u).start()

            @pl.when(jnp.logical_not(inner))
            def _():
                own_copy(u).start()

            return
        push(u, own(u, stage, x), mine, 0, dev_z[0])
        push(u, own(u, stage, x), mine, 10, dev_y)
        push(u, own(u, stage), cell(u, z, y, c), 17, dev_s)
        pltpu.make_async_copy(own(u, stage), cell(u, z, y, c), local.at[u]).start()

    def near_copy(u):
        return pltpu.make_async_remote_copy(
            src_ref=own(u, stage, x),
            dst_ref=cell(u, z, y, c, x),
            send_sem=send.at[u, 0],
            recv_sem=recv.at[u, 1 + zi],
            device_id=dev_z[0],
            device_id_type=MESH_ID,
        )

    def own_copy(u):
        return pltpu.make_async_copy(own(u, stage, x), cell(u, z, y, c, x), recv.at[u, 1 + zi])

    def near(u):
        if u in late:
            return
        arrived(u, cell(u, z, 1 - y, c, x), 10)
        push(u, cell(u, z, 1 - y, c, x), cell(u, z, 1 - y, c, x), 6, dev_x)
        side(u, 0, z_src[0], 0)

    def side(u, j, zz, idx):
        piece = cell(u, zz, y, c, x)
        arrived(u, piece, idx)
        if u not in late and j > 0:
            relay(u, piece, j)
        push(u, piece, piece, 3 + j, dev_x)
        push(u, piece, piece, 7 + j, dev_y)

    def spread(u):
        if u in late:
            for j in range(2):
                side(u, j, z_mine + j, 1 + j)
        else:
            for j in (1, 2):
                side(u, j, z_src[j], j)

    def turn(u, j, zz):
        arrived(u, cell(u, zz, y, c, 1 - x), 3 + j)
        part = cell(u, zz, y, c, 1 - x, 0)
        push(u, part, part, 11 + j, dev_y)
        arrived(u, cell(u, zz, 1 - y, c, x), 7 + j)
        part = cell(u, zz, 1 - y, c, x, 1)
        push(u, part, part, 14 + j, dev_x)

    def near_corner(u):
        if u not in late:
            turn(u, 0, z_src[0])
            slab = cell(u, z_src[0], y, c)
            push(u, slab, slab, 19, dev_s)

    def corner(u):
        if u in late:
            for j in range(2):
                turn(u, j, z_mine + j)
        else:
            for j in (1, 2):
                turn(u, j, z_src[j])
                slab = cell(u, z_src[j], y, c)
                push(u, slab, slab, 19 + j, dev_s)

    def corners_in(u, j, zz):
        arrived(u, cell(u, zz, 1 - y, c, 1 - x, 0), 11 + j)
        arrived(u, cell(u, zz, 1 - y, c, 1 - x, 1), 14 + j)

    def finish(u):
        if u in late:
            for j in range(2):
                corners_in(u, j, z_mine + j)
                for yy in range(2):
                    slab = cell(u, z_mine + j, yy, c)
                    push(u, slab, slab, (0, 5, 6, 9)[2 * j + yy], dev_z[0], slot=(2, 5, 6, 9)[2 * j + yy])
                    push(u, slab, slab, 17 + 2 * j + yy, dev_s)
            return
        arrived(u, cell(u, z, 1 - y, c, 1 - x), 6)
        slab = cell(u, z, 1 - y, c)
        push(u, slab, slab, 18, dev_s)
        for j in range(3):
            corners_in(u, j, z_src[j])
            slab = cell(u, z_src[j], 1 - y, c)
            push(u, slab, slab, 22 + j, dev_s)

    def last(u):
        if u in late:
            for j in range(2):
                for yy in range(2):
                    slab = cell(u, z_theirs + j, yy, c)
                    arrived(u, slab, (0, 5, 6, 9)[2 * j + yy])
                    push(u, slab, slab, 21 + 2 * j + yy, dev_s)

    n = len(units)
    order = sorted(range(n), key=lambda u: u not in late)
    events = [(1.0 * i - lags[7], begin, u) for i, u in enumerate(order)]
    events += [(lags[0] + 1.0 * i, spread, u) for i, u in enumerate(order)]
    events += [(lags[1] + 1.0 * i, corner, u) for i, u in enumerate(order)]
    events += [(lags[2] + 1.0 * i, finish, u) for i, u in enumerate(order)]
    events += [(lags[3] + 1.0 * i, last, u) for i, u in enumerate(order)]
    events += [(lags[4] + lags[5] * i, near, u) for i, u in enumerate(order)]
    events += [(lags[6] + 1.0 * i, near_corner, u) for i, u in enumerate(order)]
    for _, act, u in sorted(events, key=lambda e: e[0]):
        act(u)
    for u in range(n):
        if u in late:
            for j in range(2):
                for yy in range(2):
                    arrived(u, cell(u, z_mine + j, yy, 1 - c), 17 + 2 * j + yy)
                    arrived(u, cell(u, z_theirs + j, yy, 1 - c), 21 + 2 * j + yy)

            @pl.when(inner)
            def _():
                near_copy(u).wait_send()

            continue
        arrived(u, cell(u, z, y, 1 - c), 17)
        arrived(u, cell(u, z, 1 - y, 1 - c), 18)
        for j in range(3):
            arrived(u, cell(u, z_src[j], y, 1 - c), 19 + j)
            arrived(u, cell(u, z_src[j], 1 - y, 1 - c), 22 + j)
        pltpu.make_async_copy(own(u, stage), cell(u, z, y, c), local.at[u]).wait()
        for j in (1, 2):

            @pl.when(inner)
            def _():
                relay_copy(u, cell(u, z_src[j], y, c, x), j).wait_send()

    for cp in started:
        cp.wait_send()


def gather_blocks(shards, collective_id):
    units = units_of(shards, 0.5)
    out = [
        jax.ShapeDtypeStruct((s.shape[0] // 2, 16 * s.shape[1], s.shape[2]), s.dtype)
        for s in shards
    ]
    n = len(units)
    return pl.pallas_call(
        functools.partial(gather_kernel, units, LATE, GATHER_LAGS, len(shards)),
        out_shape=out,
        in_specs=[pl.BlockSpec(memory_space=pl.ANY)] * len(shards),
        out_specs=[pl.BlockSpec(memory_space=pl.ANY)] * len(shards),
        scratch_shapes=[
            pltpu.SemaphoreType.DMA((n, 27)),
            pltpu.SemaphoreType.DMA((n, 25)),
            pltpu.SemaphoreType.DMA((n,)),
        ],
        compiler_params=pltpu.CompilerParams(collective_id=collective_id, has_side_effects=True),
        name="gather_blocks",
    )(*shards)


TOKENS = 256
HALF_LANES = 64
FORWARD_VMEM = 58 * 2**20


def lane_of(shape):
    return lax.broadcasted_iota(jnp.int32, shape, len(shape) - 1)


def norm_rows(hidden):
    center = hidden - jnp.mean(hidden, -1, keepdims=True)
    inverse = lax.rsqrt(jnp.mean(center * center, -1, keepdims=True) + EPS_NORM)
    return center * inverse, inverse


def gelu_and_slope(v):
    root = 0.7978845608028654
    square = v * v
    wave = jnp.tanh(root * (v + 0.044715 * (square * v)))
    near = 0.5 * (1.0 + wave)
    slope = near + (0.5 * root) * v * (1.0 - wave * wave) * (1.0 + (3 * 0.044715) * square)
    return v * near, slope


def turned_round(part):
    length = part.shape[0]
    down = lax.broadcasted_iota(jnp.int32, (length, length), 0)
    flip = (down + lane_of((length, length)) == length - 1).astype(jnp.bfloat16)
    total = None
    for _ in range(3):
        high = part.astype(jnp.bfloat16)
        part = part - high.astype(jnp.float32)
        moved = jnp.dot(flip, high, preferred_element_type=jnp.float32)
        total = moved if total is None else total + moved
    return total


def packed_pair(part, length):
    lane = lane_of((length, LANES))
    return jnp.where(lane < HALF_LANES, part[:length], pltpu.roll(part[length:], HALF_LANES, 1))


def unpacked(part, row):
    lane = lane_of(part.shape)
    part = part if row == 0 else pltpu.roll(part, HALF_LANES, 1)
    return jnp.where(lane < HALF_LANES, part, 0.0)


def facts_of(facts, batch, second, row, places):
    at = jnp.where(second, facts[batch, row, 8] - 1 - places, places)
    segment = jnp.zeros(places.shape, jnp.int32)
    for k in range(SEGS):
        segment = segment + (at >= facts[batch, row, k]).astype(jnp.int32)
    label = jnp.zeros(places.shape, jnp.int32)
    for k in range(SEGS):
        label = jnp.where(segment == k, facts[batch, row, SEGS + k], label)
    return segment, label


def columns_of(facts, batch, second, rows, length):
    parts = []
    for row in range(rows):
        places = lax.broadcasted_iota(jnp.int32, (length, LANES), 0)
        segment, label = facts_of(facts, batch, second, row, places)
        before, _ = facts_of(facts, batch, second, row, places - 1)
        parts.append((segment, label, (places >= 1) & (segment == before)))
    return [
        jnp.concatenate([part[i].astype(jnp.int32) for part in parts], 0)[:, :1] for i in range(3)
    ]


def gain_rows_of(w_side, last, out, count):
    return w_side[:, last:].astype(jnp.float32).T[out : out + count]


def both_heads(pair, first):
    zero = jnp.zeros_like(pair)
    return jnp.concatenate([jnp.where(first, pair, zero), jnp.where(first, zero, pair)], 0)


def norm_rows_back(normed, inverse, grad_normed):
    mean_grad = jnp.mean(grad_normed, -1, keepdims=True)
    mean_proj = jnp.mean(grad_normed * normed, -1, keepdims=True)
    return inverse * (grad_normed - mean_grad - normed * mean_proj)


def by_rows(left, right):
    return lax.dot_general(
        left, right, (((1,), (1,)), ((), ())), preferred_element_type=jnp.float32
    )


def down_columns(left, right):
    return lax.dot_general(
        left, right, (((0,), (0,)), ((), ())), preferred_element_type=jnp.float32
    )


def blocks_kernel(
    sizes,
    facts,
    patches,
    cotangent,
    hbm_qkv,
    hbm_o,
    hbm_up,
    hbm_down,
    hbm_side,
    out_latent,
    out_grad,
    out_gains,
    hbm_na,
    hbm_aa,
    hbm_q,
    hbm_p,
    hbm_ctx,
    hbm_nm,
    hbm_am,
    hbm_slope,
    hbm_gelu,
    hbm_stat,
    hbm_nf,
    hbm_af,
    hbm_tail,
    hbm_start,
    hbm_gqkv,
    hbm_gmid,
    hbm_gup,
    hbm_gbr,
    hbm_gstart,
    hbm_gpred,
    w_qkv,
    w_o,
    w_up,
    w_down,
    w_side,
    na,
    aa,
    qkv,
    prob,
    ctx,
    nm,
    am,
    slope,
    gelu,
    stat,
    nf,
    af,
    tail,
    start,
    gqkv,
    gmid,
    gup,
    gbr,
    gstart,
    gpred,
    hidden,
    inputs,
    gain_rows,
    gact,
    gctx,
    sent,
    received,
    w_sem,
    save_sem,
    last_sem,
    load_sem,
    once_sem,
    grad_sem,
    end_sem,
    send_sem,
    recv_sem,
):
    rows, length, table, channels = sizes
    layers, width = w_qkv.shape[0], w_qkv.shape[1]
    pairs = width // LANES
    half = lax.axis_size("rows") // 2
    me = lax.axis_index("rows")
    second = me >= half
    partner = (jnp.where(second, me - half, me + half), lax.axis_index("seq"))
    barrier = pltpu.get_barrier_semaphore()
    pl.semaphore_signal(barrier, 1, device_id=partner, device_id_type=MESH_ID)

    def hop(slot):
        return pltpu.make_async_remote_copy(
            src_ref=sent.at[slot],
            dst_ref=received.at[slot],
            send_sem=send_sem.at[slot],
            recv_sem=recv_sem.at[slot],
            device_id=partner,
            device_id_type=MESH_ID,
        )

    loads = [(hbm_side.at[0], w_side, 0)]
    for layer in range(layers):
        for i, (src, dst) in enumerate(
            ((hbm_qkv, w_qkv), (hbm_o, w_o), (hbm_up, w_up), (hbm_down, w_down))
        ):
            loads.append((src.at[layer], dst.at[layer], 1 + 4 * layer + i))
    for src, dst, i in loads:
        pltpu.make_async_copy(src, dst, w_sem.at[i]).start()
    pl.semaphore_wait(barrier, 1)
    pltpu.make_async_copy(hbm_side.at[0], w_side, w_sem.at[0]).wait()
    gain_rows[...] = gain_rows_of(w_side, table + LANES, 2 * channels, 8)
    lane = lane_of((TOKENS, LANES))

    layered = (
        (na, hbm_na),
        (aa, hbm_aa),
        (qkv, hbm_q),
        (prob, hbm_p),
        (ctx, hbm_ctx),
        (nm, hbm_nm),
        (am, hbm_am),
        (slope, hbm_slope),
        (gelu, hbm_gelu),
        (stat, hbm_stat),
    )
    single = ((nf, hbm_nf), (af, hbm_af), (tail, hbm_tail), (start, hbm_start))

    @pl.loop(0, 3)
    def _(step):
        batch = jnp.where(second, jnp.maximum(step - 1, 0), jnp.minimum(step, 1))

        def saving(layer, i):
            src, dst = layered[i]
            src = src if i == 7 else src.at[layer]
            return pltpu.make_async_copy(src, dst.at[step, layer], save_sem.at[layer, i])

        def ready(layer, i, dst):
            @pl.when(step == 0)
            def _():
                view = dst.at[layer]
                pltpu.make_async_copy(view, view, w_sem.at[1 + 4 * layer + i]).wait()

        for slot in range(2):

            @pl.when(step == slot + 1)
            def _():
                hop(slot).wait_recv()

        for row in range(rows):
            toks = pl.ds(row * length, length)

            @pl.when(jnp.logical_not(second))
            def _():
                inputs[toks, :] = patches[batch, toks, :]

            @pl.when(second & (step > 0))
            def _():
                before = received[jnp.maximum(step - 1, 0)]
                inputs[toks, :] = turned_round(unpacked(before, row))

            @pl.when(second & (step == 0))
            def _():
                inputs[toks, :] = jnp.zeros((length, LANES), jnp.float32)

        seg_col, labels, same = columns_of(facts, batch, second, rows, length)
        start[:, :table] = (labels == lane_of((TOKENS, table))).astype(jnp.bfloat16)
        start[:, table:] = inputs[...].astype(jnp.bfloat16)
        hidden[...] = by_rows(start[...], w_side[:, : table + LANES])
        for layer in range(layers):
            normed, inverse_a = norm_rows(hidden[...])
            na[layer] = normed
            saving(layer, 0).start()
            aa[layer] = (normed * gain_rows[2 * layer : 2 * layer + 1, :]).astype(jnp.bfloat16)
            saving(layer, 1).start()
            ready(layer, 0, w_qkv)

            @pl.loop(0, 3)
            def _(i):
                cols = pl.ds(pl.multiple_of(i * width, LANES), width)
                qkv[layer, :, cols] = jnp.dot(
                    aa[layer], w_qkv[layer, :, cols], preferred_element_type=jnp.float32
                ).astype(jnp.bfloat16)

            saving(layer, 2).start()
            for row in range(rows):
                toks = pl.ds(row * length, length)
                causal = lax.broadcasted_iota(jnp.int32, (length, length), 0) >= lane_of(
                    (length, length)
                )
                places = lax.broadcasted_iota(jnp.int32, (8, length), 1)
                seg_row = facts_of(facts, batch, second, row, places)[0][:1]
                attend = (seg_col[row * length : (row + 1) * length] == seg_row) & causal
                attend = jnp.concatenate([attend.astype(jnp.float32)] * 2, 0) > 0.5
                first = lane_of((length, LANES)) < HALF_LANES
                for pair in range(pairs):

                    def part(i):
                        return qkv[layer, toks, pl.ds(i * width + pair * LANES, LANES)]

                    scores = by_rows(both_heads(part(0), first), part(1)) * HEAD_DIM ** (-0.5)
                    scores = jnp.where(attend, scores, MASKED)
                    expo = jnp.exp(scores - jnp.max(scores, -1, keepdims=True))
                    soft = expo / jnp.sum(expo, -1, keepdims=True)
                    prob[layer, row * pairs + pair] = soft
                    mixed = jnp.dot(
                        soft.astype(jnp.bfloat16), part(2), preferred_element_type=jnp.float32
                    )
                    ctx[layer, toks, pl.ds(pair * LANES, LANES)] = jnp.where(
                        first, mixed[:length], mixed[length:]
                    ).astype(jnp.bfloat16)

            saving(layer, 3).start()
            saving(layer, 4).start()
            ready(layer, 1, w_o)
            hidden[...] = hidden[...] + jnp.dot(
                ctx[layer], w_o[layer], preferred_element_type=jnp.float32
            )
            normed, inverse_m = norm_rows(hidden[...])
            nm[layer] = normed
            saving(layer, 5).start()
            am[layer] = (normed * gain_rows[2 * layer + 1 : 2 * layer + 2, :]).astype(jnp.bfloat16)
            saving(layer, 6).start()
            stat[layer] = jnp.where(lane == 0, inverse_a, inverse_m)
            saving(layer, 9).start()
            ready(layer, 2, w_up)
            if layer > 0:
                saving(layer - 1, 7).wait()

            @pl.loop(0, w_up.shape[2] // width)
            def _(i):
                cols = pl.ds(pl.multiple_of(i * width, LANES), width)
                upper = jnp.dot(am[layer], w_up[layer, :, cols], preferred_element_type=jnp.float32)
                value, rate = gelu_and_slope(upper)
                gelu[layer, :, cols] = value.astype(jnp.bfloat16)
                slope[:, cols] = rate

            saving(layer, 7).start()
            saving(layer, 8).start()
            ready(layer, 3, w_down)
            hidden[...] = hidden[...] + jnp.dot(
                gelu[layer], w_down[layer], preferred_element_type=jnp.float32
            )

        normed, inverse_f = norm_rows(hidden[...])
        nf[...] = normed
        af[...] = (normed * gain_rows[2 * layers : 2 * layers + 1, :]).astype(jnp.bfloat16)
        prediction = jnp.dot(
            af[...], w_side[:, table + LANES :], preferred_element_type=jnp.float32
        )
        previous = pltpu.roll(prediction, 1, 0)
        shown = (same > 0) & (lane < channels)
        shift_alpha = jnp.where(shown, pltpu.roll(previous, LANES - channels, 1), 0.0)
        shift_mu = jnp.where(shown, previous, 0.0)
        latent = (inputs[...] - shift_mu) * jnp.exp(-shift_alpha)
        logdet = -jnp.sum(shift_alpha, -1, keepdims=True)
        result = jnp.where(lane == channels, logdet + inputs[...], latent)
        out_latent[step] = result
        for slot in range(2):

            @pl.when(step == slot)
            def _():
                sent[slot] = packed_pair(result, length)
                hop(slot).start()

        tail[0] = latent
        tail[1] = shift_alpha
        tail[2] = jnp.broadcast_to(inverse_f, (TOKENS, LANES))
        for i, (src, dst) in enumerate(single):
            pltpu.make_async_copy(src, dst.at[step], last_sem.at[i]).start()
        for layer in range(layers):
            for i in range(len(layered)):
                if i != 7 or layer == layers - 1:
                    saving(layer, i).wait()
        for i, (src, dst) in enumerate(single):
            pltpu.make_async_copy(src, dst.at[step], last_sem.at[i]).wait()

    back = ((nm, hbm_nm), (prob, hbm_p), (qkv, hbm_q), (na, hbm_na), (stat, hbm_stat))
    once = ((tail, hbm_tail), (nf, hbm_nf))
    order = list(reversed(range(layers)))

    @pl.loop(0, 3)
    def _(turn):
        batch = jnp.where(second, jnp.maximum(1 - turn, 0), jnp.minimum(2 - turn, 1))
        slot_of = 2 - turn

        def fetch(layer, i, step):
            src, dst = back[i][1], back[i][0]
            return pltpu.make_async_copy(src.at[step, layer], dst.at[layer], load_sem.at[layer, i])

        def fetch_slope(layer, step):
            return pltpu.make_async_copy(hbm_slope.at[step, layer], slope, load_sem.at[layer, 5])

        def fetch_once(i, step):
            return pltpu.make_async_copy(once[i][1].at[step], once[i][0], once_sem.at[i])

        def refill(copy_of):
            @pl.when(turn < 2)
            def _():
                copy_of(jnp.maximum(slot_of - 1, 0)).start()

        def await_load(copy_of):
            @pl.when(turn > 0)
            def _():
                copy_of(slot_of).wait()

        def saving(layer, i):
            src, dst = ((gqkv, hbm_gqkv), (gmid, hbm_gmid), (gup, hbm_gup), (gbr, hbm_gbr))[i]
            src = src if i == 2 else src.at[layer]
            return pltpu.make_async_copy(src, dst.at[slot_of, layer], grad_sem.at[layer, i])

        for slot in (2, 3):

            @pl.when(turn == slot - 1)
            def _():
                hop(slot).wait_recv()

        for row in range(rows):
            toks = pl.ds(row * length, length)

            @pl.when(second)
            def _():
                inputs[toks, :] = cotangent[batch, toks, :]

            @pl.when(jnp.logical_not(second) & (turn > 0))
            def _():
                before = received[jnp.maximum(turn, 1) + 1]
                inputs[toks, :] = turned_round(unpacked(before, row))

            @pl.when(jnp.logical_not(second) & (turn == 0))
            def _():
                inputs[toks, :] = jnp.zeros((length, LANES), jnp.float32)

        same = columns_of(facts, batch, second, rows, length)[2]
        await_load(functools.partial(fetch_once, 0))
        await_load(functools.partial(fetch_once, 1))
        scaled = inputs[...] * jnp.exp(-tail[1])
        grad_alpha = 1.0 - inputs[...] * tail[0]
        grad_prev = jnp.where(lane < channels, -scaled, pltpu.roll(grad_alpha, channels, 1))
        grad_prev = jnp.where((same > 0) & (lane < 2 * channels), grad_prev, 0.0)
        gpred[...] = pltpu.roll(grad_prev, TOKENS - 1, 0).astype(jnp.bfloat16)
        gact[...] = by_rows(gpred[...], w_side[:, table + LANES :])
        out_gains[turn] = jnp.zeros((8, width), jnp.float32)

        def through_norm(normed, inverse, index):
            grad = gact[...]
            out_gains[turn, index : index + 1, :] = jnp.sum(grad * normed, 0, keepdims=True)
            return norm_rows_back(normed, inverse, grad * gain_rows[index : index + 1, :])

        hidden[...] = through_norm(nf[...], tail[2][:, :1], 2 * layers)
        refill(functools.partial(fetch_once, 0))
        refill(functools.partial(fetch_once, 1))
        for layer in order:
            gbr[layer] = hidden[...].astype(jnp.bfloat16)
            saving(layer, 3).start()
            if layer == order[0]:
                await_load(functools.partial(fetch_slope, layer))
            else:
                fetch_slope(layer, slot_of).wait()
                saving(layer + 1, 2).wait()

            @pl.loop(0, w_up.shape[2] // width)
            def _(i):
                cols = pl.ds(pl.multiple_of(i * width, LANES), width)
                gup[:, cols] = (
                    by_rows(gbr[layer], w_down[layer, cols, :]) * slope[:, cols]
                ).astype(jnp.bfloat16)

            saving(layer, 2).start()
            if layer > 0:
                fetch_slope(layer - 1, slot_of).start()
            else:
                refill(functools.partial(fetch_slope, order[0]))
            gact[...] = by_rows(gup[...], w_up[layer])
            await_load(functools.partial(fetch, layer, 0))
            await_load(functools.partial(fetch, layer, 4))
            hidden[...] = hidden[...] + through_norm(
                nm[layer], stat[layer][:, 1:2], 2 * layer + 1
            )
            refill(functools.partial(fetch, layer, 0))
            gmid[layer] = hidden[...].astype(jnp.bfloat16)
            saving(layer, 1).start()
            gctx[...] = by_rows(gmid[layer], w_o[layer]).astype(jnp.bfloat16)
            await_load(functools.partial(fetch, layer, 1))
            await_load(functools.partial(fetch, layer, 2))
            for row in range(rows):
                toks = pl.ds(row * length, length)
                first = lane_of((length, LANES)) < HALF_LANES
                for pair in range(pairs):

                    def at(i):
                        return pl.ds(i * width + pair * LANES, LANES)

                    query = both_heads(qkv[layer, toks, at(0)], first)
                    key = qkv[layer, toks, at(1)]
                    value = qkv[layer, toks, at(2)]
                    grad = both_heads(gctx[toks, at(0)], first)
                    soft = prob[layer, row * pairs + pair]
                    grad_soft = by_rows(grad, value)
                    delta = jnp.sum(soft * grad_soft, -1, keepdims=True)
                    grad_scores = (soft * (grad_soft - delta)).astype(jnp.bfloat16)
                    factor = HEAD_DIM ** (-0.5)
                    mixed = jnp.dot(grad_scores, key, preferred_element_type=jnp.float32) * factor
                    gqkv[layer, toks, at(0)] = jnp.where(
                        first, mixed[:length], mixed[length:]
                    ).astype(jnp.bfloat16)
                    gqkv[layer, toks, at(1)] = (
                        down_columns(grad_scores, query) * factor
                    ).astype(jnp.bfloat16)
                    gqkv[layer, toks, at(2)] = down_columns(
                        soft.astype(jnp.bfloat16), grad
                    ).astype(jnp.bfloat16)

            refill(functools.partial(fetch, layer, 1))
            refill(functools.partial(fetch, layer, 2))
            saving(layer, 0).start()
            gact[...] = by_rows(gqkv[layer], w_qkv[layer])
            await_load(functools.partial(fetch, layer, 3))
            hidden[...] = hidden[...] + through_norm(na[layer], stat[layer][:, :1], 2 * layer)
            refill(functools.partial(fetch, layer, 3))
            refill(functools.partial(fetch, layer, 4))
        gstart[...] = hidden[...].astype(jnp.bfloat16)
        grad_inputs = scaled + jnp.dot(
            gstart[...], w_side[:, table : table + LANES], preferred_element_type=jnp.float32
        )
        grad_inputs = jnp.where(lane < channels, grad_inputs, 0.0)
        out_grad[turn] = grad_inputs
        for slot in (2, 3):

            @pl.when(turn == slot - 2)
            def _():
                sent[slot] = packed_pair(grad_inputs, length)
                hop(slot).start()

        ends = ((gstart, hbm_gstart), (gpred, hbm_gpred))
        for i, (src, dst) in enumerate(ends):
            pltpu.make_async_copy(src, dst.at[slot_of], end_sem.at[i]).start()
        for layer in range(layers):
            for i in range(4):
                if i != 2 or layer == 0:
                    saving(layer, i).wait()
        for i, (src, dst) in enumerate(ends):
            pltpu.make_async_copy(src, dst.at[slot_of], end_sem.at[i]).wait()

    for slot in range(4):
        hop(slot).wait_send()


def two_blocks(facts, patches, cotangent, weights, table, channels, collective_id):
    w_qkv, w_o, w_up, w_down, side = weights
    rows = facts.shape[1]
    length = TOKENS // rows
    layers, width, hidden = w_up.shape
    pairs = rows * width // LANES
    low, full = jnp.bfloat16, jnp.float32
    kept = [
        ((layers, TOKENS, width), full),
        ((layers, TOKENS, width), low),
        ((layers, TOKENS, 3 * width), low),
        ((layers, pairs, 2 * length, length), full),
        ((layers, TOKENS, width), low),
        ((layers, TOKENS, width), full),
        ((layers, TOKENS, width), low),
        ((layers, TOKENS, hidden), full),
        ((layers, TOKENS, hidden), low),
        ((layers, TOKENS, LANES), full),
        ((TOKENS, width), full),
        ((TOKENS, width), low),
        ((3, TOKENS, LANES), full),
        ((TOKENS, table + LANES), low),
        ((layers, TOKENS, 3 * width), low),
        ((layers, TOKENS, width), low),
        ((layers, TOKENS, hidden), low),
        ((layers, TOKENS, width), low),
        ((TOKENS, width), low),
        ((TOKENS, LANES), low),
    ]
    scratch = [pltpu.VMEM(w.shape, low) for w in weights[:4]] + [pltpu.VMEM(side.shape[1:], low)]
    for i, (shape, kind) in enumerate(kept):
        scratch.append(pltpu.VMEM(shape[1:] if i in (7, 16) else shape, kind))
    dma = pltpu.SemaphoreType.DMA
    scratch += [
        pltpu.VMEM((TOKENS, width), full),
        pltpu.VMEM((TOKENS, LANES), full),
        pltpu.VMEM((8, width), full),
        pltpu.VMEM((TOKENS, width), full),
        pltpu.VMEM((TOKENS, width), low),
        pltpu.VMEM((4, length, LANES), full),
        pltpu.VMEM((4, length, LANES), full),
        dma((1 + 4 * layers,)),
        dma((layers, 10)),
        dma((4,)),
        dma((layers, 6)),
        dma((2,)),
        dma((layers, 4)),
        dma((2,)),
        dma((4,)),
        dma((4,)),
    ]
    vmem, hbm = pl.BlockSpec(memory_space=pltpu.VMEM), pl.BlockSpec(memory_space=pl.ANY)
    smem = pl.BlockSpec(memory_space=pltpu.SMEM)
    results = pl.pallas_call(
        functools.partial(blocks_kernel, (rows, length, table, channels)),
        out_shape=[jax.ShapeDtypeStruct((3, TOKENS, LANES), full)] * 2
        + [jax.ShapeDtypeStruct((3, 8, width), full)]
        + [jax.ShapeDtypeStruct((3,) + shape, kind) for shape, kind in kept],
        in_specs=[smem] + [vmem] * 2 + [hbm] * 5,
        out_specs=[vmem] * 3 + [hbm] * len(kept),
        scratch_shapes=scratch,
        compiler_params=pltpu.CompilerParams(
            collective_id=collective_id, has_side_effects=True, vmem_limit_bytes=61 * 2**20
        ),
        name="two_blocks",
    )(facts, patches, cotangent, w_qkv, w_o, w_up, w_down, side)
    _, aa, _, _, ctx, _, am, _, gelu, _, _, af, _, start = results[3:17]
    gqkv, gmid, gup, gbr, gstart, gpred = results[17:]
    pairs = (aa, gqkv, ctx, gmid, am, gup, gelu, gbr, start, gstart, af, gpred)
    return results[:3], pairs


def products_kernel(units, n_pairs, out_count, *refs):
    per = 2 * n_pairs
    steps, gain_grads = refs[:per], refs[per]
    outs = refs[per + 1 : per + 6]
    rest = refs[per + 6 :]
    bufs, made, turned = rest[:per], rest[per : per + 5], rest[per + 5]
    rest = rest[per + 6 :]
    n = len(units)
    acc, in_x, in_y, in_d, in_z = [rest[i * n : (i + 1) * n] for i in range(5)]
    gain_cols, in_sem, send, recv, local_out = rest[5 * n :]
    r, x, y, z, c = place()
    stage = z // 2
    other = 1 - stage
    zi = lax.rem(z, 2)
    dev_x = (r, 1 - x)
    dev_y = (r + 2 - 4 * y, x)
    dev_s = (r + 1 - 2 * c, x)
    z_dst = (z + 1 - 2 * zi, other * 2, other * 2 + 1)
    dev_z = tuple((zz * 4 + y * 2 + c, x) for zz in z_dst)
    barrier = pltpu.get_barrier_semaphore()
    partners = (dev_x, dev_y, dev_s) + dev_z
    for dev in partners:
        pl.semaphore_signal(barrier, 1, device_id=dev, device_id_type=MESH_ID)

    def loads(i, layer):
        copies = []
        for k, step in enumerate((1, 2 * stage)):
            src = steps[i].at[step, layer] if len(steps[i].shape) == 4 else steps[i].at[step]
            dst = bufs[i].at[pl.ds(k * TOKENS, TOKENS)]
            copies.append(pltpu.make_async_copy(src, dst, in_sem.at[layer, 2 * i + k]))
        return copies

    def fetch(i, layer):
        for copy in loads(i, layer):
            copy.start()

    def fetched(i, layer):
        for copy in loads(i, layer):
            copy.wait()

    for i in (8, 9, 10, 11):
        fetch(i, 0)
    for i in range(8):
        fetch(i, 0)
    pl.semaphore_wait(barrier, len(partners))
    started = {}

    def push(u, src, dst, slot, dev, idx=None):
        cp = pltpu.make_async_remote_copy(
            src_ref=src,
            dst_ref=dst,
            send_sem=send.at[u, slot],
            recv_sem=recv.at[u, slot if idx is None else idx],
            device_id=dev,
            device_id_type=MESH_ID,
        )
        cp.start()
        started[u, slot] = cp

    def arrived(u, dst, idx):
        wait_all_of(dst, recv.at[u, idx])

    def part_of(u, part):
        _, _, _, rows, half, (dim, cut) = units[u]
        if dim == 0:
            return (pl.ds(0, cut), pl.ds(0, half)) if part == 0 else (pl.ds(cut, rows - cut), pl.ds(0, half))
        return (pl.ds(0, rows), pl.ds(0, cut)) if part == 0 else (pl.ds(0, rows), pl.ds(cut, half - cut))

    block, strip = turned.shape[0], 3 * LANES

    def multiply(out, rows, right, m, begin, count, wide, extra=None):
        def one(cols, out_cols):
            product = jnp.dot(turned[...], right[:, cols], preferred_element_type=jnp.float32)
            if extra is not None:
                product = product + extra[...]
            product = product.astype(jnp.bfloat16)
            for k in range(block // rows):
                s = m * (block // rows) + k
                out[s // 4, (s // 2) % 2, s % 2, :, out_cols] = product[k * rows : (k + 1) * rows]

        if count == 1:
            one(slice(0, wide), slice(begin, begin + wide))
        else:

            @pl.loop(0, count)
            def _(i):
                cols = pl.ds(pl.multiple_of(i * wide, LANES), wide)
                one(cols, cols)

    def product(u):
        a, layer, _, rows, half, _ = units[u]
        if a == 4:
            for i in (8, 9, 10, 11):
                fetched(i, 0)
            turned[...] = bufs[9][...].T
            multiply(made[4], rows, bufs[8], 0, 0, bufs[8].shape[1] // strip, strip)
            turned[...] = bufs[10][...].T
            gains = gain_grads[1] + gain_grads[2 - 2 * stage]
            zeros = jnp.zeros((LANES, gains.shape[1]), jnp.float32)
            tall = jnp.concatenate([zeros[:out_count], gains, zeros[out_count + 8 :]], 0)
            gain_cols[...] = tall.T
            multiply(made[4], rows, bufs[11], 0, bufs[8].shape[1], 1, LANES, gain_cols)
        else:
            fetched(2 * a, layer)
            fetched(2 * a + 1, layer)
            if layer > 0:
                for h in range(2):
                    started.pop((u - 4, h)).wait_send()
            for m in range(bufs[2 * a].shape[1] // block):
                turned[...] = bufs[2 * a][:, m * block : (m + 1) * block].T
                multiply(made[a], rows, bufs[2 * a + 1], m, 0, 2 * half // strip, strip)
            if layer + 1 < units[-1][1] + 1:
                fetch(2 * a, layer + 1)
                fetch(2 * a + 1, layer + 1)
        for h in range(2):
            cols = pl.ds(h * half, half)
            push(u, made[a].at[:, :, 1 - c, :, cols], acc[u].at[:, :, h], h, dev_s)

    def chip_sum(u):
        a, layer, _, rows, half, _ = units[u]
        for h in range(2):
            arrived(u, acc[u].at[:, :, h], h)

        @pl.loop(0, 4)
        def _(zz):
            for yy in range(2):
                for h in range(2):
                    mine = made[a][zz, yy, c, :, h * half : (h + 1) * half]
                    acc[u][zz, yy, h] = acc[u][zz, yy, h] + mine

        for part, dev in ((0, dev_y), (1, dev_x)):
            rs, cs = part_of(u, part)
            push(u, acc[u].at[:, 1 - y, 1 - x, rs, cs], in_d[u].at[:, rs, cs], 2 + part, dev)

    def side_sum(u):
        for part, yy, h, dev, into in ((0, y, 1 - x, dev_x, in_x), (1, 1 - y, x, dev_y, in_y)):
            rs, cs = part_of(u, part)
            arrived(u, in_d[u].at[:, rs, cs], 2 + part)

            @pl.loop(0, 4)
            def _(zz):
                acc[u][zz, yy, h, rs, cs] = acc[u][zz, yy, h, rs, cs] + in_d[u][zz, rs, cs]

            push(u, acc[u].at[:, yy, h], into[u], 4 + part, dev)

    def plane_sum(u):
        arrived(u, in_x[u], 4)
        arrived(u, in_y[u], 5)

        @pl.loop(0, 4)
        def _(zz):
            acc[u][zz, y, x] = (
                acc[u][zz, y, x].astype(jnp.float32)
                + in_x[u][zz].astype(jnp.float32)
                + in_y[u][zz].astype(jnp.float32)
            ).astype(jnp.bfloat16)

        for i in range(2):
            push(u, acc[u].at[z_dst[1 + i], y, x], in_z[u].at[1 + zi], 7 + i, dev_z[1 + i], idx=7 + zi)
        push(u, acc[u].at[z_dst[0], y, x], in_z[u].at[0], 6, dev_z[0])

    def owned(u, b, h):
        a, layer, layers, _, half, _ = units[u]
        return outs[a].at[layers * b + layer, :, pl.ds(pl.multiple_of(h * half, LANES), half)]

    def totals(u):
        return ((acc[u].at[z, y, x], stage), (in_z[u].at[1], other))

    def total(u):
        for j in range(3):
            arrived(u, in_z[u].at[j], 6 + j)
        acc[u][z, y, x] = acc[u][z, y, x] + in_z[u][0]
        in_z[u][1] = in_z[u][1] + in_z[u][2]
        for k, (src, b) in enumerate(totals(u)):
            push(u, src, owned(u, b, x), 9 + k, dev_x)
            pltpu.make_async_copy(src, owned(u, b, x), local_out.at[u, k]).start()

    lags = (0, 1, 3, 5, 7)
    for t in range(n + lags[-1]):
        for lag, part in zip(lags, (product, chip_sum, side_sum, plane_sum, total)):
            if 0 <= t - lag < n:
                part(t - lag)
    for u in range(n):
        for k, (src, b) in enumerate(totals(u)):
            arrived(u, owned(u, b, 1 - x), 9 + k)
            pltpu.make_async_copy(src, owned(u, b, x), local_out.at[u, k]).wait()
    for cp in started.values():
        cp.wait_send()


def summed_products(operands, gain_grads, out_count, shards, collective_id):
    low = jnp.bfloat16
    out = [jax.ShapeDtypeStruct(s.shape, low) for s in shards]
    units = units_of(out, 0.75)
    n = len(units)
    layers = max(u[1] for u in units) + 1
    n_pairs = len(operands) // 2
    width = operands[0].shape[-1]
    hbm, vmem = pl.BlockSpec(memory_space=pl.ANY), pl.BlockSpec(memory_space=pltpu.VMEM)

    def slots(lead):
        return [pltpu.VMEM(lead + (u[3], u[4]), low) for u in units]

    return pl.pallas_call(
        functools.partial(products_kernel, units, n_pairs, out_count),
        out_shape=out,
        in_specs=[hbm] * (2 * n_pairs) + [vmem],
        out_specs=[hbm] * 5,
        scratch_shapes=[
            pltpu.VMEM((2 * TOKENS, part.shape[-1]), low) for part in operands
        ]
        + [pltpu.VMEM((4, 2, 2) + s.shape[1:], low) for s in shards]
        + [pltpu.VMEM((width, 2 * TOKENS), low)]
        + slots((4, 2, 2))
        + slots((4,))
        + slots((4,))
        + slots((4,))
        + slots((3,))
        + [
            pltpu.VMEM((width, LANES), jnp.float32),
            pltpu.SemaphoreType.DMA((layers, 4 * n_pairs)),
            pltpu.SemaphoreType.DMA((n, 11)),
            pltpu.SemaphoreType.DMA((n, 11)),
            pltpu.SemaphoreType.DMA((n, 2)),
        ],
        compiler_params=pltpu.CompilerParams(
            collective_id=collective_id, has_side_effects=True, vmem_limit_bytes=62 * 2**20
        ),
        name="summed_products",
    )(*operands, gain_grads)


def dot(left, right, dims=((1,), (0,))):
    return lax.dot_general(left, right, (dims, ((), ())), preferred_element_type=jnp.float32)


def normalize(hidden):
    center = hidden - jnp.mean(hidden, -1, keepdims=True)
    inverse = lax.rsqrt(jnp.mean(center * center, -1, keepdims=True) + EPS_NORM)
    return (center * inverse, inverse)


def normalize_back(normed, inverse, grad_normed):
    mean_grad = jnp.mean(grad_normed, -1, keepdims=True)
    mean_proj = jnp.mean(grad_normed * normed, -1, keepdims=True)
    return inverse * (grad_normed - mean_grad - normed * mean_proj)


def padded(count, unit):
    return -(-count // unit) * unit


def side_columns(classes, channels, out, gains):
    table = padded(classes, LANES)
    last = table + padded(channels, LANES)
    return table, last, padded(last + out + gains, 2 * LANES)


def pack_side(w_table, w_in, w_out, gains):
    blocks, classes, shard = w_table.shape
    channels, out, gain_count = w_in.shape[1], w_out.shape[2], gains.shape[1]
    table, last, total = side_columns(classes, channels, out, gain_count)

    def gap(count):
        return jnp.zeros((blocks, shard, count), w_table.dtype)

    return jnp.concatenate(
        [
            jnp.swapaxes(w_table, 1, 2),
            gap(table - classes),
            jnp.swapaxes(w_in, 1, 2),
            gap(last - table - channels),
            w_out,
            jnp.swapaxes(gains, 1, 2),
            gap(total - last - out - gain_count),
        ],
        2,
    )


def split_side(side, classes, channels, out, gains):
    table, last, _ = side_columns(classes, channels, out, gains)
    return (
        jnp.swapaxes(side[..., :classes], -1, -2),
        jnp.swapaxes(side[..., table : table + channels], -1, -2),
        side[..., last : last + out],
        jnp.swapaxes(side[..., last + out : last + out + gains], -1, -2),
    )


def heads_of(flat, rows):
    return flat.reshape(rows, -1, HEADS, HEAD_DIM)


def attention_scores(query, key_rows, attend):
    scores = jnp.einsum(
        "rqhd,rkhd->rhqk", query, key_rows, preferred_element_type=jnp.float32
    ) * HEAD_DIM ** (-0.5)
    return jnp.where(attend[:, None], scores, MASKED)


def forward_block(inputs, seg_ids, labels, weights, sizes):
    w_qkv, w_o, w_up, w_down, side = weights
    classes, channels, out, gain_count = sizes
    table, last, _ = side_columns(*sizes)
    rows, length, _ = inputs.shape
    tokens = rows * length
    width = side.shape[0]
    places = jnp.arange(length, dtype=jnp.int32)
    attend = (seg_ids[:, :, None] == seg_ids[:, None, :]) & (
        places[None, :, None] >= places[None, None, :]
    )
    same_seg = jnp.concatenate(
        [jnp.zeros((rows, 1), bool), seg_ids[:, 1:] == seg_ids[:, :-1]], 1
    )[..., None]
    onehot = labels.reshape(tokens, 1) == jnp.arange(table)[None, :]
    start = jnp.concatenate(
        [
            onehot.astype(jnp.bfloat16),
            inputs.reshape(tokens, channels).astype(jnp.bfloat16),
            jnp.zeros((tokens, last - table - channels), jnp.bfloat16),
        ],
        1,
    )
    gain_rows = side[:, last + out : last + out + gain_count].astype(jnp.float32).T
    hidden = dot(start, side[:, :last], ((1,), (1,)))
    kept = []
    for layer in range(w_qkv.shape[0]):
        normed_a, inverse_a = normalize(hidden)
        act_a = (normed_a * gain_rows[2 * layer]).astype(jnp.bfloat16)
        qkv = dot(act_a, w_qkv[layer]).astype(jnp.bfloat16)
        query, key_rows, value_rows = [
            heads_of(qkv[:, i * width : (i + 1) * width], rows) for i in range(3)
        ]
        scores = attention_scores(query, key_rows, attend)
        row_top = jnp.max(scores, -1, keepdims=True)
        expo_rows = jnp.exp(scores - row_top)
        row_total = jnp.sum(expo_rows, -1, keepdims=True)
        soft_low = (expo_rows / row_total).astype(jnp.bfloat16)
        log_total = row_top + jnp.log(row_total)
        context = jnp.einsum(
            "rhqk,rkhd->rqhd", soft_low, value_rows, preferred_element_type=jnp.float32
        )
        context = context.reshape(tokens, width).astype(jnp.bfloat16)
        middle = hidden + dot(context, w_o[layer])
        normed_m, inverse_m = normalize(middle)
        act_m = (normed_m * gain_rows[2 * layer + 1]).astype(jnp.bfloat16)
        upper = dot(act_m, w_up[layer])
        gelu_low = jax.nn.gelu(upper, approximate=True).astype(jnp.bfloat16)
        hidden = middle + dot(gelu_low, w_down[layer])
        kept.append(
            (
                normed_a,
                inverse_a,
                act_a,
                qkv,
                log_total,
                context,
                normed_m,
                inverse_m,
                act_m,
                upper,
                gelu_low,
            )
        )
    normed_f, inverse_f = normalize(hidden)
    act_f = (normed_f * gain_rows[gain_count - 1]).astype(jnp.bfloat16)
    prediction = dot(act_f, side[:, last : last + out]).reshape(rows, length, out)
    previous = jnp.concatenate([jnp.zeros((rows, 1, out), jnp.float32), prediction[:, :-1]], 1)
    shift = jnp.where(same_seg, previous, 0.0)
    shift_alpha = shift[..., channels:]
    latent = (inputs - shift[..., :channels]) * jnp.exp(-shift_alpha)
    saved = (attend, same_seg, start, kept, normed_f, inverse_f, act_f, shift_alpha, latent)
    return (latent, -jnp.sum(shift_alpha, -1), saved)


def backward_block(grad_latent, saved, weights, sizes):
    w_qkv, w_o, w_up, w_down, side = weights
    classes, channels, out, gain_count = sizes
    table, last, _ = side_columns(*sizes)
    attend, same_seg, start, kept, normed_f, inverse_f, act_f, shift_alpha, latent = saved
    rows, length, _ = latent.shape
    tokens = rows * length
    width = side.shape[0]
    factor = HEAD_DIM ** (-0.5)
    gain_rows = side[:, last + out : last + out + gain_count].astype(jnp.float32).T
    scale_back = jnp.exp(-shift_alpha)
    grad_inputs = grad_latent * scale_back
    grad_prev = jnp.where(
        same_seg, jnp.concatenate([-grad_inputs, 1.0 - grad_latent * latent], 2), 0.0
    )
    grad_pred = jnp.concatenate([grad_prev[:, 1:], jnp.zeros((rows, 1, out), jnp.float32)], 1)
    grad_pred = grad_pred.reshape(tokens, out).astype(jnp.bfloat16)
    grad_act = dot(grad_pred, side[:, last : last + out], ((1,), (1,)))
    gain_grads = [None] * gain_count
    gain_grads[-1] = jnp.sum(grad_act * normed_f, 0)
    grad_hidden = normalize_back(normed_f, inverse_f, grad_act * gain_rows[gain_count - 1])
    pairs = [None] * w_qkv.shape[0]
    for layer in reversed(range(w_qkv.shape[0])):
        (
            normed_a,
            inverse_a,
            act_a,
            qkv,
            log_total,
            context,
            normed_m,
            inverse_m,
            act_m,
            upper,
            gelu_low,
        ) = kept[layer]
        grad_branch = grad_hidden.astype(jnp.bfloat16)
        grad_gelu = dot(grad_branch, w_down[layer], ((1,), (1,)))
        gelu_pull = jax.vjp(partial(jax.nn.gelu, approximate=True), upper)[1]
        grad_upper = gelu_pull(grad_gelu)[0].astype(jnp.bfloat16)
        grad_act_m = dot(grad_upper, w_up[layer], ((1,), (1,)))
        gain_grads[2 * layer + 1] = jnp.sum(grad_act_m * normed_m, 0)
        grad_middle = grad_hidden + normalize_back(
            normed_m, inverse_m, grad_act_m * gain_rows[2 * layer + 1]
        )
        grad_mid_low = grad_middle.astype(jnp.bfloat16)
        grad_context = heads_of(
            dot(grad_mid_low, w_o[layer], ((1,), (1,))).astype(jnp.bfloat16), rows
        )
        query, key_rows, value_rows = [
            heads_of(qkv[:, i * width : (i + 1) * width], rows) for i in range(3)
        ]
        soft_rows = jnp.exp(attention_scores(query, key_rows, attend) - log_total)
        soft_low = soft_rows.astype(jnp.bfloat16)
        grad_soft = jnp.einsum(
            "rqhd,rkhd->rhqk", grad_context, value_rows, preferred_element_type=jnp.float32
        )
        row_delta = jnp.sum(soft_rows * grad_soft, -1, keepdims=True)
        grad_scores = (soft_rows * (grad_soft - row_delta)).astype(jnp.bfloat16)
        grad_query = factor * jnp.einsum(
            "rhqk,rkhd->rqhd", grad_scores, key_rows, preferred_element_type=jnp.float32
        )
        grad_keys = factor * jnp.einsum(
            "rhqk,rqhd->rkhd", grad_scores, query, preferred_element_type=jnp.float32
        )
        grad_values = jnp.einsum(
            "rhqk,rqhd->rkhd", soft_low, grad_context, preferred_element_type=jnp.float32
        )
        grad_qkv = jnp.concatenate(
            [part.reshape(tokens, width) for part in (grad_query, grad_keys, grad_values)], 1
        ).astype(jnp.bfloat16)
        grad_act_a = dot(grad_qkv, w_qkv[layer], ((1,), (1,)))
        gain_grads[2 * layer] = jnp.sum(grad_act_a * normed_a, 0)
        grad_hidden = grad_middle + normalize_back(
            normed_a, inverse_a, grad_act_a * gain_rows[2 * layer]
        )
        pairs[layer] = (
            (act_a, grad_qkv),
            (context, grad_mid_low),
            (act_m, grad_upper),
            (gelu_low, grad_branch),
        )
    grad_start = grad_hidden.astype(jnp.bfloat16)
    grad_inputs = grad_inputs + dot(grad_start, side[:, table : table + channels]).reshape(
        rows, length, channels
    )
    return grad_inputs, (
        pairs,
        (start, grad_start),
        (act_f, grad_pred),
        jnp.stack(gain_grads, 1),
    )


def weight_grads(parts, side_total):
    pairs, (start, grad_start), (act_f, grad_pred), gain_grads = parts
    arrays = [
        jnp.stack([dot(*layer[i], ((0,), (0,))).astype(jnp.bfloat16) for layer in pairs], 0)
        for i in range(4)
    ]
    side = [
        dot(grad_start, start, ((0,), (0,))),
        dot(act_f, grad_pred, ((0,), (0,))),
        gain_grads,
    ]
    count = sum(part.shape[1] for part in side)
    side.append(jnp.zeros((gain_grads.shape[0], side_total - count), jnp.float32))
    side = jnp.concatenate(side, 1).astype(jnp.bfloat16)
    return arrays + [side[None]]


def adam_step(weight, first, second, grad, rate):
    first_new = BETA_ONE * first + (1.0 - BETA_ONE) * grad
    second_new = BETA_TWO * second + (1.0 - BETA_TWO) * grad * grad
    first_hat = first_new / (1.0 - BETA_ONE**STEP)
    second_hat = second_new / (1.0 - BETA_TWO**STEP)
    weight_new = weight - rate * (first_hat / (jnp.sqrt(second_hat) + EPS_ADAM) + DECAY * weight)
    return (first_new, second_new, weight_new)


def segment_of(places, seg_ends):
    return jnp.sum((places[None, :, None] >= seg_ends[:, None, :]).astype(jnp.int32), -1)


def row_facts(seg_lengths, class_labels, length):
    seg_ids = segment_of(jnp.arange(length, dtype=jnp.int32), jnp.cumsum(seg_lengths, 1))
    picked = seg_ids[:, :, None] == jnp.arange(SEGS)[None, None, :]
    return seg_ids, jnp.sum(jnp.where(picked, class_labels[:, None, :], 0), -1)


def pack_kernel(sizes, w_table, w_in, w_out, gains, side):
    classes, channels, out, gain_count = sizes
    table, last, _ = side_columns(*sizes)
    shard = w_out.shape[1]
    down = lax.broadcasted_iota(jnp.int32, (shard, shard), 0)
    same = (down == lane_of((shard, shard))).astype(jnp.bfloat16)
    side[...] = jnp.zeros_like(side)
    for b in range(2):

        def across(part):
            return by_rows(same, part.astype(jnp.bfloat16)).astype(jnp.bfloat16)

        side[b, :, :classes] = w_table[b].astype(jnp.bfloat16)
        side[b, :, table : table + channels] = across(w_in[b])
        side[b, :, last : last + out] = w_out[b].astype(jnp.bfloat16)
        side[b, :, last + out : last + out + gain_count] = across(gains[:, b])


def packed_side(w_table, w_in, w_out, gains, sizes):
    shape = (2, w_out.shape[1], side_columns(*sizes)[2])
    return pl.pallas_call(
        functools.partial(pack_kernel, sizes),
        out_shape=jax.ShapeDtypeStruct(shape, jnp.bfloat16),
        compiler_params=pltpu.CompilerParams(vmem_limit_bytes=32 * 2**20),
        name="pack_side",
    )(jnp.swapaxes(w_table, 1, 2), w_in, w_out, jnp.swapaxes(gains, 0, 1))


def small_updates_kernel(sizes, side, *refs):
    classes, channels, out, gain_count = sizes
    table, last, _ = side_columns(*sizes)
    args, outs = refs[:12], refs[12:]
    shard = side.shape[1]
    down = lax.broadcasted_iota(jnp.int32, (shard, shard), 0)
    same = (down == lane_of((shard, shard))).astype(jnp.bfloat16)
    for b in range(2):

        def across(begin, end):
            return down_columns(side[b, :, begin:end], same)

        tail = across(last, last + LANES)
        grads = (
            across(table, table + LANES)[:channels],
            side[b, :, :classes].astype(jnp.float32),
            side[b, :, last : last + LANES].astype(jnp.float32)[:, :out],
            tail[out : out + gain_count],
        )
        rates = (RATES[0], RATES[1], RATES[6], RATES[7])
        for i in range(4):
            at = (slice(None), b) if i == 3 else (b,)
            now = [ref[at] for ref in args[3 * i : 3 * i + 3]]
            for ref, value in zip(outs[3 * i : 3 * i + 3], adam_step(*now, grads[i], rates[i])):
                ref[at] = value


def small_updates(side, groups, sizes):
    turns = ((0, 0), (1, 2), (0, 0), (0, 1))
    arrays = [jnp.swapaxes(part, *turn) for turn, group in zip(turns, groups) for part in group]
    results = pl.pallas_call(
        functools.partial(small_updates_kernel, sizes),
        out_shape=[jax.ShapeDtypeStruct(part.shape, part.dtype) for part in arrays],
        compiler_params=pltpu.CompilerParams(vmem_limit_bytes=48 * 2**20),
        name="small_updates",
    )(side, *arrays)
    return [jnp.swapaxes(part, *turns[i // 3]) for i, part in enumerate(results)]


def staged(patches, seg_lengths, class_labels, cotangent, low, sizes):
    half = lax.axis_size("rows") // 2
    second = lax.axis_index("rows") >= half
    x = lax.axis_index("seq")
    swap = [(i, (i + half) % (2 * half)) for i in range(2 * half)]
    beside = [(0, 1), (1, 0)]
    both = ("rows", "seq")
    across = [(2 * i + s, 2 * j + 1 - s) for i, j in swap for s in range(2)]
    classes, channels, out, gain_count = sizes
    table, last, _ = side_columns(*sizes)
    held, group, _ = patches.shape
    rows, length = held // 2, 2 * group

    pieces = jnp.concatenate([patches.astype(jnp.float32), cotangent], 2)
    pieces = jnp.pad(pieces, ((0, 0), (0, 0), (0, LANES - 2 * channels)))
    pieces = pieces.reshape(2, rows, group, LANES)
    keep = lax.dynamic_index_in_dim(pieces, x, 0, keepdims=False)
    give = lax.dynamic_index_in_dim(pieces, 1 - x, 0, keepdims=False)
    got = lax.ppermute(give, "seq", beside)
    mine = jnp.where(
        x == 0, jnp.concatenate([keep, got], 1), jnp.concatenate([got, keep], 1)
    ).reshape(TOKENS, LANES)
    theirs = lax.ppermute(mine, "rows", swap)
    facts = jnp.concatenate(
        [jnp.cumsum(seg_lengths, 1), class_labels, jnp.full((held, 1), length, jnp.int32)], 1
    )
    facts = lax.dynamic_slice_in_dim(facts, x * rows, rows, 0)
    their_facts = lax.ppermute(facts, "rows", swap)
    facts = jnp.where(
        second, jnp.stack([their_facts, facts], 0), jnp.stack([facts, their_facts], 0)
    )
    batches = jnp.where(second, jnp.stack([theirs, mine], 0), jnp.stack([mine, theirs], 0))
    batches, facts, low = lax.optimization_barrier((batches, facts, low))
    weights = gather_blocks(low, 1)
    lane = jnp.arange(LANES) < channels
    inputs = jnp.where(lane, batches, 0.0)
    cotangent = jnp.where(lane, jnp.roll(batches, -channels, 2), 0.0)
    (latents, grad_inputs, gain_grads), pairs = two_blocks(
        facts, inputs, cotangent, weights, table, channels, 3
    )

    def halves(part):
        part = part.reshape(rows, 2, group, LANES)
        ours = lax.dynamic_index_in_dim(part, x, 1, keepdims=False)
        return ours, lax.dynamic_index_in_dim(part, 1 - x, 1, keepdims=False)

    def in_order(ours, beside_us):
        return jnp.where(
            x == 0, jnp.concatenate([ours, beside_us], 0), jnp.concatenate([beside_us, ours], 0)
        )

    own = halves(jnp.where(second, latents[2], grad_inputs[2]))
    away = halves(jnp.where(second, latents[1], grad_inputs[1]))
    own_side = lax.ppermute(own[1], "seq", beside)
    away_here = lax.ppermute(away[0], "rows", swap)
    away_side = lax.ppermute(away[1], both, across)
    sums = summed_products(pairs, gain_grads, out, low, 2)
    ours, others = in_order(own[0], own_side), in_order(away_here, away_side)
    outcome = jnp.where(second, ours, others)
    patch_grad = jnp.where(second, others, ours)
    return outcome[..., :channels], outcome[..., channels], patch_grad[..., :channels], sums


def unstaged(mine, low, sizes):
    inputs, cotangent, seg_ids, labels = mine
    whole = [lax.all_gather(part, "rows", axis=1, tiled=True) for part in low]

    def block(index):
        picked = [part[index * LAYERS : (index + 1) * LAYERS] for part in whole[:4]]
        return picked + [whole[4][index]]

    back = seg_ids[:, ::-1], labels[:, ::-1]
    latent_one, det_one, saved_one = forward_block(inputs, seg_ids, labels, block(0), sizes)
    latent_two, det_two, saved_two = forward_block(latent_one[:, ::-1], *back, block(1), sizes)
    outcome = jnp.concatenate([latent_two, (det_two + det_one[:, ::-1])[..., None]], 2)
    grad_mid, parts_two = backward_block(cotangent, saved_two, block(1), sizes)
    patch_grad, parts_one = backward_block(grad_mid[:, ::-1], saved_one, block(0), sizes)
    grads = [
        jnp.concatenate(pair, 0)
        for pair in zip(
            weight_grads(parts_one, low[4].shape[2]), weight_grads(parts_two, low[4].shape[2])
        )
    ]
    sums = [
        lax.psum(
            lax.psum_scatter(grad, "rows", scatter_dimension=1, tiled=True).astype(jnp.float32),
            "seq",
        )
        for grad in grads
    ]
    return outcome, patch_grad, sums


def body(
    patches,
    seg_lengths,
    class_labels,
    cotangent,
    w_in,
    m_in,
    v_in,
    w_table,
    m_table,
    v_table,
    w_qkv,
    m_qkv,
    v_qkv,
    w_o,
    m_o,
    v_o,
    w_up,
    m_up,
    v_up,
    w_down,
    m_down,
    v_down,
    w_out,
    m_out,
    v_out,
    gains,
    m_gains,
    v_gains,
):
    masters = (w_in, w_table, w_qkv, w_o, w_up, w_down, w_out, gains)
    firsts = (m_in, m_table, m_qkv, m_o, m_up, m_down, m_out, m_gains)
    seconds = (v_in, v_table, v_qkv, v_o, v_up, v_down, v_out, v_gains)
    sizes = (w_table.shape[1], w_in.shape[1], w_out.shape[2], gains.shape[1])
    shards = [weight.astype(jnp.bfloat16) for weight in masters[2:6]]
    held, group, channels = patches.shape
    seq_count = lax.axis_size("seq")
    length = group * seq_count
    groups = list(zip(masters, firsts, seconds))
    fits = held == 4 and group * held == TOKENS and sizes[2] == 2 * channels and sizes[2] % 8 == 0
    if seq_count == 2 and lax.axis_size("rows") == 16 and fits:
        shards.append(packed_side(w_table, w_in, w_out, gains, sizes))
        latents, logdet, patch_grad, sums = staged(
            patches, seg_lengths, class_labels, cotangent, shards, sizes
        )
        small = small_updates(sums[4], [groups[i] for i in (0, 1, 6, 7)], sizes)
        updates = [None] * 8
        for i, where_at in enumerate((0, 1, 6, 7)):
            updates[where_at] = small[3 * i : 3 * i + 3]
        for i, where_at in enumerate((2, 3, 4, 5)):
            updates[where_at] = adam_step(
                *groups[where_at], sums[i].astype(jnp.float32), RATES[where_at]
            )
        results = (latents, logdet, patch_grad)
    else:
        small = [masters[i].astype(jnp.bfloat16) for i in (1, 0, 6, 7)]
        shards.append(pack_side(*small))
        share = max(1, held // seq_count)
        copies = seq_count * share // held
        first_row = (lax.axis_index("seq") // copies) * share
        pieces = jnp.concatenate([patches.astype(jnp.float32), cotangent], 2)
        pieces = lax.all_gather(pieces, "seq", axis=1, tiled=True)
        pieces = lax.dynamic_slice_in_dim(pieces, first_row, share, 0)
        seg_ids, labels = row_facts(
            lax.dynamic_slice_in_dim(seg_lengths, first_row, share, 0),
            lax.dynamic_slice_in_dim(class_labels, first_row, share, 0),
            length,
        )
        mine = (pieces[..., :channels], pieces[..., channels:], seg_ids, labels)
        outcome, patch_grad, sums = unstaged(mine, shards, sizes)
        results = lax.all_gather(jnp.concatenate([outcome, patch_grad], 2), "seq", axis=0)
        results = results[::copies].reshape((held,) + results.shape[2:])
        results = lax.dynamic_slice_in_dim(results, lax.axis_index("seq") * group, group, 1)
        results = (
            results[..., :channels],
            results[..., channels],
            results[..., channels + 1 :],
        )
        sums = [total.astype(jnp.float32) / copies for total in sums]
        table, first, last, gain = split_side(sums[4], *sizes)
        grads = (first, table, sums[0], sums[1], sums[2], sums[3], last, gain)
        updates = [adam_step(*item) for item in zip(masters, firsts, seconds, grads, RATES)]
    return results + tuple(part for update in updates for part in update)


def solution(mesh):
    tokens = P("rows", "seq", None)
    row = P("rows", None)
    last, middle = P(None, None, "rows"), P(None, "rows", None)
    weights = (last,) * 6 + (middle,) * 15 + (last,) * 3
    return jax.shard_map(
        body,
        mesh=mesh,
        in_specs=(tokens, row, row, tokens) + weights,
        out_specs=(tokens, P("rows", "seq"), tokens) + weights,
        check_vma=False,
    )
```

time: 916 us -> 496 us (0.54)
  matrix products: 235 us -> 0 us
  local copies, waits for them, and re-layouts: 188 us -> 5.99 us
  Pallas kernels: 317 us -> 443 us
  other arithmetic: 124 us -> 29.5 us
  starting transfers between devices: 20.2 us -> 9.01 us
  blocking collectives: 11 us -> 0 us
    dot_general x106 -> x0, matrix products: 235 us -> none  [the longest x70 201 us: dot(): lax.dot_general(left, right, (dims, ((), ())), preferred_element_type=jnp...]
    pallas_call x2 -> x5, Pallas kernels: 317 us -> 443 us  [the longest x1 177 us: summed_products(): pl.pallas_call(functools.partial(products_kernel, units, n_pairs, out_cou...]
    unnamed x743 -> x56, local copies, waits for them, and re-layouts: 50.6 us -> 3.95 us
    reshape x30 -> x0, local copies, waits for them, and re-layouts: 39.5 us -> none  [the longest x24 34.9 us: heads_of(): return flat.reshape(rows, -1, HEADS, HEAD_DIM)]
    slice x31 -> x3, local copies, waits for them, and re-layouts: 37.9 us -> 1.35 us  [the longest x1 0.65 us: staged(): outcome[..., :channels]]
    another operation x8 -> x1, other arithmetic: 23.6 us -> 0.85 us  [staged(): jnp.cumsum(seg_lengths, 1)]
    select_n x23 -> x7, other arithmetic: 23.8 us -> 3.34 us  [the longest x1 1.13 us: staged(): own = halves(jnp.where(second, latents[2], grad_inputs[2]))]
    another operation x21 -> x1, local copies, waits for them, and re-layouts: 18.8 us -> 0.01 us  [staged(): jnp.stack([their_facts, facts], 0)]
  transfers between devices with their start and end apart: 9 -> 6, of which waited for: 1 -> 1; matrix products, arithmetic and copies ran while one was open for 43% -> 5% of each run, Pallas kernels for 35% -> 36%
where the time goes in v3:
time: 496 us; the launch traced here: 491 us
  Pallas kernels  443 us (89%)
  other arithmetic  29.5 us (6%)
  starting transfers between devices  9.01 us (2%)
  local copies, waits for them, and re-layouts  5.99 us (1%)
    pallas_call x1, Pallas kernels, summed_products(): pl.pallas_call(functools.partial(products_kernel, units, n_pairs, out_cou...  177 us
    pallas_call x1, Pallas kernels, two_blocks(): pl.pallas_call(functools.partial(blocks_kernel, (rows, length, table, cha...  143 us
    pallas_call x1, Pallas kernels, gather_blocks(): pl.pallas_call(functools.partial(gather_kernel, units, LATE, GATHER_LAGS,...  121 us
    sub x4, other arithmetic, adam_step(): weight - rate * (first_hat / (jnp.sqrt(second_hat) + EPS_ADAM) + DECAY *...  16.2 us
  transfers between devices with their start and end apart: 6, of which 1 were waited for; matrix products, arithmetic and copies ran while one was open for 5% of the time, Pallas kernels for 36%

profile of v3, /device:TPU:8, one launch (start us, length us, event | category | flops | bytes accessed | tf_op | source)
XLA Modules:
  0.0 491.2 jit_solution(15865932783375681456)
XLA Ops:
  0.7 0.1 pad.21.clone
  0.7 0.9 reduce_window_sum.11
  1.6 0.8 add_add_fusion
  2.4 2.6 collective-permute-start.2
  5.0 0.8 convert_element_type.29
  5.8 0.9 select_maximum_fusion
  6.7 0.0 copy-start.14
  6.7 0.1 copy.56
  6.8 1.6 collective-permute-start
  8.4 0.1 copy.55
  8.5 2.7 collective-permute-done
  11.2 0.4 collective-permute-start.1
  11.6 1.8 convert_element_type.31.refs_1_
  13.4 2.5 convert_element_type.30.refs_0_
  15.9 1.2 convert_element_type.32.refs_2_
  17.0 0.9 copy-done.16
  18.0 1.1 convert_element_type.33.refs_3_
  19.1 0.2 pack_side.1.refs_4_
  19.3 0.7 copy-done.1
  20.0 0.0 collective-permute-done.2
  20.0 0.6 add_select_fusion.facts
  20.6 0.0 collective-permute-done.1
  20.6 0.1 slice.29
  20.8 0.9 maximum_select_fusion.1
  21.7 121.2 %gather_blocks.1 = (bf16[2,768,2304]{2,1,0:T(8,128)(2,1)}, bf16[2,768,768]{2,1,0:T(8,128)(2,1)}, bf16[2,768,3072]{2,1,0:T(8,128)(2,1)}, bf16[2,3072,768]{2,1,0:T(8,128)(2,1)}, bf16[1,768,1280]{2,1,0:T(8,128)(2,1)}) custom-call(bf16[4,48,2304]{2,1,0:T(8,128)(2,1)} %convert_element_type.30.refs_0_, bf16[4,48,768]{2,1,0:T(8,128)(2,1)} %convert_element_type.31.refs_1_, ...), custom_call_target="tpu_custom_call" | custom-call | tf_op jit(solution)/shard_map/gather_blocks/pallas_call | solution.py:292
  142.9 142.9 %two_blocks.1 = (f32[3,256,128]{2,1,0:T(8,128)}, f32[3,256,128]{2,1,0:T(8,128)}, f32[3,8,768]{2,1,0:T(8,128)}, f32[3,2,256,768]{3,2,1,0:T(8,128)}, bf16[3,2,256,...) custom-call(s32[2,2,9]{2,1,0:T(2,128)} %add_select_fusion.facts, ...), custom_call_target="tpu_custom_call" | custom-call | tf_op jit(solution)/shard_map/two_blocks/pallas_call | solution.py:900
  285.7 1.1 slice_select_fusion.1
  286.9 0.1 copy.60
  287.0 0.1 copy.59
  287.1 0.1 copy.58
  287.2 0.6 collective-permute-start.3
  287.8 1.0 collective-permute-start.4
  288.8 2.9 collective-permute-start.5
  291.7 176.9 %summed_products.1 = (bf16[4,48,2304]{2,1,0:T(8,128)(2,1)}, bf16[4,48,768]{2,1,0:T(8,128)(2,1)}, bf16[4,48,3072]{2,1,0:T(8,128)(2,1)}, bf16[4,192,768]{2,1,0:T(8,128)(2,1)}, bf16[2,48,1280]{2,1,0:T(8,128)(2,1)}) custom-call(bf16[3,2,256,768]{3,2,1,0:T(8,128)(2,1)} %get-tuple-element.85.refs_0_, bf16[3,2,256,2304]{3,2,1,0:T(8,128)(2,1)} %get-tuple-element.86.refs_1_, ...), custom_call_target="tpu_custom_call" | custom-call | tf_op jit(solution)/shard_map/summed_products/pallas_call | solution.py:1122
  468.6 0.0 copy-start.15
  468.6 0.0 copy-start.19
  468.6 0.0 copy-start.20
  468.7 6.2 %multiply_subtract_fusion.2 = (f32[4,48,2304]{2,1,0:T(8,128)}, f32[4,48,2304]{2,1,0:T(8,128)}, f32[4,48,2304]{2,1,0:T(8,128)}) fusion(f32[4,48,2304]{2,1,0:T(8,128)} %param.38, bf16[4,48,2304]{2,1,0:T(8,128)(2,1)} %get-tuple-element.105, f32[4,48,2304]{2,1,0:T(8,128)} %param.40, f32[4,48,2304]{2,1,0:T(8,128)} %param.39), kind=kLoop, calls=%fused_computation.14 | loop fusion | flops 7077888 | bytes 11501568 | tf_op jit(solution)/shard_map/sub | solution.py:1411
  474.9 0.7 copy-done.24
  475.6 4.4 multiply_subtract_fusion.1
  480.0 1.2 copy-done.22
  481.2 0.3 copy-done.23
  481.5 4.1 multiply_subtract_fusion
  485.7 0.0 copy-start.8
  485.7 0.0 copy-start.9
  485.7 0.0 copy-start.10
  485.7 0.0 copy-start.12
  485.7 0.0 copy-start.13
  485.8 1.5 multiply_subtract_fusion.3
  487.2 0.1 copy.57
  487.3 0.0 copy-done.2
  487.4 0.0 copy-done.3
  487.4 0.0 copy-done.4
  487.4 0.0 copy-done.7
  487.4 0.0 copy-done.8
  487.4 0.0 copy-done.9
  487.4 1.5 small_updates.1
  489.0 0.0 collective-permute-done.3
  489.0 0.0 collective-permute-done.4
  489.0 0.0 collective-permute-done.5
  489.0 0.1 broadcast_select_fusion.1
  489.1 0.6 slice.39
  489.6 0.6 slice.38
  490.3 0.7 slice_select_fusion.2
  (43 shorter events, 0.2 us)
Async XLA Ops:
  2.4 17.7 %collective-permute-start.2 = (s32[2,9]{1,0:T(2,128)S(1)}, s32[2,9]{1,0:T(2,128)S(1)}, u32[]{:S(2)}, u32[]{:S(2)}) collective-permute-start(s32[2,9]{1,0:T(2,128)S(1)} %constant_dynamic-slice_fusion.4), channel_id=1, source_target_pairs={{0,16},{2,18},{4,20},{6,22},{8,24},{10,26},{12,28},{14,30},{16,0},... | collective-permute-start | bytes 224 | tf_op jit(solution)/shard_map/ppermute | solution.py:1519
  6.7 9.2 %copy-start.14 = (f32[4,48,3072]{2,1,0:T(8,128)S(1)}, f32[4,48,3072]{2,1,0:T(8,128)}, u32[]{:S(2)}) copy-start(f32[4,48,3072]{2,1,0:T(8,128)} %param.44) | copy-start | bytes 7077892
  6.8 4.3 collective-permute-start
  11.2 9.5 %collective-permute-start.1 = (f32[256,128]{1,0:T(8,128)S(1)}, f32[256,128]{1,0:T(8,128)S(1)}, u32[]{:S(2)}, u32[]{:S(2)}) collective-permute-start(f32[256,128]{1,0:T(8,128)S(1)} %bitcast.41), channel_id=1, source_target_pairs={{0,16},{2,18},{4,20},{6,22},{8,24},{10,26},{12,28},{14,30},{16,0},... | collective-permute-start | bytes 393224 | tf_op jit(solution)/shard_map/ppermute | solution.py:1514
  15.9 2.1 copy-start.16
  18.0 1.1 copy-start
  18.0 1.1 copy-start.5
  18.0 1.1 copy-start.6
  18.0 1.1 copy-start.11
  19.3 0.7 copy-start.1
  287.2 201.7 %collective-permute-start.3 = (f32[2,64,128]{1,2,0:T(8,128)S(1)}, f32[2,64,128]{1,2,0:T(8,128)S(1)}, u32[]{:S(2)}, u32[]{:S(2)}) collective-permute-start(f32[2,64,128]{1,2,0:T(8,128)S(1)} %bitcast.49), channel_id=1, source_target_pairs={{0,1},{1,0},{2,3},{3,2},{4,5},{5,4},{6,7},{7,6},{8,9},{9,8},{10,11... | collective-permute-start | bytes 196616 | tf_op jit(solution)/shard_map/ppermute | solution.py:1545
  287.8 201.2 %collective-permute-start.4 = (f32[2,64,128]{1,2,0:T(8,128)S(1)}, f32[2,64,128]{1,2,0:T(8,128)S(1)}, u32[]{:S(2)}, u32[]{:S(2)}) collective-permute-start(f32[2,64,128]{1,2,0:T(8,128)S(1)} %bitcast.48), channel_id=1, source_target_pairs={{0,16},{2,18},{4,20},{6,22},{8,24},{10,26},{12,28},{14,30},{16,0},... | collective-permute-start | bytes 196616 | tf_op jit(solution)/shard_map/ppermute | solution.py:1546
  288.8 200.2 %collective-permute-start.5 = (f32[2,64,128]{1,2,0:T(8,128)S(1)}, f32[2,64,128]{1,2,0:T(8,128)S(1)}, u32[]{:S(2)}, u32[]{:S(2)}) collective-permute-start(f32[2,64,128]{1,2,0:T(8,128)S(1)} %bitcast.47), channel_id=1, source_target_pairs={{0,17},{1,16},{2,19},{3,18},{4,21},{5,20},{6,23},{7,22},{8,25},{9,... | collective-permute-start | bytes 196616 | tf_op jit(solution)/shard_map/ppermute | solution.py:1547
  468.6 6.2 %copy-start.15 = (f32[4,48,3072]{2,1,0:T(8,128)S(1)}, f32[4,48,3072]{2,1,0:T(8,128)}, u32[]{:S(2)}) copy-start(f32[4,48,3072]{2,1,0:T(8,128)} %param.44) | copy-start | bytes 7077892
  468.6 6.2 %copy-start.19 = (f32[4,48,3072]{2,1,0:T(8,128)S(1)}, f32[4,48,3072]{2,1,0:T(8,128)}, u32[]{:S(2)}) copy-start(f32[4,48,3072]{2,1,0:T(8,128)} %param.46) | copy-start | bytes 7077892
  468.6 6.2 %copy-start.20 = (f32[4,48,3072]{2,1,0:T(8,128)S(1)}, f32[4,48,3072]{2,1,0:T(8,128)}, u32[]{:S(2)}) copy-start(f32[4,48,3072]{2,1,0:T(8,128)} %param.45) | copy-start | bytes 7077892
  468.7 6.9 %copy-start.24 = (bf16[4,48,3072]{2,1,0:T(8,128)(2,1)S(1)}, bf16[4,48,3072]{2,1,0:T(8,128)(2,1)}, u32[]{:S(2)}) copy-start(bf16[4,48,3072]{2,1,0:T(8,128)(2,1)} %get-tuple-element.107) | copy-start | bytes 3538948
  475.6 4.4 copy-start.17
  475.6 4.4 copy-start.21
  475.6 5.6 %copy-start.22 = (f32[4,192,768]{2,1,0:T(8,128)S(1)}, f32[4,192,768]{2,1,0:T(8,128)}, u32[]{:S(2)}) copy-start(f32[4,192,768]{2,1,0:T(8,128)} %param.48) | copy-start | bytes 7077892
  475.6 5.9 %copy-start.23 = (bf16[4,192,768]{2,1,0:T(8,128)(2,1)S(1)}, bf16[4,192,768]{2,1,0:T(8,128)(2,1)}, u32[]{:S(2)}) copy-start(bf16[4,192,768]{2,1,0:T(8,128)(2,1)} %get-tuple-element.108) | copy-start | bytes 3538948
  481.5 4.2 copy-start.18
  481.5 4.2 copy-start.25
  481.5 4.2 copy-start.26
  481.5 4.2 copy-start.27
  485.6 1.7 copy-start.2
  485.6 1.7 copy-start.3
  485.6 1.7 copy-start.4
  485.6 1.7 copy-start.7
  485.7 1.7 copy-start.8
  485.7 1.7 copy-start.9
  485.7 1.7 copy-start.10
  485.7 1.7 copy-start.12
  485.7 1.7 copy-start.13
